TPU v7x, 32 devices: a whole 2x2x4 slice. The times are simulated.
32 devices in a mesh: dp: 4 (over z), fsdp: 8 (over y, x, core).
Axes of the slice: x: 2, y: 2, z: 4, core: 2. Of those that a mesh axis runs over, the one named last changes fastest.
Arguments:
- tokens: bfloat16 [16384, 768], P(('dp', 'fsdp')), may hold values from -6 to 6
- segment_ids: int32 [32, 512], P(('dp', 'fsdp')), may hold values from 0 to 7, never falling along the last dimension, each value on 1 to 128 neighbouring positions
- output_grad: bfloat16 [4, 16384, 768], P(None, ('dp', 'fsdp')), may hold values from -6 to 6
- query_weight: bfloat16 [768, 768], P(('dp', 'fsdp')), may hold values from -0.21875 to 0.21875
- query_bias: bfloat16 [768], P(('dp', 'fsdp')), may hold values from -3 to 3
- key_weight: bfloat16 [768, 768], P(('dp', 'fsdp')), may hold values from -0.21875 to 0.21875
- value_weight: bfloat16 [768, 768], P(('dp', 'fsdp')), may hold values from -0.21875 to 0.21875
- value_bias: bfloat16 [768], P(('dp', 'fsdp')), may hold values from -3 to 3
- output_weight: bfloat16 [768, 768], P(('dp', 'fsdp')), may hold values from -1.25 to 1.25
- output_bias: bfloat16 [768], P(('dp', 'fsdp')), may hold values from -3 to 3
- first_gain: bfloat16 [768], P(('dp', 'fsdp')), may hold values from 0.25 to 1.75
- first_shift: bfloat16 [768], P(('dp', 'fsdp')), may hold values from -3 to 3
- inner_weight: bfloat16 [768, 3072], P(('dp', 'fsdp')), may hold values from -0.21875 to 0.21875
- inner_bias: bfloat16 [3072], P(('dp', 'fsdp')), may hold values from -3 to 3
- outer_weight: bfloat16 [768, 3072], P(('dp', 'fsdp')), may hold values from -0.15625 to 0.15625
- outer_bias: bfloat16 [768], P(('dp', 'fsdp')), may hold values from -3 to 3
- second_gain: bfloat16 [768], P(('dp', 'fsdp')), may hold values from 0.25 to 1.75
- second_shift: bfloat16 [768], P(('dp', 'fsdp')), may hold values from -3 to 3
Outputs:
- layer_output: bfloat16 [4, 16384, 768], P(None, ('dp', 'fsdp'))
- input_grad: float32 [4, 16384, 768], P(None, ('dp', 'fsdp'))
- query_weight_grad: float32 [768, 768], P(('dp', 'fsdp'))
- query_bias_grad: float32 [768], P(('dp', 'fsdp'))
- key_weight_grad: float32 [768, 768], P(('dp', 'fsdp'))
- value_weight_grad: float32 [768, 768], P(('dp', 'fsdp'))
- value_bias_grad: float32 [768], P(('dp', 'fsdp'))
- output_weight_grad: float32 [768, 768], P(('dp', 'fsdp'))
- output_bias_grad: float32 [768], P(('dp', 'fsdp'))
- first_gain_grad: float32 [768], P(('dp', 'fsdp'))
- first_shift_grad: float32 [768], P(('dp', 'fsdp'))
- inner_weight_grad: float32 [768, 3072], P(('dp', 'fsdp'))
- inner_bias_grad: float32 [3072], P(('dp', 'fsdp'))
- outer_weight_grad: float32 [768, 3072], P(('dp', 'fsdp'))
- outer_bias_grad: float32 [768], P(('dp', 'fsdp'))
- second_gain_grad: float32 [768], P(('dp', 'fsdp'))
- second_shift_grad: float32 [768], P(('dp', 'fsdp'))
Inputs may be any that keep to these rules, and one draw needn't show every extreme that they name: `segment_ids`: along each sequence segment numbers never fall; each segment holds 1 to 128 tokens and one holds exactly 128.
All inputs are finite; a program needn't handle non-finite values.
Results may differ from a plain program's by a relative error of at most 0.012.
The roundings to bfloat16 on the way count: a program that leaves them out, or rounds other values in their place, can miss the bound.
Values may be sent and summed in bfloat16 or wider, within the bound.
No kernel may reach another device: no remote copies, remote signals or barrier semaphores. Data moves between devices by JAX's collectives and lax.ppermute only.
A program may use at most 256 MiB of HBM per device.

v0:
```python
import math

import jax
import jax.numpy as jnp
from jax import lax
from jax.sharding import PartitionSpec as P

HEADS = 12
HEAD_DIM = 64
WIDTHS = 4


def matmul(left_side, right_side):
    return jnp.dot(left_side, right_side, preferred_element_type=jnp.float32)


def matmul_last(left_side, right_side):
    return lax.dot_general(
        left_side, right_side, (((1,), (1,)), ((), ())), preferred_element_type=jnp.float32
    )


def matmul_first(left_side, right_side):
    return lax.dot_general(
        left_side, right_side, (((0,), (0,)), ((), ())), preferred_element_type=jnp.float32
    )


def layer_norm(values, gain, shift):
    center = values - jnp.mean(values, axis=-1, keepdims=True)
    spread = jnp.mean(center * center, axis=-1, keepdims=True)
    return center * lax.rsqrt(spread + 1e-12) * gain + shift


def gelu_exact(values):
    return jax.nn.gelu(values, approximate=False)


def masked_scores(queries, key_rows, labels):
    factor = 1.0 / math.sqrt(queries.shape[-1])
    scores = (
        jnp.einsum("qhd,khd->hqk", queries, key_rows, preferred_element_type=jnp.float32) * factor
    )
    matched = labels[:, None] == labels[None, :]
    return jnp.where(matched[None], scores, -1e30)


def attend_forward(blocks):
    queries, key_rows, value_rows, labels = blocks
    scores = masked_scores(queries, key_rows, labels)
    highest = jnp.max(scores, axis=-1, keepdims=True)
    shifted = jnp.exp(scores - highest)
    summed = jnp.sum(shifted, axis=-1, keepdims=True)
    weights = (shifted / summed).astype(jnp.bfloat16)
    mixture = jnp.einsum("hqk,khd->qhd", weights, value_rows, preferred_element_type=jnp.float32)
    return (mixture, highest + jnp.log(summed))


def attend_backward(blocks):
    queries, key_rows, value_rows, labels, log_summed, mixture_grad = blocks
    factor = 1.0 / math.sqrt(queries.shape[-1])
    scores = masked_scores(queries, key_rows, labels)
    chances = jnp.exp(scores - log_summed)
    chance_grad = jnp.einsum(
        "qhd,khd->hqk", mixture_grad, value_rows, preferred_element_type=jnp.float32
    )
    value_grad = jnp.einsum(
        "hqk,qhd->khd",
        chances.astype(jnp.bfloat16),
        mixture_grad,
        preferred_element_type=jnp.float32,
    )
    row_term = jnp.sum(chances * chance_grad, axis=-1, keepdims=True)
    score_grad = (chances * (chance_grad - row_term)).astype(jnp.bfloat16)
    query_grad = (
        jnp.einsum("hqk,khd->qhd", score_grad, key_rows, preferred_element_type=jnp.float32)
        * factor
    )
    key_grad = (
        jnp.einsum("hqk,qhd->khd", score_grad, queries, preferred_element_type=jnp.float32) * factor
    )
    return (query_grad, key_grad, value_grad)


def pad_columns(matrix, columns):
    return jnp.pad(matrix, ((0, 0), (0, columns - matrix.shape[1])))


def pad_vector(vector, entries):
    return jnp.pad(vector, (0, entries - vector.shape[0]))


def per_device(
    tokens,
    segment_ids,
    output_grad,
    query_weight,
    query_bias,
    key_weight,
    value_weight,
    value_bias,
    output_weight,
    output_bias,
    first_gain,
    first_shift,
    inner_weight,
    inner_bias,
    outer_weight,
    outer_bias,
    second_gain,
    second_shift,
):
    width_full = tokens.shape[1]
    hidden_full = inner_weight.shape[1]
    seq_count = segment_ids.shape[0]
    seq_length = segment_ids.shape[1]
    totals = [
        jnp.zeros((width_full, width_full), jnp.float32),
        jnp.zeros((width_full,), jnp.float32),
        jnp.zeros((width_full, width_full), jnp.float32),
        jnp.zeros((width_full, width_full), jnp.float32),
        jnp.zeros((width_full,), jnp.float32),
        jnp.zeros((width_full, width_full), jnp.float32),
        jnp.zeros((width_full,), jnp.float32),
        jnp.zeros((width_full,), jnp.float32),
        jnp.zeros((width_full,), jnp.float32),
        jnp.zeros((width_full, hidden_full), jnp.float32),
        jnp.zeros((hidden_full,), jnp.float32),
        jnp.zeros((width_full, hidden_full), jnp.float32),
        jnp.zeros((width_full,), jnp.float32),
        jnp.zeros((width_full,), jnp.float32),
        jnp.zeros((width_full,), jnp.float32),
    ]
    column_counts = (
        width_full,
        0,
        width_full,
        width_full,
        0,
        width_full,
        0,
        0,
        0,
        hidden_full,
        0,
        hidden_full,
        0,
        0,
        0,
    )
    layer_outputs = []
    input_grads = []
    for section in range(WIDTHS):
        heads_kept = HEADS * (section + 1) // 4
        width_kept = heads_kept * HEAD_DIM
        hidden_kept = hidden_full * (section + 1) // 4
        fetched = (
            lax.all_gather(query_weight[:, :width_kept], ("dp", "fsdp"), axis=0, tiled=True),
            lax.all_gather(key_weight[:, :width_kept], ("dp", "fsdp"), axis=0, tiled=True),
            lax.all_gather(value_weight[:, :width_kept], ("dp", "fsdp"), axis=0, tiled=True),
            lax.all_gather(output_weight[:, :width_kept], ("dp", "fsdp"), axis=0, tiled=True),
            lax.all_gather(inner_weight[:, :hidden_kept], ("dp", "fsdp"), axis=0, tiled=True),
            lax.all_gather(outer_weight[:, :hidden_kept], ("dp", "fsdp"), axis=0, tiled=True),
            lax.all_gather(query_bias, ("dp", "fsdp"), axis=0, tiled=True),
            lax.all_gather(value_bias, ("dp", "fsdp"), axis=0, tiled=True),
            lax.all_gather(output_bias, ("dp", "fsdp"), axis=0, tiled=True),
            lax.all_gather(first_gain, ("dp", "fsdp"), axis=0, tiled=True),
            lax.all_gather(first_shift, ("dp", "fsdp"), axis=0, tiled=True),
            lax.all_gather(inner_bias, ("dp", "fsdp"), axis=0, tiled=True),
            lax.all_gather(outer_bias, ("dp", "fsdp"), axis=0, tiled=True),
            lax.all_gather(second_gain, ("dp", "fsdp"), axis=0, tiled=True),
            lax.all_gather(second_shift, ("dp", "fsdp"), axis=0, tiled=True),
        )
        w_query = fetched[0]
        w_key = fetched[1]
        w_value = fetched[2]
        w_output = fetched[3]
        w_inner = fetched[4]
        w_outer = fetched[5]
        b_query = fetched[6][:width_kept].astype(jnp.float32)
        b_value = fetched[7][:width_kept].astype(jnp.float32)
        b_output = fetched[8].astype(jnp.float32)
        gain_one = fetched[9].astype(jnp.float32)
        shift_one = fetched[10].astype(jnp.float32)
        b_inner = fetched[11][:hidden_kept].astype(jnp.float32)
        b_outer = fetched[12].astype(jnp.float32)
        gain_two = fetched[13].astype(jnp.float32)
        shift_two = fetched[14].astype(jnp.float32)
        queries = (matmul(tokens, w_query) + b_query).astype(jnp.bfloat16)
        key_rows = matmul(tokens, w_key).astype(jnp.bfloat16)
        value_rows = (matmul(tokens, w_value) + b_value).astype(jnp.bfloat16)
        shaped = (seq_count, seq_length, heads_kept, HEAD_DIM)
        query_blocks = queries.reshape(shaped)
        key_blocks = key_rows.reshape(shaped)
        value_blocks = value_rows.reshape(shaped)
        mixture, log_summed = lax.map(
            attend_forward, (query_blocks, key_blocks, value_blocks, segment_ids)
        )
        attended = mixture.reshape(-1, width_kept).astype(jnp.bfloat16)
        branch = matmul_last(attended, w_output) + b_output
        first_sum = tokens.astype(jnp.float32) + branch
        normed, first_pull = jax.vjp(layer_norm, first_sum, gain_one, shift_one)
        normed_low = normed.astype(jnp.bfloat16)
        inner_pre = matmul(normed_low, w_inner) + b_inner
        active, gelu_pull = jax.vjp(gelu_exact, inner_pre)
        active_low = active.astype(jnp.bfloat16)
        second_sum = normed + matmul_last(active_low, w_outer) + b_outer
        result, second_pull = jax.vjp(layer_norm, second_sum, gain_two, shift_two)
        layer_outputs.append(result.astype(jnp.bfloat16))
        second_grad, gain_two_grad, shift_two_grad = second_pull(
            output_grad[section].astype(jnp.float32)
        )
        feed_grad = second_grad.astype(jnp.bfloat16)
        outer_grad = matmul_first(feed_grad, active_low)
        outer_bias_part = jnp.sum(feed_grad.astype(jnp.float32), axis=0)
        active_grad = matmul(feed_grad, w_outer)
        (inner_raw,) = gelu_pull(active_grad)
        inner_low = inner_raw.astype(jnp.bfloat16)
        inner_grad = matmul_first(normed_low, inner_low)
        inner_bias_part = jnp.sum(inner_low.astype(jnp.float32), axis=0)
        normed_grad = second_grad + matmul_last(inner_low, w_inner)
        first_grad, gain_one_grad, shift_one_grad = first_pull(normed_grad)
        branch_grad = first_grad.astype(jnp.bfloat16)
        output_part = matmul_first(branch_grad, attended)
        output_bias_part = jnp.sum(branch_grad.astype(jnp.float32), axis=0)
        attended_grad = matmul(branch_grad, w_output).astype(jnp.bfloat16)
        query_raw, key_raw, value_raw = lax.map(
            attend_backward,
            (
                query_blocks,
                key_blocks,
                value_blocks,
                segment_ids,
                log_summed,
                attended_grad.reshape(shaped),
            ),
        )
        query_low = query_raw.reshape(-1, width_kept).astype(jnp.bfloat16)
        key_low = key_raw.reshape(-1, width_kept).astype(jnp.bfloat16)
        value_low = value_raw.reshape(-1, width_kept).astype(jnp.bfloat16)
        query_part = matmul_first(tokens, query_low)
        key_part = matmul_first(tokens, key_low)
        value_part = matmul_first(tokens, value_low)
        query_bias_part = pad_vector(jnp.sum(query_low.astype(jnp.float32), axis=0), width_full)
        value_bias_part = pad_vector(jnp.sum(value_low.astype(jnp.float32), axis=0), width_full)
        inner_bias_full = pad_vector(inner_bias_part, hidden_full)
        token_grad = (
            first_grad
            + matmul_last(query_low, w_query)
            + matmul_last(key_low, w_key)
            + matmul_last(value_low, w_value)
        )
        input_grads.append(token_grad)
        pieces = (
            query_part,
            query_bias_part,
            key_part,
            value_part,
            value_bias_part,
            output_part,
            output_bias_part,
            gain_one_grad,
            shift_one_grad,
            inner_grad,
            inner_bias_full,
            outer_grad,
            outer_bias_part,
            gain_two_grad,
            shift_two_grad,
        )
        updated = []
        for position in range(15):
            piece = pieces[position]
            if column_counts[position] > 0:
                piece = pad_columns(piece, column_counts[position])
            updated.append(totals[position] + piece)
        totals = updated
    totals = (
        lax.psum_scatter(totals[0], ("dp", "fsdp"), scatter_dimension=0, tiled=True),
        lax.psum_scatter(totals[1], ("dp", "fsdp"), scatter_dimension=0, tiled=True),
        lax.psum_scatter(totals[2], ("dp", "fsdp"), scatter_dimension=0, tiled=True),
        lax.psum_scatter(totals[3], ("dp", "fsdp"), scatter_dimension=0, tiled=True),
        lax.psum_scatter(totals[4], ("dp", "fsdp"), scatter_dimension=0, tiled=True),
        lax.psum_scatter(totals[5], ("dp", "fsdp"), scatter_dimension=0, tiled=True),
        lax.psum_scatter(totals[6], ("dp", "fsdp"), scatter_dimension=0, tiled=True),
        lax.psum_scatter(totals[7], ("dp", "fsdp"), scatter_dimension=0, tiled=True),
        lax.psum_scatter(totals[8], ("dp", "fsdp"), scatter_dimension=0, tiled=True),
        lax.psum_scatter(totals[9], ("dp", "fsdp"), scatter_dimension=0, tiled=True),
        lax.psum_scatter(totals[10], ("dp", "fsdp"), scatter_dimension=0, tiled=True),
        lax.psum_scatter(totals[11], ("dp", "fsdp"), scatter_dimension=0, tiled=True),
        lax.psum_scatter(totals[12], ("dp", "fsdp"), scatter_dimension=0, tiled=True),
        lax.psum_scatter(totals[13], ("dp", "fsdp"), scatter_dimension=0, tiled=True),
        lax.psum_scatter(totals[14], ("dp", "fsdp"), scatter_dimension=0, tiled=True),
    )
    return (
        jnp.stack(layer_outputs),
        jnp.stack(input_grads),
        totals[0],
        totals[1],
        totals[2],
        totals[3],
        totals[4],
        totals[5],
        totals[6],
        totals[7],
        totals[8],
        totals[9],
        totals[10],
        totals[11],
        totals[12],
        totals[13],
        totals[14],
    )


def solution(mesh):
    placed = (
        P(("dp", "fsdp"), None),
        P(("dp", "fsdp"), None),
        P(None, ("dp", "fsdp"), None),
        P(("dp", "fsdp"), None),
        P(("dp", "fsdp")),
        P(("dp", "fsdp"), None),
        P(("dp", "fsdp"), None),
        P(("dp", "fsdp")),
        P(("dp", "fsdp"), None),
        P(("dp", "fsdp")),
        P(("dp", "fsdp")),
        P(("dp", "fsdp")),
        P(("dp", "fsdp"), None),
        P(("dp", "fsdp")),
        P(("dp", "fsdp"), None),
        P(("dp", "fsdp")),
        P(("dp", "fsdp")),
        P(("dp", "fsdp")),
    )
    return jax.shard_map(
        per_device,
        mesh=mesh,
        in_specs=placed,
        out_specs=(
            P(None, ("dp", "fsdp"), None),
            P(None, ("dp", "fsdp"), None),
            P(("dp", "fsdp"), None),
            P(("dp", "fsdp")),
            P(("dp", "fsdp"), None),
            P(("dp", "fsdp"), None),
            P(("dp", "fsdp")),
            P(("dp", "fsdp"), None),
            P(("dp", "fsdp")),
            P(("dp", "fsdp")),
            P(("dp", "fsdp")),
            P(("dp", "fsdp"), None),
            P(("dp", "fsdp")),
            P(("dp", "fsdp"), None),
            P(("dp", "fsdp")),
            P(("dp", "fsdp")),
            P(("dp", "fsdp")),
        ),
        check_vma=False,
    )
```

profile of v0, /device:TPU:0, one launch (start us, length us, event | category | flops | bytes accessed | tf_op | source)
XLA Modules:
  0.0 1572.3 jit_solution(4229374927919327168)
XLA Ops:
  22.8 42.5 %all-reduce.46 = (bf16[768]{0:T(1024)(128)(2,1)S(1)}, bf16[768]{0:T(1024)(128)(2,1)S(1)}, bf16[768]{0:T(1024)(128)(2,1)S(1)}, bf16[768]{0:T(1024)(128)(2,1)S(1)}...) all-reduce(bf16[768]{0:T(1024)(128)(2,1)S(1)} %dynamic-update-slice, ...), channel_id=1, replica_groups=mesh['dp'=4,'fsdp'=8] {'dp','fsdp'}, use_global_device_ids=true, to_apply=%add.27 | all-reduce | flops 9216 | bytes 36864
  67.9 43.1 %all_gather.147 = bf16[768,576]{1,0:T(8,128)(2,1)S(1)} all-gather(bf16[24,576]{1,0:T(8,128)(2,1)S(1)} %slice.111), channel_id=1, replica_groups=mesh['dp'=4,'fsdp'=8] {'dp','fsdp'}, dimensions={0}, use_global_device_ids=true | all-gather | bytes 912384 | tf_op jit(solution)/shard_map/all_gather | solution.py:160
  111.0 39.5 %all_gather.148 = bf16[768,576]{1,0:T(8,128)(2,1)S(1)} all-gather(bf16[24,576]{1,0:T(8,128)(2,1)S(1)} %slice.113), channel_id=1, replica_groups=mesh['dp'=4,'fsdp'=8] {'dp','fsdp'}, dimensions={0}, use_global_device_ids=true | all-gather | bytes 912384 | tf_op jit(solution)/shard_map/all_gather | solution.py:158
  150.5 41.1 %all_gather.149 = bf16[768,576]{1,0:T(8,128)(2,1)S(1)} all-gather(bf16[24,576]{1,0:T(8,128)(2,1)S(1)} %slice.115), channel_id=1, replica_groups=mesh['dp'=4,'fsdp'=8] {'dp','fsdp'}, dimensions={0}, use_global_device_ids=true | all-gather | bytes 912384 | tf_op jit(solution)/shard_map/all_gather | solution.py:159
  200.5 40.4 %all_gather.150 = bf16[768,576]{1,0:T(8,128)(2,1)S(1)} all-gather(bf16[24,576]{1,0:T(8,128)(2,1)S(1)} %slice.116), channel_id=1, replica_groups=mesh['dp'=4,'fsdp'=8] {'dp','fsdp'}, dimensions={0}, use_global_device_ids=true | all-gather | bytes 912384 | tf_op jit(solution)/shard_map/all_gather | solution.py:161
  243.5 39.6 %all_gather.126 = bf16[768,192]{1,0:T(8,128)(2,1)S(1)} all-gather(bf16[24,192]{1,0:T(8,128)(2,1)S(1)} %slice.93), channel_id=1, replica_groups=mesh['dp'=4,'fsdp'=8] {'dp','fsdp'}, dimensions={0}, use_global_device_ids=true | all-gather | bytes 304128 | tf_op jit(solution)/shard_map/all_gather | solution.py:160
  283.1 37.8 %all_gather.128 = bf16[768,192]{1,0:T(8,128)(2,1)S(1)} all-gather(bf16[24,192]{1,0:T(8,128)(2,1)S(1)} %slice.95), channel_id=1, replica_groups=mesh['dp'=4,'fsdp'=8] {'dp','fsdp'}, dimensions={0}, use_global_device_ids=true | all-gather | bytes 304128 | tf_op jit(solution)/shard_map/all_gather | solution.py:158
  320.9 39.3 %all_gather.130 = bf16[768,192]{1,0:T(8,128)(2,1)S(1)} all-gather(bf16[24,192]{1,0:T(8,128)(2,1)S(1)} %slice.97), channel_id=1, replica_groups=mesh['dp'=4,'fsdp'=8] {'dp','fsdp'}, dimensions={0}, use_global_device_ids=true | all-gather | bytes 304128 | tf_op jit(solution)/shard_map/all_gather | solution.py:159
  364.5 38.2 %all_gather.131 = bf16[768,192]{1,0:T(8,128)(2,1)S(1)} all-gather(bf16[24,192]{1,0:T(8,128)(2,1)S(1)} %slice.98), channel_id=1, replica_groups=mesh['dp'=4,'fsdp'=8] {'dp','fsdp'}, dimensions={0}, use_global_device_ids=true | all-gather | bytes 304128 | tf_op jit(solution)/shard_map/all_gather | solution.py:161
  404.3 40.3 %all_gather.141 = bf16[768,384]{1,0:T(8,128)(2,1)S(1)} all-gather(bf16[24,384]{1,0:T(8,128)(2,1)S(1)} %slice.102), channel_id=1, replica_groups=mesh['dp'=4,'fsdp'=8] {'dp','fsdp'}, dimensions={0}, use_global_device_ids=true | all-gather | bytes 608256 | tf_op jit(solution)/shard_map/all_gather | solution.py:160
  444.7 39.0 %all_gather.142 = bf16[768,384]{1,0:T(8,128)(2,1)S(1)} all-gather(bf16[24,384]{1,0:T(8,128)(2,1)S(1)} %slice.104), channel_id=1, replica_groups=mesh['dp'=4,'fsdp'=8] {'dp','fsdp'}, dimensions={0}, use_global_device_ids=true | all-gather | bytes 608256 | tf_op jit(solution)/shard_map/all_gather | solution.py:158
  483.7 39.8 %all_gather.143 = bf16[768,384]{1,0:T(8,128)(2,1)S(1)} all-gather(bf16[24,384]{1,0:T(8,128)(2,1)S(1)} %slice.106), channel_id=1, replica_groups=mesh['dp'=4,'fsdp'=8] {'dp','fsdp'}, dimensions={0}, use_global_device_ids=true | all-gather | bytes 608256 | tf_op jit(solution)/shard_map/all_gather | solution.py:159
  529.8 38.8 %all_gather.144 = bf16[768,384]{1,0:T(8,128)(2,1)S(1)} all-gather(bf16[24,384]{1,0:T(8,128)(2,1)S(1)} %slice.107), channel_id=1, replica_groups=mesh['dp'=4,'fsdp'=8] {'dp','fsdp'}, dimensions={0}, use_global_device_ids=true | all-gather | bytes 608256 | tf_op jit(solution)/shard_map/all_gather | solution.py:161
  571.4 6.7 multiply_convert_fusion.9
  599.2 4.8 fusion.76
  608.0 11.2 multiply_convert_fusion.6
  619.2 3.7 fusion.153
  624.5 16.0 %multiply_convert_fusion.4 = (bf16[512,2304]{1,0:T(8,128)(2,1)}, f32[512,2304]{1,0:T(8,128)}, f32[512,2304]{1,0:T(8,128)}) fusion(f32[2304]{0:T(1024)S(1)} %copy-done.190, bf16[768,2304]{1,0:T(8,128)(2,1)} %all-gather.21.cloned.1.call-done, f32[512,768]{1,0:T(8,128)} %copy-done.27, f32[512]{0:T(512)S(1)} %fusion.113, f32[512]{0:T(512)S(1)} %broadcast_multiply_fusion.3, ...), kind=kOutput, calls=%fused_computation.56 | convolution fusion | flops 1891762176 | bytes 16927744 | tf_op jit(solution)/shard_map/dot_general | solution.py:14
  640.5 4.9 fusion.147
  645.7 20.1 %all-gather.33.cloned.1.call-done = bf16[768,3072]{1,0:T(8,128)(2,1)} async-done(((bf16[24,3072]{1,0:T(8,128)(2,1)}), bf16[768,3072]{1,0:T(8,128)(2,1)}) %all-gather.33.cloned.1.call-update) | async-done | bytes 4718608 | tf_op jit(solution)/shard_map/all_gather | solution.py:162
  665.9 20.9 %multiply_convert_fusion.3 = (bf16[512,3072]{1,0:T(8,128)(2,1)}, f32[512,3072]{1,0:T(8,128)}, f32[512,3072]{1,0:T(8,128)}) fusion(f32[3072]{0:T(1024)S(1)} %copy-done.189, bf16[768,3072]{1,0:T(8,128)(2,1)} %all-gather.33.cloned.1.call-done, f32[512,768]{1,0:T(8,128)} %copy-done.45, f32[512]{0:T(512)S(1)} %fusion.115, f32[512]{0:T(512)S(1)} %broadcast_multiply_fusion.1, ...), kind=kOutput, calls=%fused_computation.29 | convolution fusion | flops 2521694208 | bytes 22042624 | tf_op jit(solution)/shard_map/dot_general | solution.py:14
  686.8 44.3 %all-gather.35.cloned.1.call-done = bf16[768,3072]{1,0:T(8,128)(2,1)} async-done(((bf16[24,3072]{1,0:T(8,128)(2,1)}), bf16[768,3072]{1,0:T(8,128)(2,1)}) %all-gather.35.cloned.1.call-update) | async-done | bytes 4718608 | tf_op jit(solution)/shard_map/all_gather | solution.py:163
  731.1 6.2 fusion.155
  738.8 4.9 fusion.61
  745.2 8.8 convert_reduce_fusion
  754.0 3.6 multiply_reduce_fusion.4
  763.0 6.7 convert_reduce_fusion.1
  784.3 5.3 multiply_reduce_fusion.7
  794.9 11.1 multiply_reduce_fusion
  807.8 7.0 multiply_convert_fusion
  819.8 5.1 fusion.133
  827.5 5.0 multiply_reduce_fusion.1
  832.5 11.3 multiply_convert_fusion.1
  843.8 4.1 convert_reduce_fusion.19
  849.8 4.4 multiply_reduce_fusion.2
  877.6 4.2 fusion.78
  891.6 3.3 convert_reduce_fusion.22
  895.3 4.8 convert_reduce_fusion.20
  901.3 6.5 convert_reduce_fusion.18
  909.1 3.8 convert_reduce_fusion.16
  937.9 6.3 add_add_fusion.1
  951.4 5.4 add_add_fusion
  968.8 40.8 %all-reduce.45 = (f32[768]{0:T(1024)S(1)}, f32[768]{0:T(1024)S(1)}, f32[768]{0:T(1024)S(1)}, f32[768]{0:T(1024)S(1)}, f32[768]{0:T(1024)S(1)}, /*index=5*/f32[30...) all-reduce(f32[768]{0:T(1024)S(1)} %add_add_fusion.26, ...), channel_id=3, replica_groups=mesh['dp'=4,'fsdp'=8] {'dp','fsdp'}, use_global_device_ids=true, to_apply=%region_49.50.clone | all-reduce | flops 9216 | bytes 73728
  1037.4 36.8 %reduce-scatter.21.cloned.1.call-done = f32[24,768]{1,0:T(8,128)} async-done(((f32[768,768]{1,0:T(8,128)}), f32[24,768]{1,0:T(8,128)}) %reduce-scatter.21.cloned.1.call-update) | async-done | bytes 73744
  1074.1 103.8 %reduce-scatter.23.cloned.1.call-done = f32[24,768]{1,0:T(8,128)} async-done(((f32[768,768]{1,0:T(8,128)}), f32[24,768]{1,0:T(8,128)}) %reduce-scatter.23.cloned.1.call-update) | async-done | bytes 73744
  1177.9 104.6 %reduce-scatter.25.cloned.1.call-done = f32[24,768]{1,0:T(8,128)} async-done(((f32[768,768]{1,0:T(8,128)}), f32[24,768]{1,0:T(8,128)}) %reduce-scatter.25.cloned.1.call-update) | async-done | bytes 73744
  1282.5 140.8 %reduce-scatter.15.cloned.1.call-done = f32[24,3072]{1,0:T(8,128)} async-done(((f32[768,3072]{1,0:T(8,128)}), f32[24,3072]{1,0:T(8,128)}) %reduce-scatter.15.cloned.1.call-update) | async-done | bytes 294928 | tf_op jit(solution)/shard_map/reduce_scatter | solution.py:288
  1423.3 142.0 %reduce-scatter.17.cloned.1.call-done = f32[24,3072]{1,0:T(8,128)} async-done(((f32[768,3072]{1,0:T(8,128)}), f32[24,3072]{1,0:T(8,128)}) %reduce-scatter.17.cloned.1.call-update) | async-done | bytes 294928 | tf_op jit(solution)/shard_map/reduce_scatter | solution.py:290
  (758 shorter events, 216.3 us)
Async XLA Ops:
  7.3 14.6 copy-start.209
  7.3 14.8 copy-start.210
  7.3 15.1 copy-start.211
  7.3 15.3 copy-start.212
  7.3 564.1 %all-gather.13.cloned.1.call-start = ((), (), s32[]{:S(2)}) async-start(), calls=%async_computation.6 | async-start | bytes 1216512 | tf_op jit(solution)/shard_map/all_gather | solution.py:162
  8.8 569.3 %all-gather.15.cloned.1.call-start = ((), (), s32[]{:S(2)}) async-start(), calls=%async_computation.7 | async-start | bytes 1216512 | tf_op jit(solution)/shard_map/all_gather | solution.py:163
  10.3 572.4 %all-gather.25.cloned.1.call-start = ((), (), s32[]{:S(2)}) async-start(), calls=%async_computation.12 | async-start | bytes 1216512 | tf_op jit(solution)/shard_map/all_gather | solution.py:160
  11.0 574.2 %all-gather.27.cloned.1.call-start = ((), (), s32[]{:S(2)}) async-start(), calls=%async_computation.13 | async-start | bytes 1216512 | tf_op jit(solution)/shard_map/all_gather | solution.py:158
  11.6 576.3 %all-gather.29.cloned.1.call-start = ((), (), s32[]{:S(2)}) async-start(), calls=%async_computation.14 | async-start | bytes 1216512 | tf_op jit(solution)/shard_map/all_gather | solution.py:159
  12.2 591.8 %all-gather.31.cloned.1.call-start = ((), (), s32[]{:S(2)}) async-start(), calls=%async_computation.15 | async-start | bytes 1216512 | tf_op jit(solution)/shard_map/all_gather | solution.py:161
  12.8 595.3 %all-gather.17.cloned.1.call-start = ((), (), s32[]{:S(2)}) async-start(), calls=%async_computation.8 | async-start | bytes 2433024 | tf_op jit(solution)/shard_map/all_gather | solution.py:162
  14.4 604.9 %all-gather.19.cloned.1.call-start = ((), (), s32[]{:S(2)}) async-start(), calls=%async_computation.9 | async-start | bytes 2433024 | tf_op jit(solution)/shard_map/all_gather | solution.py:163
  16.0 608.5 %all-gather.21.cloned.1.call-start = ((), (), s32[]{:S(2)}) async-start(), calls=%async_computation.10 | async-start | bytes 3649536 | tf_op jit(solution)/shard_map/all_gather | solution.py:162
  17.6 622.9 %all-gather.23.cloned.1.call-start = ((), (), s32[]{:S(2)}) async-start(), calls=%async_computation.11 | async-start | bytes 3649536 | tf_op jit(solution)/shard_map/all_gather | solution.py:163
  19.2 646.7 %all-gather.33.cloned.1.call-start = ((), (), s32[]{:S(2)}) async-start(), calls=%async_computation.16 | async-start | bytes 4866048 | tf_op jit(solution)/shard_map/all_gather | solution.py:162
  19.9 711.2 %all-gather.35.cloned.1.call-start = ((), (), s32[]{:S(2)}) async-start(), calls=%async_computation.17 | async-start | bytes 4866048 | tf_op jit(solution)/shard_map/all_gather | solution.py:163
  20.5 1016.8 %reduce-scatter.19.cloned.1.call-start = ((), (), s32[]{:S(2)}) async-start(), calls=%async_computation.20 | async-start | bytes 2433024
  20.7 170.9 %copy-start.191 = (s32[1,512]{1,0:T(1,128)S(1)}, s32[1,512]{1,0:T(1,128)}, u32[]{:S(2)}) copy-start(s32[1,512]{1,0:T(1,128)} %param.19) | copy-start | bytes 6148
  66.6 125.2 %copy-start.1 = (bf16[512,768]{1,0:T(8,128)(2,1)S(1)}, bf16[512,768]{1,0:T(8,128)(2,1)}, u32[]{:S(2)}) copy-start(bf16[512,768]{1,0:T(8,128)(2,1)} %param.18) | copy-start | bytes 2359300
  111.0 86.6 %copy-start.60 = (bf16[768,576]{1,0:T(8,128)(2,1)}, bf16[768,576]{1,0:T(8,128)(2,1)S(1)}, u32[]{:S(2)}) copy-start(bf16[768,576]{1,0:T(8,128)(2,1)S(1)} %all_gather.147) | copy-start | bytes 2654212
  150.5 42.0 %copy-start.62 = (bf16[768,576]{1,0:T(8,128)(2,1)}, bf16[768,576]{1,0:T(8,128)(2,1)S(1)}, u32[]{:S(2)}) copy-start(bf16[768,576]{1,0:T(8,128)(2,1)S(1)} %all_gather.148) | copy-start | bytes 2654212
  191.8 406.8 %copy-start.19 = (pred[512,512]{0,1:T(8,128)(4,1)}, pred[512,512]{0,1:T(8,128)(4,1)S(1)}, u32[]{:S(2)}) copy-start(pred[512,512]{0,1:T(8,128)(4,1)S(1)} %broadcast_compare_fusion) | copy-start | bytes 786436
  200.5 41.4 %copy-start.150 = (bf16[9,64,512]{2,1,0:T(8,128)(2,1)}, bf16[9,64,512]{2,1,0:T(8,128)(2,1)S(1)}, u32[]{:S(2)}) copy-start(bf16[9,64,512]{2,1,0:T(8,128)(2,1)S(1)} %fusion.81) | copy-start | bytes 1769476
  241.9 118.8 %copy-start.27 = (f32[512,768]{1,0:T(8,128)}, f32[512,768]{1,0:T(8,128)S(1)}, u32[]{:S(2)}) copy-start(f32[512,768]{1,0:T(8,128)S(1)} %get-tuple-element.395) | copy-start | bytes 4718596
  242.2 118.9 %copy-start.172 = (f32[512]{0:T(512)}, f32[512]{0:T(512)S(1)}, u32[]{:S(2)}) copy-start(f32[512]{0:T(512)S(1)} %multiply_reduce_fusion.15) | copy-start | bytes 6148
  283.1 80.3 %copy-start.68 = (bf16[768,192]{1,0:T(8,128)(2,1)}, bf16[768,192]{1,0:T(8,128)(2,1)S(1)}, u32[]{:S(2)}) copy-start(bf16[768,192]{1,0:T(8,128)(2,1)S(1)} %all_gather.126) | copy-start | bytes 884740
  320.9 40.2 %copy-start.72 = (bf16[768,192]{1,0:T(8,128)(2,1)}, bf16[768,192]{1,0:T(8,128)(2,1)S(1)}, u32[]{:S(2)}) copy-start(bf16[768,192]{1,0:T(8,128)(2,1)S(1)} %all_gather.128) | copy-start | bytes 884740
  364.5 39.8 %copy-start.143 = (bf16[3,64,512]{2,1,0:T(8,128)(2,1)}, bf16[3,64,512]{2,1,0:T(8,128)(2,1)S(1)}, u32[]{:S(2)}) copy-start(bf16[3,64,512]{2,1,0:T(8,128)(2,1)S(1)} %fusion.101) | copy-start | bytes 589828
  404.0 174.1 %copy-start.12 = (f32[512,768]{1,0:T(8,128)}, f32[512,768]{1,0:T(8,128)S(1)}, u32[]{:S(2)}) copy-start(f32[512,768]{1,0:T(8,128)S(1)} %get-tuple-element.402) | copy-start | bytes 4718596
  404.0 174.1 %copy-start.163 = (f32[512]{0:T(512)}, f32[512]{0:T(512)S(1)}, u32[]{:S(2)}) copy-start(f32[512]{0:T(512)S(1)} %broadcast_multiply_fusion.7) | copy-start | bytes 6148
  404.3 119.8 %copy-start.174 = (f32[512]{0:T(512)}, f32[512]{0:T(512)S(1)}, u32[]{:S(2)}) copy-start(f32[512]{0:T(512)S(1)} %multiply_reduce_fusion.19) | copy-start | bytes 6148
  404.3 173.8 %copy-start.169 = (f32[512]{0:T(512)}, f32[512]{0:T(512)S(1)}, u32[]{:S(2)}) copy-start(f32[512]{0:T(512)S(1)} %fusion.109) | copy-start | bytes 6148
  444.7 83.2 %copy-start.109 = (bf16[768,384]{1,0:T(8,128)(2,1)}, bf16[768,384]{1,0:T(8,128)(2,1)S(1)}, u32[]{:S(2)}) copy-start(bf16[768,384]{1,0:T(8,128)(2,1)S(1)} %all_gather.141) | copy-start | bytes 1769476
  483.7 40.9 %copy-start.105 = (bf16[768,384]{1,0:T(8,128)(2,1)}, bf16[768,384]{1,0:T(8,128)(2,1)S(1)}, u32[]{:S(2)}) copy-start(bf16[768,384]{1,0:T(8,128)(2,1)S(1)} %all_gather.142) | copy-start | bytes 1769476
  529.7 39.5 %copy-start.133 = (bf16[6,64,512]{2,1,0:T(8,128)(2,1)}, bf16[6,64,512]{2,1,0:T(8,128)(2,1)S(1)}, u32[]{:S(2)}) copy-start(bf16[6,64,512]{2,1,0:T(8,128)(2,1)S(1)} %fusion.96) | copy-start | bytes 1179652
  608.0 174.8 %copy-start.192 = (f32[512]{0:T(512)}, f32[512]{0:T(512)S(1)}, u32[]{:S(2)}) copy-start(f32[512]{0:T(512)S(1)} %fusion.115) | copy-start | bytes 6148
  624.4 16.0 %copy-start.28 = (f32[512,768]{1,0:T(8,128)S(1)}, f32[512,768]{1,0:T(8,128)}, u32[]{:S(2)}) copy-start(f32[512,768]{1,0:T(8,128)} %copy-done.27) | copy-start | bytes 4718596
  640.5 25.4 %copy-start.189 = (f32[3072]{0:T(1024)S(1)}, f32[3072]{0:T(1024)}, u32[]{:S(2)}) copy-start(f32[3072]{0:T(1024)} %convert_element_type.601) | copy-start | bytes 36868
  645.7 85.4 %copy-start.46 = (f32[512,768]{1,0:T(8,128)S(1)}, f32[512,768]{1,0:T(8,128)}, u32[]{:S(2)}) copy-start(f32[512,768]{1,0:T(8,128)} %copy-done.45) | copy-start | bytes 4718596
  762.0 17.1 %copy-start.52 = (bf16[512,768]{1,0:T(8,128)(2,1)}, bf16[512,768]{1,0:T(8,128)(2,1)S(1)}, u32[]{:S(2)}) copy-start(bf16[512,768]{1,0:T(8,128)(2,1)S(1)} %get-tuple-element.321) | copy-start | bytes 2359300
  871.5 202.6 %reduce-scatter.21.cloned.1.call-start = ((), (), s32[]{:S(2)}) async-start(), calls=%async_computation.21 | async-start | bytes 2433024
  891.5 286.4 %reduce-scatter.23.cloned.1.call-start = ((), (), s32[]{:S(2)}) async-start(), calls=%async_computation.22 | async-start | bytes 2433024
  919.1 363.4 %reduce-scatter.25.cloned.1.call-start = ((), (), s32[]{:S(2)}) async-start(), calls=%async_computation.23 | async-start | bytes 2433024
  929.3 494.0 %reduce-scatter.15.cloned.1.call-start = ((), (), s32[]{:S(2)}) async-start(), calls=%async_computation.18 | async-start | bytes 9732096 | tf_op jit(solution)/shard_map/reduce_scatter | solution.py:288
  944.3 621.0 %reduce-scatter.17.cloned.1.call-start = ((), (), s32[]{:S(2)}) async-start(), calls=%async_computation.19 | async-start | bytes 9732096 | tf_op jit(solution)/shard_map/reduce_scatter | solution.py:290
  958.8 56.0 %copy-start.75 = (bf16[768,192]{1,0:T(8,128)(2,1)S(1)}, bf16[768,192]{1,0:T(8,128)(2,1)}, u32[]{:S(2)}) copy-start(bf16[768,192]{1,0:T(8,128)(2,1)} %copy-done.74) | copy-start | bytes 884740
  959.8 56.4 %copy-start.73 = (bf16[768,192]{1,0:T(8,128)(2,1)S(1)}, bf16[768,192]{1,0:T(8,128)(2,1)}, u32[]{:S(2)}) copy-start(bf16[768,192]{1,0:T(8,128)(2,1)} %copy-done.72) | copy-start | bytes 884740
  959.8 56.4 %copy-start.121 = (bf16[3,64,512]{2,1,0:T(8,128)(2,1)S(1)}, bf16[3,64,512]{2,1,0:T(8,128)(2,1)}, u32[]{:S(2)}) copy-start(bf16[3,64,512]{2,1,0:T(8,128)(2,1)} %copy-done.120) | copy-start | bytes 589828
  (211 other events, 805.4 us)
Sparse Core Ops, SparseCore 0:
  11.6 56.7 all-gather.12
  71.9 53.7 all-gather.14
  128.6 55.2 all-gather.24
  186.6 52.9 all-gather.26
  242.4 54.8 all-gather.28
  300.0 53.5 all-gather.30
  357.1 56.9 all-gather.16
  417.5 57.2 all-gather.18
  478.3 61.7 all-gather.20
  542.8 57.6 all-gather.22
  603.4 62.3 all-gather.32
  668.6 62.4 all-gather.34
  871.6 97.8 reduce-scatter.18
  976.1 97.9 reduce-scatter.20
  1079.8 97.9 reduce-scatter.22
  1184.4 98.0 reduce-scatter.24
  1288.8 134.4 reduce-scatter.14
  1430.6 134.5 reduce-scatter.16
where the time goes:
time: 1580 us; the launch traced here: 1570 us
  waiting for transfers between devices  596 us (38%)
  blocking collectives  560 us (35%)
  matrix products  247 us (16%)
  local copies, waits for them, and re-layouts  82.7 us (5%)
  other arithmetic  68 us (4%)
  between operations  17.2 us (1%)
    unnamed x22, waiting for transfers between devices  249 us
    reduce_scatter x1, waiting for transfers between devices, per_device(): lax.psum_scatter(totals[11], ('dp', 'fsdp'), scatter_dimension=0, tiled=T...  142 us
    reduce_scatter x1, waiting for transfers between devices, per_device(): lax.psum_scatter(totals[9], ('dp', 'fsdp'), scatter_dimension=0, tiled=True)  141 us
    all_gather x3, blocking collectives, per_device(): lax.all_gather(value_weight[:, :width_kept], ('dp', 'fsdp'), axis=0, tile...  123 us
    all_gather x3, blocking collectives, per_device(): lax.all_gather(key_weight[:, :width_kept], ('dp', 'fsdp'), axis=0, tiled=...  120 us
    all_gather x3, blocking collectives, per_device(): lax.all_gather(output_weight[:, :width_kept], ('dp', 'fsdp'), axis=0, til...  117 us
    all_gather x3, blocking collectives, per_device(): lax.all_gather(query_weight[:, :width_kept], ('dp', 'fsdp'), axis=0, tile...  116 us
    dot_general x24, matrix products, matmul(): return jnp.dot(left_side, right_side, preferred_element_type=jnp.float32)  90.7 us
  transfers between devices with their start and end apart: 18, of which 7 were waited for; matrix products, arithmetic and copies ran while one was open for 15% of the time, Pallas kernels for 0%

commit v1 on v0

v1 whole, which is shorter than its diff:
```python
import math

import jax
import jax.numpy as jnp
from jax import lax
from jax.experimental import pallas as pl
from jax.experimental.pallas import tpu as pltpu
from jax.sharding import PartitionSpec as P

HEADS = 12
HEAD_DIM = 64
WIDTHS = 4
BLOCK = 128
AXES = ("dp", "fsdp")
BF = jnp.bfloat16
F32 = jnp.float32
VMEM_LIMIT = 60 * 1024 * 1024


def matmul(left_side, right_side):
    return lax.dot_general(
        left_side, right_side, (((1,), (0,)), ((), ())), preferred_element_type=F32
    )


def matmul_last(left_side, right_side):
    return lax.dot_general(
        left_side, right_side, (((1,), (1,)), ((), ())), preferred_element_type=F32
    )


def windows(length):
    count = length // BLOCK
    spans = []
    for i in range(count):
        start = max(0, i - 1) * BLOCK
        spans.append((start, min(count, i + 2) * BLOCK - start))
    return spans


def call(kernel, flops, moved, **options):
    return pl.pallas_call(
        kernel,
        compiler_params=pltpu.CompilerParams(vmem_limit_bytes=VMEM_LIMIT),
        cost_estimate=pl.CostEstimate(flops=flops, bytes_accessed=moved, transcendentals=0),
        **options,
    )


def shape_of(shape, dtype):
    return jax.ShapeDtypeStruct(shape, dtype)


def whole(shape):
    return pl.BlockSpec(shape, lambda *_: (0,) * len(shape))


def attend_kernel(x, wq, wk, wv, bq, bv, seg_col, seg_row, q_o, k_o, v_o, a_o, p_o, bias):
    spans = windows(x.shape[0])

    @pl.when(pl.program_id(0) == 0)
    def _():
        for i, (start, span) in enumerate(spans):
            same = seg_col[i * BLOCK : (i + 1) * BLOCK, :] == seg_row[:, start : start + span]
            bias[i, :, :span] = jnp.where(same, 0.0, -1e30)

    rows = x[...]
    q_o[...] = (matmul(rows, wq[...]) + bq[...]).astype(BF)
    k_o[...] = matmul(rows, wk[...]).astype(BF)
    v_o[...] = (matmul(rows, wv[...]) + bv[...]).astype(BF)
    lane = lax.broadcasted_iota(jnp.int32, (BLOCK, BLOCK), 1)
    low_half = lane < HEAD_DIM
    factor = 1.0 / math.sqrt(HEAD_DIM)
    masks = (
        jnp.where(low_half, factor, 0.0).astype(BF),
        jnp.where(low_half, 0.0, factor).astype(BF),
    )
    for pair in range(q_o.shape[1] // BLOCK):
        cols = slice(pair * BLOCK, (pair + 1) * BLOCK)
        for i, (start, span) in enumerate(spans):
            here = slice(i * BLOCK, (i + 1) * BLOCK)
            q_here = q_o[here, cols]
            k_near = k_o[start : start + span, cols]
            v_near = v_o[start : start + span, cols]
            mixed = []
            for half in range(2):
                scores = matmul_last(q_here * masks[half], k_near) + bias[i, :, :span]
                highest = jnp.max(scores, axis=1, keepdims=True)
                shifted = jnp.exp(scores - highest)
                total = jnp.sum(shifted, axis=1, keepdims=True)
                chances = (shifted * (1.0 / total)).astype(BF)
                p_o[2 * pair + half, i, :, :span] = chances
                mixed.append(matmul(chances, v_near))
            a_o[here, cols] = jnp.where(low_half, mixed[0], mixed[1]).astype(BF)


def attend(x, wq, wk, wv, bq, bv, segments):
    length, width = x.shape
    step = 256
    count = length // BLOCK
    part = pl.BlockSpec((length, step), lambda p: (0, p))
    weight = pl.BlockSpec((width, step), lambda p: (0, p))
    vector = pl.BlockSpec((1, step), lambda p: (0, p))
    heads = step // HEAD_DIM
    return call(
        attend_kernel,
        6 * length * width * width,
        16 * length * width,
        grid=(width // step,),
        in_specs=[whole(x.shape), weight, weight, weight, vector, vector, whole((length, 1)), whole((1, length))],
        out_specs=[part, part, part, part, pl.BlockSpec((heads, count, BLOCK, 3 * BLOCK), lambda p: (p, 0, 0, 0))],
        out_shape=[shape_of((length, width), BF)] * 4 + [shape_of((HEADS, count, BLOCK, 3 * BLOCK), BF)],
        scratch_shapes=[pltpu.VMEM((count, BLOCK, 3 * BLOCK), F32)],
        name="attend",
    )(x, wq, wk, wv, bq, bv, segments.reshape(length, 1), segments.reshape(1, length))


def norm_parts(values):
    center = values - jnp.mean(values, axis=1, keepdims=True)
    scale = lax.rsqrt(jnp.mean(center * center, axis=1, keepdims=True) + 1e-12)
    return center * scale, scale


def norm_back(spread_grad, hat, scale):
    return scale * (
        spread_grad
        - jnp.mean(spread_grad, axis=1, keepdims=True)
        - hat * jnp.mean(spread_grad * hat, axis=1, keepdims=True)
    )


def chunk_mask(w, rows):
    lane = lax.broadcasted_iota(jnp.int32, (rows, 2 * BLOCK), 1)
    start = HEAD_DIM * (w % 2)
    return (lane >= start) & (lane < start + 3 * HEAD_DIM)


def window_at(w):
    return w + w // 2


def first_kernel(x, att_a, att_b, wo_a, wo_b, vec, first_o, normed_o, normed_t_o, second_o, x_t_o, branch):
    w = pl.program_id(0)

    @pl.when(w == 0)
    def _():
        branch[...] = x[...].astype(F32) + vec[0:1, :]
        x_t_o[...] = x[...].T

    kept = jnp.where(chunk_mask(w, x.shape[0]), jnp.concatenate([att_a[...], att_b[...]], axis=1).astype(F32), 0.0)
    weight = jnp.concatenate([wo_a[...], wo_b[...]], axis=1)
    first = branch[...] + matmul_last(kept.astype(BF), weight)
    branch[...] = first
    first_o[0] = first
    hat, _ = norm_parts(first)
    normed = hat * vec[1:2, :] + vec[2:3, :]
    second_o[0] = normed + vec[3:4, :]
    low = normed.astype(BF)
    normed_o[0] = low
    normed_t_o[0] = low.T


def first_norm(x, att, wo, vec):
    length, width = x.shape
    per_width = pl.BlockSpec((1, length, width), lambda w: (w, 0, 0))
    return call(
        first_kernel,
        2 * length * width * width,
        40 * length * width,
        grid=(WIDTHS,),
        in_specs=[
            whole(x.shape),
            pl.BlockSpec((length, BLOCK), lambda w: (0, window_at(w))),
            pl.BlockSpec((length, BLOCK), lambda w: (0, window_at(w) + 1)),
            pl.BlockSpec((width, BLOCK), lambda w: (0, window_at(w))),
            pl.BlockSpec((width, BLOCK), lambda w: (0, window_at(w) + 1)),
            whole(vec.shape),
        ],
        out_specs=[
            per_width,
            per_width,
            pl.BlockSpec((1, width, length), lambda w: (w, 0, 0)),
            per_width,
            whole((width, length)),
        ],
        out_shape=[
            shape_of((WIDTHS, length, width), F32),
            shape_of((WIDTHS, length, width), BF),
            shape_of((WIDTHS, width, length), BF),
            shape_of((WIDTHS, length, width), F32),
            shape_of((width, length), BF),
        ],
        scratch_shapes=[pltpu.VMEM((length, width), F32)],
        name="first_norm",
    )(x, att, att, wo, wo, vec)


ERF_T = 0.3275911 / math.sqrt(2.0)
ERF_A = (0.254829592, -0.284496736, 1.421413741, -1.453152027, 1.061405429)


def gelu_pair(values):
    bell = jnp.exp(-0.5 * values * values)
    t = 1.0 / (1.0 + ERF_T * jnp.abs(values))
    poly = 0.5 * ERF_A[4]
    for entry in (ERF_A[3], ERF_A[2], ERF_A[1], ERF_A[0]):
        poly = poly * t + 0.5 * entry
    tail = poly * t * bell
    phi = jnp.where(values >= 0.0, 1.0 - tail, tail)
    return values * phi, phi + values * bell * (1.0 / math.sqrt(2.0 * math.pi))


def feed_kernel(j_of, w_of, normed, wi, wu, bi, second_in, og, vec, act_o, slope_o, out_o, feed_o, feed_t_o, second_g_o, sums_o, second):
    step = pl.program_id(0)
    j, w = j_of[step], w_of[step]

    @pl.when(step == 0)
    def _():
        sums_o[...] = jnp.zeros_like(sums_o)

    @pl.when(j == 0)
    def _():
        second[...] = second_in[0]

    length = normed.shape[1]
    rows_step = 256
    for r in range(0, length, rows_step):
        rows = slice(r, r + rows_step)
        inner = matmul(normed[0, rows, :], wi[...]) + bi[0]
        active, slope = gelu_pair(inner)
        active = active.astype(BF)
        act_o[0, rows, :] = active
        slope_o[0, rows, :] = slope.astype(BF)
        second[rows, :] += matmul_last(active, wu[...])

    @pl.when(j == w)
    def _():
        hat, scale = norm_parts(second[...])
        out_o[0] = (hat * vec[0:1, :] + vec[1:2, :]).astype(BF)
        grad = og[0].astype(F32)
        sums_o[0:1, :] += jnp.sum(grad * hat, axis=0, keepdims=True)
        sums_o[1:2, :] += jnp.sum(grad, axis=0, keepdims=True)
        second_g = norm_back(grad * vec[0:1, :], hat, scale)
        second_g_o[0] = second_g
        low = second_g.astype(BF)
        feed_o[0] = low
        feed_t_o[0] = low.T
        sums_o[2:3, :] += jnp.sum(low.astype(F32), axis=0, keepdims=True)


def feed_forward(normed, wi, wu, bi, second, og, vec):
    _, length, width = normed.shape
    order = [(j, w) for w in range(WIDTHS) for j in range(w + 1)]
    j_of = jnp.array([j for j, _ in order], jnp.int32)
    w_of = jnp.array([w for _, w in order], jnp.int32)
    per_width = pl.BlockSpec((1, length, width), lambda s, j, w: (w[s], 0, 0))
    per_step = pl.BlockSpec((1, length, width), lambda s, j, w: (s, 0, 0))
    weight = pl.BlockSpec((width, width), lambda s, j, w: (0, j[s]))
    steps = len(order)
    return call(
        feed_kernel,
        4 * steps * length * width * width,
        steps * 8 * length * width,
        grid_spec=pltpu.PrefetchScalarGridSpec(
            num_scalar_prefetch=2,
            grid=(steps,),
            in_specs=[
                per_width,
                weight,
                weight,
                pl.BlockSpec((1, 1, width), lambda s, j, w: (j[s], 0, 0)),
                per_width,
                per_width,
                whole(vec.shape),
            ],
            out_specs=[
                per_step,
                per_step,
                per_width,
                per_width,
                pl.BlockSpec((1, width, length), lambda s, j, w: (w[s], 0, 0)),
                per_width,
                whole((8, width)),
            ],
            scratch_shapes=[pltpu.VMEM((length, width), F32)],
        ),
        out_shape=[
            shape_of((steps, length, width), BF),
            shape_of((steps, length, width), BF),
            shape_of((WIDTHS, length, width), BF),
            shape_of((WIDTHS, length, width), BF),
            shape_of((WIDTHS, width, length), BF),
            shape_of((WIDTHS, length, width), F32),
            shape_of((8, width), F32),
        ],
        name="feed_forward",
    )(j_of, w_of, normed, wi, wu, bi, second, og, vec)


def back_kernel(j_of, w_of, s_of, feed, feed_t, normed_t, act, slope, second_g, wi, wu, grad_in, outer_o, inner_o, normed_g_o, bias_o, outer, inner):
    step = pl.program_id(0)
    j, w = j_of[step], w_of[step]
    if grad_in is not None:

        @pl.when(step == 0)
        def _():
            normed_g_o[...] = grad_in[...]

    @pl.when(j == w)
    def _():
        normed_g_o[w] = second_g[0]

    first = w == j

    length = feed.shape[1]
    rows_step = 256
    bias = jnp.zeros((1, feed.shape[2]), F32)
    inner_low = []
    for r in range(0, length, rows_step):
        rows = slice(r, r + rows_step)
        low = (slope[0, rows, :].astype(F32) * matmul(feed[0, rows, :], wu[...])).astype(BF)
        bias += jnp.sum(low.astype(F32), axis=0, keepdims=True)
        normed_g_o[w, rows, :] += matmul_last(low, wi[...])
        inner_low.append(low)
    low = jnp.concatenate(inner_low, axis=0)
    outer_part = matmul(feed_t[0], act[0])
    inner_part = matmul(normed_t[0], low)

    @pl.when(first)
    def _():
        outer[...] = outer_part
        inner[...] = inner_part
        bias_o[0] = bias

    @pl.when(jnp.logical_not(first))
    def _():
        outer[...] += outer_part
        inner[...] += inner_part
        bias_o[0] += bias

    @pl.when(w == WIDTHS - 1)
    def _():
        outer_o[...] = outer[...].astype(BF)
        inner_o[...] = inner[...].astype(BF)


def feed_backward(chunks, feed, feed_t, normed_t, act, slope, second_g, wi, wu, grad_in):
    _, length, width = feed.shape
    place = {}
    for w in range(WIDTHS):
        for j in range(w + 1):
            place[(j, w)] = len(place)
    order = [(j, w) for j in chunks for w in range(j, WIDTHS)]
    base = min(chunks)
    j_of = jnp.array([j for j, _ in order], jnp.int32)
    w_of = jnp.array([w for _, w in order], jnp.int32)
    s_of = jnp.array([place[key] for key in order], jnp.int32)
    per_width = pl.BlockSpec((1, length, width), lambda s, j, w, p: (w[s], 0, 0))
    per_width_t = pl.BlockSpec((1, width, length), lambda s, j, w, p: (w[s], 0, 0))
    per_step = pl.BlockSpec((1, length, width), lambda s, j, w, p: (p[s], 0, 0))
    weight = pl.BlockSpec((width, width), lambda s, j, w, p: (0, j[s]))
    local = pl.BlockSpec((width, width), lambda s, j, w, p: (0, j[s] - base))
    full = (WIDTHS, length, width)
    steps = len(order)
    kernel = back_kernel
    extra_specs, extra = [], []
    if grad_in is None:
        kernel = lambda *refs: back_kernel(*refs[:11], None, *refs[11:])
    else:
        extra_specs, extra = [whole(full)], [grad_in]
    return call(
        kernel,
        8 * steps * length * width * width,
        steps * 12 * length * width,
        grid_spec=pltpu.PrefetchScalarGridSpec(
            num_scalar_prefetch=3,
            grid=(steps,),
            in_specs=[per_width, per_width_t, per_width_t, per_step, per_step, per_width, weight, weight] + extra_specs,
            out_specs=[
                local,
                local,
                whole(full),
                pl.BlockSpec((1, 1, width), lambda s, j, w, p: (j[s] - base, 0, 0)),
            ],
            scratch_shapes=[pltpu.VMEM((width, width), F32), pltpu.VMEM((width, width), F32)],
        ),
        out_shape=[
            shape_of((width, width * len(chunks)), BF),
            shape_of((width, width * len(chunks)), BF),
            shape_of(full, F32),
            shape_of((len(chunks), 1, width), F32),
        ],
        name="feed_backward",
    )(j_of, w_of, s_of, feed, feed_t, normed_t, act, slope, second_g, wi, wu, *extra)


def first_back_kernel(first, normed_g, wo, att_a, att_b, vec, first_g_o, att_g_o, wo_g_o, sums_o, total, wo_g):
    step = pl.program_id(0)
    w = WIDTHS - 1 - step

    @pl.when(step == 0)
    def _():
        sums_o[...] = jnp.zeros_like(sums_o)
        total[...] = jnp.zeros_like(total)
        wo_g[...] = jnp.zeros_like(wo_g)

    hat, scale = norm_parts(first[0])
    grad = normed_g[0]
    sums_o[0:1, :] += jnp.sum(grad * hat, axis=0, keepdims=True)
    sums_o[1:2, :] += jnp.sum(grad, axis=0, keepdims=True)
    first_g = norm_back(grad * vec[1:2, :], hat, scale)
    first_g_o[0] = first_g
    low = first_g.astype(BF)
    wide = low.astype(F32)
    sums_o[2:3, :] += jnp.sum(wide, axis=0, keepdims=True)
    total[...] += wide
    length, width = wide.shape
    lane = lax.broadcasted_iota(jnp.int32, (length, width), 1)
    kept = lane < (w + 1) * (3 * HEAD_DIM)
    att_g_o[0] = jnp.where(kept, matmul(low, wo[...]), 0.0).astype(BF)
    att = jnp.where(chunk_mask(w, length), jnp.concatenate([att_a[...], att_b[...]], axis=1).astype(F32), 0.0)
    part = matmul(total[...].astype(BF).T, att.astype(BF))
    start = pl.multiple_of(BLOCK * window_at(w), BLOCK)
    wo_g[:, pl.ds(start, 2 * BLOCK)] += part

    @pl.when(w == 0)
    def _():
        wo_g_o[...] = wo_g[...].astype(BF)


def first_backward(first, normed_g, wo, att, vec):
    _, length, width = first.shape
    last = WIDTHS - 1
    per_width = pl.BlockSpec((1, length, width), lambda s: (last - s, 0, 0))
    return call(
        first_back_kernel,
        10 * length * width * width,
        60 * length * width,
        grid=(WIDTHS,),
        in_specs=[
            per_width,
            per_width,
            whole(wo.shape),
            pl.BlockSpec((length, BLOCK), lambda s: (0, window_at(last - s))),
            pl.BlockSpec((length, BLOCK), lambda s: (0, window_at(last - s) + 1)),
            whole(vec.shape),
        ],
        out_specs=[per_width, per_width, whole((width, width)), whole((8, width))],
        out_shape=[
            shape_of((WIDTHS, length, width), F32),
            shape_of((WIDTHS, length, width), BF),
            shape_of((width, width), BF),
            shape_of((8, width), F32),
        ],
        scratch_shapes=[pltpu.VMEM((length, width), F32), pltpu.VMEM((width, width), F32)],
        name="first_backward",
    )(first, normed_g, wo, att, att, vec)


def attend_back_kernel(q, k, v, p, g, dq_o, dk_o, dv_o, dqs_o, dks_o, dvs_o, sums_o, dk_t, dv_t):
    pair = pl.program_id(0)
    length = q.shape[0]
    spans = windows(length)
    factor = 1.0 / math.sqrt(HEAD_DIM)
    lane = lax.broadcasted_iota(jnp.int32, (BLOCK, BLOCK), 1)
    low_half = lane < HEAD_DIM
    masks = (
        jnp.where(low_half, 1.0, 0.0).astype(BF),
        jnp.where(low_half, 0.0, 1.0).astype(BF),
    )

    def run(first):
        widths = list(range(first, WIDTHS))
        dk_t[...] = jnp.zeros_like(dk_t)
        dv_t[...] = jnp.zeros_like(dv_t)
        q_t = (q[...] * jnp.asarray(factor, BF)).T
        g_t = [g[w].T for w in widths]
        for i, (start, span) in enumerate(spans):
            here = slice(i * BLOCK, (i + 1) * BLOCK)
            near = slice(start, start + span)
            k_near = k[near, :] * jnp.asarray(factor, BF)
            v_near = v[near, :]
            g_here = jnp.concatenate([g[w, here, :] for w in widths], axis=0)
            found = []
            for half in range(2):
                chances_low = p[half, i, :, :span]
                chances = chances_low.astype(F32)
                mask = jnp.concatenate([masks[half]] * len(widths), axis=0)
                chance_g = matmul_last(g_here * mask, v_near)
                rows_of = slice(half * HEAD_DIM, (half + 1) * HEAD_DIM)
                scores_g = []
                for n, w in enumerate(widths):
                    part = chance_g[n * BLOCK : (n + 1) * BLOCK, :]
                    product = chances * part
                    row = jnp.sum(product, axis=1, keepdims=True)
                    low = (product - chances * row).astype(BF)
                    scores_g.append(low)
                    dk_t[w, rows_of, near] += matmul(q_t[rows_of, here], low)
                found.append(matmul(jnp.concatenate(scores_g, axis=0), k_near))
                stacked = jnp.concatenate([g_t[n][rows_of, here] for n in range(len(widths))], axis=0)
                values_g = matmul(stacked, chances_low)
                for n, w in enumerate(widths):
                    dv_t[w, rows_of, near] += values_g[n * HEAD_DIM : (n + 1) * HEAD_DIM, :]
            wide = jnp.concatenate([low_half] * len(widths), axis=0)
            dq = jnp.where(wide, found[0], found[1]).astype(BF)
            for n, w in enumerate(widths):
                dq_o[w, here, :] = dq[n * BLOCK : (n + 1) * BLOCK, :]
        totals = [jnp.zeros((length, BLOCK), F32) for _ in range(3)]
        for w in range(WIDTHS):
            if w < first:
                for ref in (dq_o, dk_o, dv_o):
                    ref[w] = jnp.zeros((length, BLOCK), BF)
                continue
            dk_o[w] = dk_t[w].astype(BF).T
            dv_o[w] = dv_t[w].astype(BF).T
            for n, ref in enumerate((dq_o, dk_o, dv_o)):
                totals[n] += ref[w].astype(F32)
        dqs_o[...] = totals[0].astype(BF)
        dks_o[...] = totals[1].astype(BF)
        dvs_o[...] = totals[2].astype(BF)
        sums_o[0:1, :] = jnp.sum(totals[0], axis=0, keepdims=True)
        sums_o[1:2, :] = jnp.sum(totals[2], axis=0, keepdims=True)

    heads_each = HEADS // WIDTHS
    firsts = [(2 * n) // heads_each for n in range(HEADS // 2)]
    for first in sorted(set(firsts)):
        members = [n for n, f in enumerate(firsts) if f == first]

        @pl.when((pair >= members[0]) & (pair <= members[-1]))
        def _(first=first):
            run(first)


def attend_backward(q, k, v, p, g):
    length, width = q.shape
    pairs = width // BLOCK
    part = pl.BlockSpec((length, BLOCK), lambda n: (0, n))
    wide = pl.BlockSpec((WIDTHS, length, BLOCK), lambda n: (0, 0, n))
    return call(
        attend_back_kernel,
        40 * length * 3 * BLOCK * width,
        24 * length * width,
        grid=(pairs,),
        in_specs=[part, part, part, pl.BlockSpec((2,) + p.shape[1:], lambda n: (n, 0, 0, 0)), wide],
        out_specs=[wide, wide, wide, part, part, part, pl.BlockSpec((8, BLOCK), lambda n: (0, n))],
        out_shape=[shape_of((WIDTHS, length, width), BF)] * 3
        + [shape_of((length, width), BF)] * 3
        + [shape_of((8, width), F32)],
        scratch_shapes=[pltpu.VMEM((WIDTHS, BLOCK, length), F32)] * 2,
        name="attend_backward",
    )(q, k, v, p, g)


def project_kernel(x_t, dq, dk, dv, out_q, out_k, out_v):
    rows = x_t[...]
    out_q[...] = matmul(rows, dq[...]).astype(BF)
    out_k[...] = matmul(rows, dk[...]).astype(BF)
    out_v[...] = matmul(rows, dv[...]).astype(BF)


def project_grads(x_t, dqs, dks, dvs):
    width, length = x_t.shape
    step = 256
    part = pl.BlockSpec((length, step), lambda n: (0, n))
    out = pl.BlockSpec((width, step), lambda n: (0, n))
    return call(
        project_kernel,
        6 * length * width * width,
        16 * length * width,
        grid=(width // step,),
        in_specs=[whole(x_t.shape), part, part, part],
        out_specs=[out, out, out],
        out_shape=[shape_of((width, width), BF)] * 3,
        name="project_grads",
    )(x_t, dqs, dks, dvs)


def input_kernel(first_g, dq, dk, dv, wq, wk, wv, out):
    w = pl.program_id(0)
    for section in range(WIDTHS):
        kept = -(-(section + 1) * 3 * HEAD_DIM // BLOCK) * BLOCK

        @pl.when(w == section)
        def _():
            out[0] = (
                first_g[0]
                + matmul_last(dq[0, :, :kept], wq[:, :kept])
                + matmul_last(dk[0, :, :kept], wk[:, :kept])
                + matmul_last(dv[0, :, :kept], wv[:, :kept])
            )


def input_grads(first_g, dq, dk, dv, wq, wk, wv):
    _, length, width = first_g.shape
    per_width = pl.BlockSpec((1, length, width), lambda w: (w, 0, 0))
    return call(
        input_kernel,
        15 * length * width * width,
        80 * length * width,
        grid=(WIDTHS,),
        in_specs=[per_width] * 4 + [whole(wq.shape)] * 3,
        out_specs=per_width,
        out_shape=shape_of(first_g.shape, F32),
        name="input_grads",
    )(first_g, dq, dk, dv, wq, wk, wv)


def local_step(x, segments, og, weights, vectors):
    wq, wk, wv, wo, wi, wu = weights
    bq, bv, bo, ga, sa, bu, gb, sb, bi = vectors
    row = lambda vector: vector.reshape(1, -1)
    q, k, v, att, p = attend(x, wq, wk, wv, row(bq), row(bv), segments)
    vec_a = jnp.concatenate([row(bo), row(ga), row(sa), row(bu)] + [row(bu)] * 4, axis=0)
    first, normed, normed_t, second, x_t = first_norm(x, att, wo, vec_a)
    vec_b = jnp.concatenate([row(gb), row(sb)] * 4, axis=0)
    act, slope, out, feed, feed_t, second_g, sums_b = feed_forward(
        normed, wi, wu, bi.reshape(WIDTHS, 1, -1), second, og, vec_b
    )
    outer_hi, inner_hi, grad, bias_hi = feed_backward((3, 2), feed, feed_t, normed_t, act, slope, second_g, wi, wu, None)
    outer_lo, inner_lo, grad, bias_lo = feed_backward((1, 0), feed, feed_t, normed_t, act, slope, second_g, wi, wu, grad)
    first_g, att_g, wo_g, sums_a = first_backward(first, grad, wo, att, vec_a)
    dq, dk, dv, dqs, dks, dvs, sums_c = attend_backward(q, k, v, p, att_g)
    wq_g, wk_g, wv_g = project_grads(x_t, dqs, dks, dvs)
    in_g = input_grads(first_g, dq, dk, dv, wq, wk, wv)
    return (out, in_g, (wq_g, wk_g, wv_g, wo_g), (inner_lo, inner_hi, outer_lo, outer_hi),
            (sums_c[0], sums_c[1], sums_a[2], sums_a[0], sums_a[1], sums_b[2], sums_b[0], sums_b[1],
             jnp.concatenate([bias_lo.reshape(-1), bias_hi.reshape(-1)])))


class Ring:
    def __init__(self, mesh):
        self.dp = mesh.shape["dp"]
        self.fsdp = mesh.shape["fsdp"]
        self.square = self.fsdp == 8 and self.dp % 2 == 0
        index = lax.axis_index("fsdp")
        self.z = lax.axis_index("dp")
        self.y, self.x, self.c = index // 4, (index // 2) % 2, index % 2

    def swap(self, value, bit):
        total = self.dp * self.fsdp
        return lax.ppermute(value, AXES, [(i, i ^ bit) for i in range(total)])

    def shift(self, value, by):
        total = self.dp * self.fsdp
        return lax.ppermute(value, AXES, [(i, (i + by * self.fsdp) % total) for i in range(total)])


CORE, X_SIDE, Y_SIDE = 1, 2, 4


def gather_rows(ring, shard):
    if not ring.square:
        return lax.all_gather(shard, AXES, axis=0, tiled=True)
    dp, half = ring.dp, ring.dp // 2
    rows, columns = shard.shape
    line = jnp.zeros((dp, rows, columns), shard.dtype)
    line = lax.dynamic_update_slice(line, shard[None], (ring.z, 0, 0))
    for by in range(1, dp):
        came = ring.shift(shard, by)
        line = lax.dynamic_update_slice(line, came[None], ((ring.z + dp - by) % dp, 0, 0))
    from_x = ring.swap(line, X_SIDE)
    from_y = ring.swap(line, Y_SIDE)
    corner_a = ring.swap(from_x[:half], Y_SIDE)
    corner_b = ring.swap(from_y[half:], X_SIDE)
    parts = (
        (line, 0, ring.y, ring.x),
        (from_x, 0, ring.y, 1 - ring.x),
        (from_y, 0, 1 - ring.y, ring.x),
        (corner_a, 0, 1 - ring.y, 1 - ring.x),
        (corner_b, half, 1 - ring.y, 1 - ring.x),
    )
    full = jnp.zeros((dp, 2, 2, 2, rows, columns), shard.dtype)
    for value, z, y, x in parts:
        for core, piece in ((ring.c, value), (1 - ring.c, ring.swap(value, CORE))):
            block = piece.reshape(piece.shape[0], 1, 1, 1, rows, columns)
            full = lax.dynamic_update_slice(full, block, (z, y, x, core, 0, 0))
    return full.reshape(dp * 8 * rows, columns)


def scatter_rows(ring, parts):
    if not ring.square:
        return lax.psum_scatter(
            jnp.concatenate(parts, axis=1).astype(F32), AXES, scatter_dimension=0, tiled=True
        )
    dp, half = ring.dp, ring.dp // 2
    rows = parts[0].shape[0] // (dp * 8)
    folded = [part.reshape(dp, 2, 2, 2, rows, part.shape[1]) for part in parts]

    def of_core(core):
        return jnp.concatenate(
            [lax.dynamic_index_in_dim(part, core, 3, keepdims=False) for part in folded], axis=-1
        )

    kept = of_core(ring.c)
    came = ring.swap(of_core(1 - ring.c), CORE)

    def block(y, x):
        def pick(value):
            value = lax.dynamic_index_in_dim(value, y, 1, keepdims=False)
            return lax.dynamic_index_in_dim(value, x, 1, keepdims=False)

        return pick(kept).astype(F32) + pick(came).astype(F32)

    corner = block(1 - ring.y, 1 - ring.x).astype(BF)
    corner_a = ring.swap(corner[:half], Y_SIDE).astype(F32)
    corner_b = ring.swap(corner[half:], X_SIDE).astype(F32)
    zeros = jnp.zeros_like(corner_a)
    to_x = (block(ring.y, 1 - ring.x) + jnp.concatenate([corner_a, zeros], axis=0)).astype(BF)
    to_y = (block(1 - ring.y, ring.x) + jnp.concatenate([zeros, corner_b], axis=0)).astype(BF)
    line = (
        block(ring.y, ring.x)
        + ring.swap(to_x, X_SIDE).astype(F32)
        + ring.swap(to_y, Y_SIDE).astype(F32)
    )
    total = lax.dynamic_index_in_dim(line, ring.z, 0, keepdims=False)
    low = line.astype(BF)
    for by in range(1, dp):
        sent = lax.dynamic_index_in_dim(low, (ring.z + by) % dp, 0, keepdims=False)
        total = total + ring.shift(sent, by).astype(F32)
    return total


def solution(mesh):
    rows_split = P(AXES, None)
    vector_split = P(AXES)

    def per_device(
        tokens,
        segment_ids,
        output_grad,
        query_weight,
        query_bias,
        key_weight,
        value_weight,
        value_bias,
        output_weight,
        output_bias,
        first_gain,
        first_shift,
        inner_weight,
        inner_bias,
        outer_weight,
        outer_bias,
        second_gain,
        second_shift,
    ):
        ring = Ring(mesh)
        width = tokens.shape[1]
        hidden = inner_weight.shape[1]
        ratio = hidden // width
        own = query_bias.shape[0]
        singles = (query_bias, value_bias, output_bias, first_gain, first_shift, outer_bias, second_gain, second_shift)
        count = len(singles)
        columns = jnp.concatenate([jnp.stack(singles, axis=1), inner_bias.reshape(own, ratio)], axis=1)
        columns = jnp.pad(columns, ((0, 0), (0, BLOCK - columns.shape[1])))
        attention = gather_rows(
            ring, jnp.concatenate([query_weight, key_weight, value_weight, output_weight, columns], axis=1)
        )
        wi = gather_rows(ring, inner_weight)
        wu = gather_rows(ring, outer_weight)
        wq, wk, wv, wo = [attention[:, n * width : (n + 1) * width] for n in range(4)]
        columns = attention[:, 4 * width :].astype(F32)
        vectors = [columns[:, n] for n in range(count)] + [columns[:, count : count + ratio].reshape(hidden)]
        out, in_g, attention_g, feed_g, vectors_g = local_step(
            tokens, segment_ids[0], output_grad, (wq, wk, wv, wo, wi, wu), vectors
        )
        high = scatter_rows(ring, feed_g[1::2])
        low = scatter_rows(ring, feed_g[0::2])
        columns_g = jnp.concatenate(
            [jnp.stack(vectors_g[:count], axis=1), vectors_g[count].reshape(width, ratio)], axis=1
        )
        columns_g = jnp.pad(columns_g, ((0, 0), (0, BLOCK - columns_g.shape[1]))).astype(BF)
        rest = scatter_rows(ring, list(attention_g) + [columns_g])
        split = hidden // 2
        inner_g = jnp.concatenate([low[:, :split], high[:, :split]], axis=1)
        outer_g = jnp.concatenate([low[:, split:], high[:, split:]], axis=1)
        wq_g, wk_g, wv_g, wo_g = [rest[:, n * width : (n + 1) * width] for n in range(4)]
        columns_g = rest[:, 4 * width :]
        bq_g, bv_g, bo_g, ga_g, sa_g, bu_g, gb_g, sb_g = [columns_g[:, n] for n in range(count)]
        bi_g = columns_g[:, count : count + ratio].reshape(own * ratio)
        return (
            out, in_g, wq_g, bq_g, wk_g, wv_g, bv_g, wo_g, bo_g, ga_g, sa_g, inner_g, bi_g, outer_g, bu_g, gb_g, sb_g,
        )

    layered = P(None, AXES, None)
    return jax.shard_map(
        per_device,
        mesh=mesh,
        in_specs=(
            rows_split, rows_split, layered, rows_split, vector_split, rows_split, rows_split, vector_split,
            rows_split, vector_split, vector_split, vector_split, rows_split, vector_split, rows_split,
            vector_split, vector_split, vector_split,
        ),
        out_specs=(
            layered, layered, rows_split, vector_split, rows_split, rows_split, vector_split, rows_split,
            vector_split, vector_split, vector_split, rows_split, vector_split, rows_split, vector_split,
            vector_split, vector_split,
        ),
        check_vma=False,
    )
```

time: 1580 us -> 425 us (0.27)
  blocking collectives: 560 us -> 0 us
  waiting for transfers between devices: 596 us -> 104 us
  matrix products: 247 us -> 0 us
  Pallas kernels: 0 us -> 179 us
  starting transfers between devices: 1.3 us -> 58.4 us
  other arithmetic: 68 us -> 19.6 us
  local copies, waits for them, and re-layouts: 82.7 us -> 54 us
    all_gather x12 -> x0, blocking collectives: 477 us -> none  [the longest x3 123 us: per_device(): lax.all_gather(value_weight[:, :width_kept], ('dp', 'fsdp'), axis=0, tile...]
    reduce_scatter x2 -> x0, waiting for transfers between devices: 283 us -> none  [the longest x1 142 us: per_device(): lax.psum_scatter(totals[11], ('dp', 'fsdp'), scatter_dimension=0, tiled=T...]
    unnamed x22 -> x0, waiting for transfers between devices: 249 us -> none
    dot_general x96 -> x0, matrix products: 247 us -> none  [the longest x24 90.7 us: matmul(): return jnp.dot(left_side, right_side, preferred_element_type=jnp.float32)]
    pallas_call x0 -> x9, Pallas kernels: none -> 179 us  [the longest x2 52.3 us: feed_backward(): call(kernel, 8 * steps * length * width * width, steps * 12 * length * wi...]
    ppermute x0 -> x60, waiting for transfers between devices: none -> 104 us  [the longest x42 76.7 us: swap(): return lax.ppermute(value, AXES, [(i, i ^ bit) for i in range(total)])]
    unnamed x2 -> x0, blocking collectives: 83.3 us -> none
    all_gather x12 -> x0, waiting for transfers between devices: 64.6 us -> none  [the longest x4 44.3 us: per_device(): lax.all_gather(outer_weight[:, :hidden_kept], ('dp', 'fsdp'), axis=0, til...]
  transfers between devices with their start and end apart: 18 -> 60, of which waited for: 7 -> 25; matrix products, arithmetic and copies ran while one was open for 15% -> 12% of each run, Pallas kernels for 0% -> 10%
where the time goes in v1:
time: 425 us; the launch traced here: 417 us
  Pallas kernels  179 us (42%)
  waiting for transfers between devices  104 us (24%)
  starting transfers between devices  58.4 us (14%)
  local copies, waits for them, and re-layouts  54 us (13%)
  other arithmetic  19.6 us (5%)
    ppermute x42, waiting for transfers between devices, swap(): return lax.ppermute(value, AXES, [(i, i ^ bit) for i in range(total)])  76.7 us
    pallas_call x2, Pallas kernels, feed_backward(): call(kernel, 8 * steps * length * width * width, steps * 12 * length * wi...  52.3 us
    pallas_call x1, Pallas kernels, feed_forward(): call(feed_kernel, 4 * steps * length * width * width, steps * 8 * length...  39.9 us
    ppermute x42, starting transfers between devices, swap(): return lax.ppermute(value, AXES, [(i, i ^ bit) for i in range(total)])  29.9 us
    ppermute x18, starting transfers between devices, shift(): lax.ppermute(value, AXES, [(i, (i + by * self.fsdp) % total) for i in ran...  28.5 us
    ppermute x18, waiting for transfers between devices, shift(): lax.ppermute(value, AXES, [(i, (i + by * self.fsdp) % total) for i in ran...  27.3 us
    pallas_call x1, Pallas kernels, attend_backward(): call(attend_back_kernel, 40 * length * 3 * BLOCK * width, 24 * length * w...  23.8 us
    pallas_call x1, Pallas kernels, attend(): call(attend_kernel, 6 * length * width * width, 16 * length * width, grid...  20.9 us
  transfers between devices with their start and end apart: 60, of which 25 were waited for; matrix products, arithmetic and copies ran while one was open for 12% of the time, Pallas kernels for 10%

profile of v1, /device:TPU:0, one launch (start us, length us, event | category | flops | bytes accessed | tf_op | source)
XLA Modules:
  0.0 417.0 jit_solution(12322601421753641251)
XLA Ops:
  0.7 3.1 collective-permute-start.12
  3.8 2.1 collective-permute-start.14
  8.4 2.2 collective-permute-start.26
  22.7 3.9 collective-permute-start.25
  26.6 6.2 %collective-permute-done.25 = bf16[24,3072]{1,0:T(8,128)(2,1)S(1)} collective-permute-done((bf16[24,3072]{1,0:T(8,128)(2,1)S(1)}, bf16[24,3072]{1,0:T(8,128)(2,1)S(1)}, u32[]{:S(2)}, u32[]{:S(2)}) %collective-permute-start.25) | collective-permute-done | bytes 147488 | tf_op jit(solution)/shard_map/ppermute | solution.py:645
  35.7 1.6 collective-permute-start.30
  39.5 4.5 %collective-permute-done = bf16[24,3200]{1,0:T(8,128)(2,1)S(1)} collective-permute-done((bf16[24,3200]{1,0:T(8,128)(2,1)S(1)}, bf16[24,3200]{1,0:T(8,128)(2,1)S(1)}, u32[]{:S(2)}, u32[]{:S(2)}) %collective-permute-start) | collective-permute-done | bytes 153632 | tf_op jit(solution)/shard_map/ppermute | solution.py:645
  48.1 3.9 collective-permute-done.30
  52.1 1.6 collective-permute-done.28
  54.2 10.5 %collective-permute-done.18 = bf16[4,24,3072]{2,1,0:T(8,128)(2,1)S(1)} collective-permute-done((bf16[4,24,3072]{2,1,0:T(8,128)(2,1)S(1)}, bf16[4,24,3072]{2,1,0:T(8,128)(2,1)S(1)}, u32[]{:S(2)}, u32[]{:S(2)}) %collective-permute-start.18) | collective-permute-done | bytes 589856 | tf_op jit(solution)/shard_map/ppermute | solution.py:641
  67.1 1.6 collective-permute-start.32
  68.8 9.1 %collective-permute-done.6 = bf16[4,24,3200]{2,1,0:T(8,128)(2,1)S(1)} collective-permute-done((bf16[4,24,3200]{2,1,0:T(8,128)(2,1)S(1)}, bf16[4,24,3200]{2,1,0:T(8,128)(2,1)S(1)}, u32[]{:S(2)}, u32[]{:S(2)}) %collective-permute-start.6) | collective-permute-done | bytes 614432 | tf_op jit(solution)/shard_map/ppermute | solution.py:641
  79.4 2.1 collective-permute-done.4
  83.3 1.8 collective-permute-done.17
  85.3 1.7 collective-permute-done.29
  87.4 1.7 collective-permute-done.19
  89.3 1.8 collective-permute-done.31
  95.6 1.8 collective-permute-done.33
  98.0 2.4 collective-permute-done.10
  104.7 2.6 fusion.41
  107.3 1.6 slice_reduce_fusion
  112.5 20.9 %attend.1 = (bf16[512,768]{1,0:T(8,128)(2,1)}, bf16[512,768]{1,0:T(8,128)(2,1)}, bf16[512,768]{1,0:T(8,128)(2,1)}, bf16[512,768]{1,0:T(8,128)(2,1)}, bf16[12,4,128,384]{3,2,1,0:T(8,128)(2,1)}) custom-call(bf16[512,768]{1,0:T(8,128)(2,1)} %x.19, bf16[768,768]{1,0:T(8,128)(2,1)} %get-tuple-element.122.wq, bf16[768,768]{1,0:T(8,128)(2,1)} %get-tuple-element.121.wk, ...), custom_call_target="tpu_custom_call" | custom-call | flops 1811939328 | bytes 6291456 | tf_op jit(solution)/shard_map/attend/pallas_call | solution.py:105
  133.4 9.2 %first_norm.1 = (f32[4,512,768]{2,1,0:T(8,128)}, bf16[4,512,768]{2,1,0:T(8,128)(2,1)}, bf16[4,768,512]{2,1,0:T(8,128)(2,1)}, f32[4,512,768]{2,1,0:T(8,128)}, bf16[768,512]{1,0:T(8,128)(2,1)}) custom-call(bf16[512,768]{1,0:T(8,128)(2,1)} %x.19, bf16[512,768]{1,0:T(8,128)(2,1)} %get-tuple-element.56.att_a.att_b, ...), custom_call_target="tpu_custom_call" | custom-call | flops 603979776 | bytes 15728640 | tf_op jit(solution)/shard_map/first_norm/pallas_call | solution.py:166
  142.5 39.9 %feed_forward.1 = (bf16[10,512,768]{2,1,0:T(8,128)(2,1)}, bf16[10,512,768]{2,1,0:T(8,128)(2,1)}, bf16[4,512,768]{2,1,0:T(8,128)(2,1)}, bf16[4,512,768]{2,1,0:T(8...) custom-call(s32[10]{0:T(128)} %constant.890.clone.j_of, ...), custom_call_target="tpu_custom_call" | custom-call | flops 12079595520 | bytes 31457280 | tf_op jit(solution)/shard_map/feed_forward/pallas_call | solution.py:260
  183.2 18.0 %feed_backward.2 = (bf16[768,1536]{1,0:T(8,128)(2,1)}, bf16[768,1536]{1,0:T(8,128)(2,1)}, f32[4,512,768]{2,1,0:T(8,128)}, f32[2,1,768]{2,1,0:T(1,128)}) custom-call(s32[3]{0:T(128)} %constant.892.clone.refs_0_, s32[3]{0:T(128)} %constant.893.clone.refs_1_, s32[3]{0:T(128)} %constant.894.clone.refs_2_, bf16[4,512,768]{2,1,0:T(8,128)(2,1)} %get-tuple-element.61.refs_3_.feed, ...), custom_call_target="tpu_custom_call" | custom-call | flops 7247757312 | bytes 14155776 | tf_op jit(solution)/shard_map/feed_backward/pallas_call | solution.py:371
  201.2 34.3 %feed_backward.3 = (bf16[768,1536]{1,0:T(8,128)(2,1)}, bf16[768,1536]{1,0:T(8,128)(2,1)}, f32[4,512,768]{2,1,0:T(8,128)}, f32[2,1,768]{2,1,0:T(1,128)}) custom-call(s32[7]{0:T(128)} %constant.895.clone.j_of, s32[7]{0:T(128)} %constant.896.clone.w_of, s32[7]{0:T(128)} %constant.897.clone.s_of, bf16[4,512,768]{2,1,0:T(8,128)(2,1)} %get-tuple-element.61.refs_3_.feed, ...), custom_call_target="tpu_custom_call" | custom-call | flops 16911433728 | bytes 33030144 | tf_op jit(solution)/shard_map/feed_backward/pallas_call | solution.py:371
  236.2 14.4 %first_backward.1 = (f32[4,512,768]{2,1,0:T(8,128)}, bf16[4,512,768]{2,1,0:T(8,128)(2,1)}, bf16[768,768]{1,0:T(8,128)(2,1)}, f32[8,768]{1,0:T(8,128)}) custom-call(f32[4,512,768]{2,1,0:T(8,128)} %get-tuple-element.60.first, f32[4,512,768]{2,1,0:T(8,128)} %get-tuple-element.68.normed_g, bf16[768,768]{1,0:T(8,128)(2,1)} %get-tuple-element.119.wo_a.wo_b.wo, ...), custom_call_target="tpu_custom_call" | custom-call | flops 3019898880 | bytes 23592960 | tf_op jit(solution)/shard_map/first_backward/pallas_call | solution.py:435
  253.2 3.0 dynamic-slice_bitcast_fusion.4
  262.1 23.8 %attend_backward.1 = (bf16[4,512,768]{2,1,0:T(8,128)(2,1)}, bf16[4,512,768]{2,1,0:T(8,128)(2,1)}, bf16[4,512,768]{2,1,0:T(8,128)(2,1)}, bf16[512,768]{1,0:T(8,12...) custom-call(bf16[512,768]{1,0:T(8,128)(2,1)} %get-tuple-element.70.q, ...), custom_call_target="tpu_custom_call" | custom-call | flops 6039797760 | bytes 9437184 | tf_op jit(solution)/shard_map/attend_backward/pallas_call | solution.py:539
  287.8 5.8 %project_grads.1 = (bf16[768,768]{1,0:T(8,128)(2,1)}, bf16[768,768]{1,0:T(8,128)(2,1)}, bf16[768,768]{1,0:T(8,128)(2,1)}) custom-call(bf16[768,512]{1,0:T(8,128)(2,1)} %get-tuple-element.78.x_t, bf16[512,768]{1,0:T(8,128)(2,1)} %get-tuple-element.79.dq, bf16[512,768]{1,0:T(8,128)(2,1)} %get-tuple-element.80.dk, bf16[512,768]{1,0:T(8,128)(2,1)} %get-tuple-element.81.dv), custom_call_target="tpu_custom_call" | custom-call | flops 1811939328 | bytes 6291456 | tf_op jit(solution)/shard_map/project_grads/pallas_call | solution.py:566
  293.6 2.4 dynamic-slice_bitcast_fusion.10
  296.0 2.0 concatenate.86
  311.2 12.7 %input_grads.1 = f32[4,512,768]{2,1,0:T(8,128)} custom-call(f32[4,512,768]{2,1,0:T(8,128)} %get-tuple-element.69.first_g, bf16[4,512,768]{2,1,0:T(8,128)(2,1)} %get-tuple-element.75.dq, bf16[4,512,768]{2,1,0:T(8,128)(2,1)} %get-tuple-element.76.dk, bf16[4,512,768]{2,1,0:T(8,128)(2,1)} %get-tuple-element.77.dv, bf16[768,768]{1,0:T(8,128)(2,1)} %get-tuple-element.122.wq, ...), custom_call_target="tpu_custom_call" | custom-call | flops 4529848320 | bytes 31457280 | tf_op jit(solution)/shard_map/input_grads/pallas_call | solution.py:596
  332.7 2.4 collective-permute-done.45
  336.3 1.7 fusion.13
  339.0 2.6 collective-permute-done.53
  342.1 1.7 fusion.11
  344.9 3.2 collective-permute-done.37
  348.6 2.0 fusion.3
  351.8 9.5 %collective-permute-done.46 = bf16[4,24,3072]{2,1,0:T(8,128)(2,1)S(1)} collective-permute-done((bf16[4,24,3072]{2,1,0:T(8,128)(2,1)S(1)}, bf16[4,24,3072]{2,1,0:T(8,128)(2,1)S(1)}, u32[]{:S(2)}, u32[]{:S(2)}) %collective-permute-start.46) | collective-permute-done | bytes 589856 | tf_op jit(solution)/shard_map/ppermute | solution.py:641
  365.2 8.7 %collective-permute-done.54 = bf16[4,24,3072]{2,1,0:T(8,128)(2,1)S(1)} collective-permute-done((bf16[4,24,3072]{2,1,0:T(8,128)(2,1)S(1)}, bf16[4,24,3072]{2,1,0:T(8,128)(2,1)S(1)}, u32[]{:S(2)}, u32[]{:S(2)}) %collective-permute-start.54) | collective-permute-done | bytes 589856 | tf_op jit(solution)/shard_map/ppermute | solution.py:641
  373.9 2.6 collective-permute-start.51
  378.0 7.8 %collective-permute-done.38 = bf16[4,24,3200]{2,1,0:T(8,128)(2,1)S(1)} collective-permute-done((bf16[4,24,3200]{2,1,0:T(8,128)(2,1)S(1)}, bf16[4,24,3200]{2,1,0:T(8,128)(2,1)S(1)}, u32[]{:S(2)}, u32[]{:S(2)}) %collective-permute-start.38) | collective-permute-done | bytes 614432 | tf_op jit(solution)/shard_map/ppermute | solution.py:641
  386.7 2.9 collective-permute-start.59
  389.6 1.6 fusion.39
  392.8 2.5 collective-permute-start.43
  396.5 10.3 %collective-permute-done.58 = bf16[24,3072]{1,0:T(8,128)(2,1)S(1)} collective-permute-done((bf16[24,3072]{1,0:T(8,128)(2,1)S(1)}, bf16[24,3072]{1,0:T(8,128)(2,1)S(1)}, u32[]{:S(2)}, u32[]{:S(2)}) %collective-permute-start.58) | collective-permute-done | bytes 147488 | tf_op jit(solution)/shard_map/ppermute | solution.py:645
  408.4 5.9 %collective-permute-done.42 = bf16[24,3200]{1,0:T(8,128)(2,1)S(1)} collective-permute-done((bf16[24,3200]{1,0:T(8,128)(2,1)S(1)}, bf16[24,3200]{1,0:T(8,128)(2,1)S(1)}, u32[]{:S(2)}, u32[]{:S(2)}) %collective-permute-start.42) | collective-permute-done | bytes 153632 | tf_op jit(solution)/shard_map/ppermute | solution.py:645
  (259 shorter events, 95.4 us)
Async XLA Ops:
  0.7 33.7 %collective-permute-start.12 = (bf16[24,3072]{1,0:T(8,128)(2,1)}, bf16[24,3072]{1,0:T(8,128)(2,1)S(1)}, u32[]{:S(2)}, u32[]{:S(2)}) collective-permute-start(bf16[24,3072]{1,0:T(8,128)(2,1)} %param.38), channel_id=1, source_target_pairs={{0,8},{1,9},{2,10},{3,11},{4,12},{5,13},{6,14},{7,15},{8,16},{9,17... | collective-permute-start | bytes 442376 | tf_op jit(solution)/shard_map/ppermute | solution.py:645
  3.8 33.5 %collective-permute-start.14 = (bf16[24,3072]{1,0:T(8,128)(2,1)}, bf16[24,3072]{1,0:T(8,128)(2,1)S(1)}, u32[]{:S(2)}, u32[]{:S(2)}) collective-permute-start(bf16[24,3072]{1,0:T(8,128)(2,1)} %param.38), channel_id=1, source_target_pairs={{0,24},{1,25},{2,26},{3,27},{4,28},{5,29},{6,30},{7,31},{8,0},{9,1... | collective-permute-start | bytes 442376 | tf_op jit(solution)/shard_map/ppermute | solution.py:645
  5.8 29.8 %collective-permute-start.13 = (bf16[24,3072]{1,0:T(8,128)(2,1)}, bf16[24,3072]{1,0:T(8,128)(2,1)S(1)}, u32[]{:S(2)}, u32[]{:S(2)}) collective-permute-start(bf16[24,3072]{1,0:T(8,128)(2,1)} %param.38), channel_id=1, source_target_pairs={{0,16},{1,17},{2,18},{3,19},{4,20},{5,21},{6,22},{7,23},{8,24},{9,... | collective-permute-start | bytes 442376 | tf_op jit(solution)/shard_map/ppermute | solution.py:645
  6.8 15.9 %collective-permute-start.24 = (bf16[24,3072]{1,0:T(8,128)(2,1)}, bf16[24,3072]{1,0:T(8,128)(2,1)S(1)}, u32[]{:S(2)}, u32[]{:S(2)}) collective-permute-start(bf16[24,3072]{1,0:T(8,128)(2,1)} %param.40), channel_id=1, source_target_pairs={{0,8},{1,9},{2,10},{3,11},{4,12},{5,13},{6,14},{7,15},{8,16},{9,17... | collective-permute-start | bytes 442376 | tf_op jit(solution)/shard_map/ppermute | solution.py:645
  8.4 25.3 %collective-permute-start.26 = (bf16[24,3072]{1,0:T(8,128)(2,1)}, bf16[24,3072]{1,0:T(8,128)(2,1)S(1)}, u32[]{:S(2)}, u32[]{:S(2)}) collective-permute-start(bf16[24,3072]{1,0:T(8,128)(2,1)} %param.40), channel_id=1, source_target_pairs={{0,24},{1,25},{2,26},{3,27},{4,28},{5,29},{6,30},{7,31},{8,0},{9,1... | collective-permute-start | bytes 442376 | tf_op jit(solution)/shard_map/ppermute | solution.py:645
  22.7 10.1 %collective-permute-start.25 = (bf16[24,3072]{1,0:T(8,128)(2,1)S(1)}, bf16[24,3072]{1,0:T(8,128)(2,1)S(1)}, u32[]{:S(2)}, u32[]{:S(2)}) collective-permute-start(bf16[24,3072]{1,0:T(8,128)(2,1)S(1)} %copy-done.12), channel_id=1, source_target_pairs={{0,16},{1,17},{2,18},{3,19},{4,20},{5,21},{6,22},{7,23},{8,24},{9,... | collective-permute-start | bytes 442376 | tf_op jit(solution)/shard_map/ppermute | solution.py:645
  32.8 14.8 %collective-permute-start.2 = (bf16[24,3200]{1,0:T(8,128)(2,1)S(1)}, bf16[24,3200]{1,0:T(8,128)(2,1)S(1)}, u32[]{:S(2)}, u32[]{:S(2)}) collective-permute-start(bf16[24,3200]{1,0:T(8,128)(2,1)S(1)} %constant_dynamic-update-slice_fusion), channel_id=1, source_target_pairs={{0,24},{1,25},{2,26},{3,27},{4,28},{5,29},{6,30},{7,31},{8,0},{9,1... | collective-permute-start | bytes 460808 | tf_op jit(solution)/shard_map/ppermute | solution.py:645
  33.7 12.4 %collective-permute-start.1 = (bf16[24,3200]{1,0:T(8,128)(2,1)S(1)}, bf16[24,3200]{1,0:T(8,128)(2,1)S(1)}, u32[]{:S(2)}, u32[]{:S(2)}) collective-permute-start(bf16[24,3200]{1,0:T(8,128)(2,1)S(1)} %constant_dynamic-update-slice_fusion), channel_id=1, source_target_pairs={{0,16},{1,17},{2,18},{3,19},{4,20},{5,21},{6,22},{7,23},{8,24},{9,... | collective-permute-start | bytes 460808 | tf_op jit(solution)/shard_map/ppermute | solution.py:645
  34.4 9.6 %collective-permute-start = (bf16[24,3200]{1,0:T(8,128)(2,1)S(1)}, bf16[24,3200]{1,0:T(8,128)(2,1)S(1)}, u32[]{:S(2)}, u32[]{:S(2)}) collective-permute-start(bf16[24,3200]{1,0:T(8,128)(2,1)S(1)} %constant_dynamic-update-slice_fusion), channel_id=1, source_target_pairs={{0,8},{1,9},{2,10},{3,11},{4,12},{5,13},{6,14},{7,15},{8,16},{9,17... | collective-permute-start | bytes 460808 | tf_op jit(solution)/shard_map/ppermute | solution.py:645
  35.7 16.3 %collective-permute-start.30 = (bf16[4,24,3072]{2,1,0:T(8,128)(2,1)S(1)}, bf16[4,24,3072]{2,1,0:T(8,128)(2,1)S(1)}, u32[]{:S(2)}, u32[]{:S(2)}) collective-permute-start(bf16[4,24,3072]{2,1,0:T(8,128)(2,1)S(1)} %bitcast_dynamic-update-slice_fusion.38), channel_id=1, source_target_pairs={{0,4},{1,5},{2,6},{3,7},{4,0},{5,1},{6,2},{7,3},{8,12},{9,13},{10,... | collective-permute-start | bytes 1769480 | tf_op jit(solution)/shard_map/ppermute | solution.py:641
  37.3 16.3 %collective-permute-start.28 = (bf16[4,24,3072]{2,1,0:T(8,128)(2,1)S(1)}, bf16[4,24,3072]{2,1,0:T(8,128)(2,1)S(1)}, u32[]{:S(2)}, u32[]{:S(2)}) collective-permute-start(bf16[4,24,3072]{2,1,0:T(8,128)(2,1)S(1)} %bitcast_dynamic-update-slice_fusion.38), channel_id=1, source_target_pairs={{0,2},{1,3},{2,0},{3,1},{4,6},{5,7},{6,4},{7,5},{8,10},{9,11},{10,... | collective-permute-start | bytes 1769480 | tf_op jit(solution)/shard_map/ppermute | solution.py:641
  44.0 20.6 %collective-permute-start.18 = (bf16[4,24,3072]{2,1,0:T(8,128)(2,1)S(1)}, bf16[4,24,3072]{2,1,0:T(8,128)(2,1)S(1)}, u32[]{:S(2)}, u32[]{:S(2)}) collective-permute-start(bf16[4,24,3072]{2,1,0:T(8,128)(2,1)S(1)} %bitcast_dynamic-update-slice_fusion.42), channel_id=1, source_target_pairs={{0,4},{1,5},{2,6},{3,7},{4,0},{5,1},{6,2},{7,3},{8,12},{9,13},{10,... | collective-permute-start | bytes 1769480 | tf_op jit(solution)/shard_map/ppermute | solution.py:641
  46.1 20.1 %collective-permute-start.16 = (bf16[4,24,3072]{2,1,0:T(8,128)(2,1)S(1)}, bf16[4,24,3072]{2,1,0:T(8,128)(2,1)S(1)}, u32[]{:S(2)}, u32[]{:S(2)}) collective-permute-start(bf16[4,24,3072]{2,1,0:T(8,128)(2,1)S(1)} %bitcast_dynamic-update-slice_fusion.42), channel_id=1, source_target_pairs={{0,2},{1,3},{2,0},{3,1},{4,6},{5,7},{6,4},{7,5},{8,10},{9,11},{10,... | collective-permute-start | bytes 1769480 | tf_op jit(solution)/shard_map/ppermute | solution.py:641
  47.6 18.7 %collective-permute-start.15 = (bf16[4,24,3072]{2,1,0:T(8,128)(2,1)S(1)}, bf16[4,24,3072]{2,1,0:T(8,128)(2,1)S(1)}, u32[]{:S(2)}, u32[]{:S(2)}) collective-permute-start(bf16[4,24,3072]{2,1,0:T(8,128)(2,1)S(1)} %bitcast_dynamic-update-slice_fusion.42), channel_id=1, source_target_pairs={{0,1},{1,0},{2,3},{3,2},{4,5},{5,4},{6,7},{7,6},{8,9},{9,8},{10,11... | collective-permute-start | bytes 1769480 | tf_op jit(solution)/shard_map/ppermute | solution.py:641
  52.0 15.0 %collective-permute-start.27 = (bf16[4,24,3072]{2,1,0:T(8,128)(2,1)S(1)}, bf16[4,24,3072]{2,1,0:T(8,128)(2,1)S(1)}, u32[]{:S(2)}, u32[]{:S(2)}) collective-permute-start(bf16[4,24,3072]{2,1,0:T(8,128)(2,1)S(1)} %bitcast_dynamic-update-slice_fusion.38), channel_id=1, source_target_pairs={{0,1},{1,0},{2,3},{3,2},{4,5},{5,4},{6,7},{7,6},{8,9},{9,8},{10,11... | collective-permute-start | bytes 1769480 | tf_op jit(solution)/shard_map/ppermute | solution.py:641
  53.6 24.2 %collective-permute-start.6 = (bf16[4,24,3200]{2,1,0:T(8,128)(2,1)S(1)}, bf16[4,24,3200]{2,1,0:T(8,128)(2,1)S(1)}, u32[]{:S(2)}, u32[]{:S(2)}) collective-permute-start(bf16[4,24,3200]{2,1,0:T(8,128)(2,1)S(1)} %bitcast_dynamic-update-slice_fusion.34), channel_id=1, source_target_pairs={{0,4},{1,5},{2,6},{3,7},{4,0},{5,1},{6,2},{7,3},{8,12},{9,13},{10,... | collective-permute-start | bytes 1843208 | tf_op jit(solution)/shard_map/ppermute | solution.py:641
  64.7 16.8 %collective-permute-start.4 = (bf16[4,24,3200]{2,1,0:T(8,128)(2,1)S(1)}, bf16[4,24,3200]{2,1,0:T(8,128)(2,1)S(1)}, u32[]{:S(2)}, u32[]{:S(2)}) collective-permute-start(bf16[4,24,3200]{2,1,0:T(8,128)(2,1)S(1)} %bitcast_dynamic-update-slice_fusion.34), channel_id=1, source_target_pairs={{0,2},{1,3},{2,0},{3,1},{4,6},{5,7},{6,4},{7,5},{8,10},{9,11},{10,... | collective-permute-start | bytes 1843208 | tf_op jit(solution)/shard_map/ppermute | solution.py:641
  66.2 16.8 %collective-permute-start.3 = (bf16[4,24,3200]{2,1,0:T(8,128)(2,1)S(1)}, bf16[4,24,3200]{2,1,0:T(8,128)(2,1)S(1)}, u32[]{:S(2)}, u32[]{:S(2)}) collective-permute-start(bf16[4,24,3200]{2,1,0:T(8,128)(2,1)S(1)} %bitcast_dynamic-update-slice_fusion.34), channel_id=1, source_target_pairs={{0,1},{1,0},{2,3},{3,2},{4,5},{5,4},{6,7},{7,6},{8,9},{9,8},{10,11... | collective-permute-start | bytes 1843208 | tf_op jit(solution)/shard_map/ppermute | solution.py:641
  66.3 31.2 %collective-permute-start.34 = (bf16[2,24,3072]{2,1,0:T(8,128)(2,1)S(1)}, bf16[2,24,3072]{2,1,0:T(8,128)(2,1)S(1)}, u32[]{:S(2)}, u32[]{:S(2)}) collective-permute-start(bf16[2,24,3072]{2,1,0:T(8,128)(2,1)S(1)} %slice.262), channel_id=1, source_target_pairs={{0,2},{1,3},{2,0},{3,1},{4,6},{5,7},{6,4},{7,5},{8,10},{9,11},{10,... | collective-permute-start | bytes 884744 | tf_op jit(solution)/shard_map/ppermute | solution.py:641
  67.1 26.2 %collective-permute-start.32 = (bf16[2,24,3072]{2,1,0:T(8,128)(2,1)S(1)}, bf16[2,24,3072]{2,1,0:T(8,128)(2,1)S(1)}, u32[]{:S(2)}, u32[]{:S(2)}) collective-permute-start(bf16[2,24,3072]{2,1,0:T(8,128)(2,1)S(1)} %slice.261), channel_id=1, source_target_pairs={{0,4},{1,5},{2,6},{3,7},{4,0},{5,1},{6,2},{7,3},{8,12},{9,13},{10,... | collective-permute-start | bytes 884744 | tf_op jit(solution)/shard_map/ppermute | solution.py:641
  77.8 17.3 %collective-permute-start.22 = (bf16[2,24,3072]{2,1,0:T(8,128)(2,1)S(1)}, bf16[2,24,3072]{2,1,0:T(8,128)(2,1)S(1)}, u32[]{:S(2)}, u32[]{:S(2)}) collective-permute-start(bf16[2,24,3072]{2,1,0:T(8,128)(2,1)S(1)} %slice.260), channel_id=1, source_target_pairs={{0,2},{1,3},{2,0},{3,1},{4,6},{5,7},{6,4},{7,5},{8,10},{9,11},{10,... | collective-permute-start | bytes 884744 | tf_op jit(solution)/shard_map/ppermute | solution.py:641
  81.5 11.2 %collective-permute-start.20 = (bf16[2,24,3072]{2,1,0:T(8,128)(2,1)S(1)}, bf16[2,24,3072]{2,1,0:T(8,128)(2,1)S(1)}, u32[]{:S(2)}, u32[]{:S(2)}) collective-permute-start(bf16[2,24,3072]{2,1,0:T(8,128)(2,1)S(1)} %slice.259), channel_id=1, source_target_pairs={{0,4},{1,5},{2,6},{3,7},{4,0},{5,1},{6,2},{7,3},{8,12},{9,13},{10,... | collective-permute-start | bytes 884744 | tf_op jit(solution)/shard_map/ppermute | solution.py:641
  91.1 9.3 %collective-permute-start.10 = (bf16[2,24,3200]{2,1,0:T(8,128)(2,1)S(1)}, bf16[2,24,3200]{2,1,0:T(8,128)(2,1)S(1)}, u32[]{:S(2)}, u32[]{:S(2)}) collective-permute-start(bf16[2,24,3200]{2,1,0:T(8,128)(2,1)S(1)} %slice.247), channel_id=1, source_target_pairs={{0,2},{1,3},{2,0},{3,1},{4,6},{5,7},{6,4},{7,5},{8,10},{9,11},{10,... | collective-permute-start | bytes 921608 | tf_op jit(solution)/shard_map/ppermute | solution.py:641
  92.7 9.1 %collective-permute-start.8 = (bf16[2,24,3200]{2,1,0:T(8,128)(2,1)S(1)}, bf16[2,24,3200]{2,1,0:T(8,128)(2,1)S(1)}, u32[]{:S(2)}, u32[]{:S(2)}) collective-permute-start(bf16[2,24,3200]{2,1,0:T(8,128)(2,1)S(1)} %slice.246), channel_id=1, source_target_pairs={{0,4},{1,5},{2,6},{3,7},{4,0},{5,1},{6,2},{7,3},{8,12},{9,13},{10,... | collective-permute-start | bytes 921608 | tf_op jit(solution)/shard_map/ppermute | solution.py:641
  258.1 65.7 %collective-permute-start.44 = (bf16[4,2,2,24,3072]{4,3,0,2,1:T(8,128)(2,1)}, bf16[4,2,2,24,3072]{4,3,0,2,1:T(8,128)(2,1)}, u32[]{:S(2)}, u32[]{:S(2)}) collective-permute-start(bf16[4,2,2,24,3072]{4,3,0,2,1:T(8,128)(2,1)} %copy.322), channel_id=1, source_target_pairs={{0,1},{1,0},{2,3},{3,2},{4,5},{5,4},{6,7},{7,6},{8,9},{9,8},{10,11... | collective-permute-start | bytes 7077896 | tf_op jit(solution)/shard_map/ppermute | solution.py:641
  262.1 64.9 %collective-permute-start.52 = (bf16[4,2,2,24,3072]{4,3,0,2,1:T(8,128)(2,1)}, bf16[4,2,2,24,3072]{4,3,0,2,1:T(8,128)(2,1)}, u32[]{:S(2)}, u32[]{:S(2)}) collective-permute-start(bf16[4,2,2,24,3072]{4,3,0,2,1:T(8,128)(2,1)} %copy.323), channel_id=1, source_target_pairs={{0,1},{1,0},{2,3},{3,2},{4,5},{5,4},{6,7},{7,6},{8,9},{9,8},{10,11... | collective-permute-start | bytes 7077896 | tf_op jit(solution)/shard_map/ppermute | solution.py:641
  306.3 24.5 %collective-permute-start.36 = (bf16[4,2,2,24,3200]{4,3,0,2,1:T(8,128)(2,1)}, bf16[4,2,2,24,3200]{4,3,0,2,1:T(8,128)(2,1)}, u32[]{:S(2)}, u32[]{:S(2)}) collective-permute-start(bf16[4,2,2,24,3200]{4,3,0,2,1:T(8,128)(2,1)} %bitcast_dynamic-update-slice_fusion.46), channel_id=1, source_target_pairs={{0,1},{1,0},{2,3},{3,2},{4,5},{5,4},{6,7},{7,6},{8,9},{9,8},{10,11... | collective-permute-start | bytes 7372808 | tf_op jit(solution)/shard_map/ppermute | solution.py:641
  325.3 9.9 %collective-permute-start.45 = (bf16[2,24,3072]{2,1,0:T(8,128)(2,1)S(1)}, bf16[2,24,3072]{2,1,0:T(8,128)(2,1)S(1)}, u32[]{:S(2)}, u32[]{:S(2)}) collective-permute-start(bf16[2,24,3072]{2,1,0:T(8,128)(2,1)S(1)} %get-tuple-element.143), channel_id=1, source_target_pairs={{0,4},{1,5},{2,6},{3,7},{4,0},{5,1},{6,2},{7,3},{8,12},{9,13},{10,... | collective-permute-start | bytes 884744 | tf_op jit(solution)/shard_map/ppermute | solution.py:641
  325.8 10.4 %collective-permute-start.47 = (bf16[2,24,3072]{2,1,0:T(8,128)(2,1)S(1)}, bf16[2,24,3072]{2,1,0:T(8,128)(2,1)S(1)}, u32[]{:S(2)}, u32[]{:S(2)}) collective-permute-start(bf16[2,24,3072]{2,1,0:T(8,128)(2,1)S(1)} %get-tuple-element.144), channel_id=1, source_target_pairs={{0,2},{1,3},{2,0},{3,1},{4,6},{5,7},{6,4},{7,5},{8,10},{9,11},{10,... | collective-permute-start | bytes 884744 | tf_op jit(solution)/shard_map/ppermute | solution.py:641
  328.2 13.3 %collective-permute-start.53 = (bf16[2,24,3072]{2,1,0:T(8,128)(2,1)S(1)}, bf16[2,24,3072]{2,1,0:T(8,128)(2,1)S(1)}, u32[]{:S(2)}, u32[]{:S(2)}) collective-permute-start(bf16[2,24,3072]{2,1,0:T(8,128)(2,1)S(1)} %get-tuple-element.148), channel_id=1, source_target_pairs={{0,4},{1,5},{2,6},{3,7},{4,0},{5,1},{6,2},{7,3},{8,12},{9,13},{10,... | collective-permute-start | bytes 884744 | tf_op jit(solution)/shard_map/ppermute | solution.py:641
  329.8 12.3 %collective-permute-start.55 = (bf16[2,24,3072]{2,1,0:T(8,128)(2,1)S(1)}, bf16[2,24,3072]{2,1,0:T(8,128)(2,1)S(1)}, u32[]{:S(2)}, u32[]{:S(2)}) collective-permute-start(bf16[2,24,3072]{2,1,0:T(8,128)(2,1)S(1)} %get-tuple-element.149), channel_id=1, source_target_pairs={{0,2},{1,3},{2,0},{3,1},{4,6},{5,7},{6,4},{7,5},{8,10},{9,11},{10,... | collective-permute-start | bytes 884744 | tf_op jit(solution)/shard_map/ppermute | solution.py:641
  332.2 15.9 %collective-permute-start.37 = (bf16[2,24,3200]{2,1,0:T(8,128)(2,1)S(1)}, bf16[2,24,3200]{2,1,0:T(8,128)(2,1)S(1)}, u32[]{:S(2)}, u32[]{:S(2)}) collective-permute-start(bf16[2,24,3200]{2,1,0:T(8,128)(2,1)S(1)} %get-tuple-element.138), channel_id=1, source_target_pairs={{0,4},{1,5},{2,6},{3,7},{4,0},{5,1},{6,2},{7,3},{8,12},{9,13},{10,... | collective-permute-start | bytes 921608 | tf_op jit(solution)/shard_map/ppermute | solution.py:641
  335.2 13.4 %collective-permute-start.39 = (bf16[2,24,3200]{2,1,0:T(8,128)(2,1)S(1)}, bf16[2,24,3200]{2,1,0:T(8,128)(2,1)S(1)}, u32[]{:S(2)}, u32[]{:S(2)}) collective-permute-start(bf16[2,24,3200]{2,1,0:T(8,128)(2,1)S(1)} %get-tuple-element.139), channel_id=1, source_target_pairs={{0,2},{1,3},{2,0},{3,1},{4,6},{5,7},{6,4},{7,5},{8,10},{9,11},{10,... | collective-permute-start | bytes 921608 | tf_op jit(solution)/shard_map/ppermute | solution.py:641
  337.9 23.3 %collective-permute-start.46 = (bf16[4,24,3072]{2,1,0:T(8,128)(2,1)S(1)}, bf16[4,24,3072]{2,1,0:T(8,128)(2,1)S(1)}, u32[]{:S(2)}, u32[]{:S(2)}) collective-permute-start(bf16[4,24,3072]{2,1,0:T(8,128)(2,1)S(1)} %get-tuple-element.123), channel_id=1, source_target_pairs={{0,2},{1,3},{2,0},{3,1},{4,6},{5,7},{6,4},{7,5},{8,10},{9,11},{10,... | collective-permute-start | bytes 1769480 | tf_op jit(solution)/shard_map/ppermute | solution.py:641
  341.5 21.3 %collective-permute-start.48 = (bf16[4,24,3072]{2,1,0:T(8,128)(2,1)S(1)}, bf16[4,24,3072]{2,1,0:T(8,128)(2,1)S(1)}, u32[]{:S(2)}, u32[]{:S(2)}) collective-permute-start(bf16[4,24,3072]{2,1,0:T(8,128)(2,1)S(1)} %get-tuple-element.124), channel_id=1, source_target_pairs={{0,4},{1,5},{2,6},{3,7},{4,0},{5,1},{6,2},{7,3},{8,12},{9,13},{10,... | collective-permute-start | bytes 1769480 | tf_op jit(solution)/shard_map/ppermute | solution.py:641
  343.7 30.2 %collective-permute-start.54 = (bf16[4,24,3072]{2,1,0:T(8,128)(2,1)S(1)}, bf16[4,24,3072]{2,1,0:T(8,128)(2,1)S(1)}, u32[]{:S(2)}, u32[]{:S(2)}) collective-permute-start(bf16[4,24,3072]{2,1,0:T(8,128)(2,1)S(1)} %get-tuple-element.125), channel_id=1, source_target_pairs={{0,2},{1,3},{2,0},{3,1},{4,6},{5,7},{6,4},{7,5},{8,10},{9,11},{10,... | collective-permute-start | bytes 1769480 | tf_op jit(solution)/shard_map/ppermute | solution.py:641
  348.1 28.5 %collective-permute-start.56 = (bf16[4,24,3072]{2,1,0:T(8,128)(2,1)S(1)}, bf16[4,24,3072]{2,1,0:T(8,128)(2,1)S(1)}, u32[]{:S(2)}, u32[]{:S(2)}) collective-permute-start(bf16[4,24,3072]{2,1,0:T(8,128)(2,1)S(1)} %get-tuple-element.126), channel_id=1, source_target_pairs={{0,4},{1,5},{2,6},{3,7},{4,0},{5,1},{6,2},{7,3},{8,12},{9,13},{10,... | collective-permute-start | bytes 1769480 | tf_op jit(solution)/shard_map/ppermute | solution.py:641
  350.7 35.1 %collective-permute-start.38 = (bf16[4,24,3200]{2,1,0:T(8,128)(2,1)S(1)}, bf16[4,24,3200]{2,1,0:T(8,128)(2,1)S(1)}, u32[]{:S(2)}, u32[]{:S(2)}) collective-permute-start(bf16[4,24,3200]{2,1,0:T(8,128)(2,1)S(1)} %get-tuple-element.117), channel_id=1, source_target_pairs={{0,2},{1,3},{2,0},{3,1},{4,6},{5,7},{6,4},{7,5},{8,10},{9,11},{10,... | collective-permute-start | bytes 1843208 | tf_op jit(solution)/shard_map/ppermute | solution.py:641
  361.3 25.5 %collective-permute-start.40 = (bf16[4,24,3200]{2,1,0:T(8,128)(2,1)S(1)}, bf16[4,24,3200]{2,1,0:T(8,128)(2,1)S(1)}, u32[]{:S(2)}, u32[]{:S(2)}) collective-permute-start(bf16[4,24,3200]{2,1,0:T(8,128)(2,1)S(1)} %get-tuple-element.118), channel_id=1, source_target_pairs={{0,4},{1,5},{2,6},{3,7},{4,0},{5,1},{6,2},{7,3},{8,12},{9,13},{10,... | collective-permute-start | bytes 1843208 | tf_op jit(solution)/shard_map/ppermute | solution.py:641
  364.3 27.0 %collective-permute-start.49 = (bf16[24,3072]{1,0:T(8,128)(2,1)S(1)}, bf16[24,3072]{1,0:T(8,128)(2,1)S(1)}, u32[]{:S(2)}, u32[]{:S(2)}) collective-permute-start(bf16[24,3072]{1,0:T(8,128)(2,1)S(1)} %get-tuple-element.140), channel_id=1, source_target_pairs={{0,8},{1,9},{2,10},{3,11},{4,12},{5,13},{6,14},{7,15},{8,16},{9,17... | collective-permute-start | bytes 442376 | tf_op jit(solution)/shard_map/ppermute | solution.py:645
  373.9 17.5 %collective-permute-start.51 = (bf16[24,3072]{1,0:T(8,128)(2,1)S(1)}, bf16[24,3072]{1,0:T(8,128)(2,1)S(1)}, u32[]{:S(2)}, u32[]{:S(2)}) collective-permute-start(bf16[24,3072]{1,0:T(8,128)(2,1)S(1)} %get-tuple-element.141), channel_id=1, source_target_pairs={{0,24},{1,25},{2,26},{3,27},{4,28},{5,29},{6,30},{7,31},{8,0},{9,1... | collective-permute-start | bytes 442376 | tf_op jit(solution)/shard_map/ppermute | solution.py:645
  376.5 16.2 %collective-permute-start.50 = (bf16[24,3072]{1,0:T(8,128)(2,1)S(1)}, bf16[24,3072]{1,0:T(8,128)(2,1)S(1)}, u32[]{:S(2)}, u32[]{:S(2)}) collective-permute-start(bf16[24,3072]{1,0:T(8,128)(2,1)S(1)} %get-tuple-element.142), channel_id=1, source_target_pairs={{0,16},{1,17},{2,18},{3,19},{4,20},{5,21},{6,22},{7,23},{8,24},{9,... | collective-permute-start | bytes 442376 | tf_op jit(solution)/shard_map/ppermute | solution.py:645
  385.8 9.6 %collective-permute-start.57 = (bf16[24,3072]{1,0:T(8,128)(2,1)S(1)}, bf16[24,3072]{1,0:T(8,128)(2,1)S(1)}, u32[]{:S(2)}, u32[]{:S(2)}) collective-permute-start(bf16[24,3072]{1,0:T(8,128)(2,1)S(1)} %get-tuple-element.145), channel_id=1, source_target_pairs={{0,8},{1,9},{2,10},{3,11},{4,12},{5,13},{6,14},{7,15},{8,16},{9,17... | collective-permute-start | bytes 442376 | tf_op jit(solution)/shard_map/ppermute | solution.py:645
  386.7 9.8 %collective-permute-start.59 = (bf16[24,3072]{1,0:T(8,128)(2,1)S(1)}, bf16[24,3072]{1,0:T(8,128)(2,1)S(1)}, u32[]{:S(2)}, u32[]{:S(2)}) collective-permute-start(bf16[24,3072]{1,0:T(8,128)(2,1)S(1)} %get-tuple-element.146), channel_id=1, source_target_pairs={{0,24},{1,25},{2,26},{3,27},{4,28},{5,29},{6,30},{7,31},{8,0},{9,1... | collective-permute-start | bytes 442376 | tf_op jit(solution)/shard_map/ppermute | solution.py:645
  391.3 15.5 %collective-permute-start.58 = (bf16[24,3072]{1,0:T(8,128)(2,1)S(1)}, bf16[24,3072]{1,0:T(8,128)(2,1)S(1)}, u32[]{:S(2)}, u32[]{:S(2)}) collective-permute-start(bf16[24,3072]{1,0:T(8,128)(2,1)S(1)} %get-tuple-element.147), channel_id=1, source_target_pairs={{0,16},{1,17},{2,18},{3,19},{4,20},{5,21},{6,22},{7,23},{8,24},{9,... | collective-permute-start | bytes 442376 | tf_op jit(solution)/shard_map/ppermute | solution.py:645
  391.4 17.0 %collective-permute-start.41 = (bf16[24,3200]{1,0:T(8,128)(2,1)S(1)}, bf16[24,3200]{1,0:T(8,128)(2,1)S(1)}, u32[]{:S(2)}, u32[]{:S(2)}) collective-permute-start(bf16[24,3200]{1,0:T(8,128)(2,1)S(1)} %get-tuple-element.135), channel_id=1, source_target_pairs={{0,8},{1,9},{2,10},{3,11},{4,12},{5,13},{6,14},{7,15},{8,16},{9,17... | collective-permute-start | bytes 460808 | tf_op jit(solution)/shard_map/ppermute | solution.py:645
  392.8 15.6 %collective-permute-start.43 = (bf16[24,3200]{1,0:T(8,128)(2,1)S(1)}, bf16[24,3200]{1,0:T(8,128)(2,1)S(1)}, u32[]{:S(2)}, u32[]{:S(2)}) collective-permute-start(bf16[24,3200]{1,0:T(8,128)(2,1)S(1)} %get-tuple-element.136), channel_id=1, source_target_pairs={{0,24},{1,25},{2,26},{3,27},{4,28},{5,29},{6,30},{7,31},{8,0},{9,1... | collective-permute-start | bytes 460808 | tf_op jit(solution)/shard_map/ppermute | solution.py:645
  395.4 18.8 %collective-permute-start.42 = (bf16[24,3200]{1,0:T(8,128)(2,1)S(1)}, bf16[24,3200]{1,0:T(8,128)(2,1)S(1)}, u32[]{:S(2)}, u32[]{:S(2)}) collective-permute-start(bf16[24,3200]{1,0:T(8,128)(2,1)S(1)} %get-tuple-element.137), channel_id=1, source_target_pairs={{0,16},{1,17},{2,18},{3,19},{4,20},{5,21},{6,22},{7,23},{8,24},{9,... | collective-permute-start | bytes 460808 | tf_op jit(solution)/shard_map/ppermute | solution.py:645
  (29 other events, 203.6 us)

commit v2 on v1

v2 whole, which is shorter than its diff:
```python
import functools
import math

import jax
import jax.numpy as jnp
from jax import lax
from jax.experimental import pallas as pl
from jax.experimental.pallas import tpu as pltpu
from jax.sharding import PartitionSpec as P

HEADS = 12
HEAD_DIM = 64
WIDTHS = 4
BLOCK = 128
AXES = ("dp", "fsdp")
BF = jnp.bfloat16
F32 = jnp.float32
MIB = 1024 * 1024
LIMIT = 60
BYTES = 3.3e6


def matmul(left_side, right_side):
    return lax.dot_general(
        left_side, right_side, (((1,), (0,)), ((), ())), preferred_element_type=F32
    )


def matmul_last(left_side, right_side):
    return lax.dot_general(
        left_side, right_side, (((1,), (1,)), ((), ())), preferred_element_type=F32
    )


def windows(length):
    count = length // BLOCK
    spans = []
    for i in range(count):
        start = max(0, i - 1) * BLOCK
        spans.append((start, min(count, i + 2) * BLOCK - start))
    return spans


def call(kernel, limit, micros, **options):
    return pl.pallas_call(
        kernel,
        compiler_params=pltpu.CompilerParams(vmem_limit_bytes=limit * MIB),
        cost_estimate=pl.CostEstimate(flops=0, bytes_accessed=int(micros * BYTES), transcendentals=0),
        **options,
    )


def shape_of(shape, dtype):
    return jax.ShapeDtypeStruct(shape, dtype)


def whole(shape):
    return pl.BlockSpec(shape, lambda *_: (0,) * len(shape))


def attend_kernel(x, wq, wk, wv, vec, seg_col, seg_row, q_o, k_o, v_o, a_o, p_o, bias):
    spans = windows(x.shape[0])

    @pl.when(pl.program_id(0) == 0)
    def _():
        for i, (start, span) in enumerate(spans):
            same = seg_col[i * BLOCK : (i + 1) * BLOCK, :] == seg_row[:, start : start + span]
            bias[i, :, :span] = jnp.where(same, 0.0, -1e30)

    rows = x[...]
    q_o[...] = (matmul(rows, wq[...]) + vec[0:1, :]).astype(BF)
    k_o[...] = matmul(rows, wk[...]).astype(BF)
    v_o[...] = (matmul(rows, wv[...]) + vec[1:2, :]).astype(BF)
    lane = lax.broadcasted_iota(jnp.int32, (BLOCK, BLOCK), 1)
    low_half = lane < HEAD_DIM
    factor = 1.0 / math.sqrt(HEAD_DIM)
    mask = jnp.concatenate(
        [jnp.where(low_half, factor, 0.0).astype(BF), jnp.where(low_half, 0.0, factor).astype(BF)], axis=0
    )
    for pair in range(q_o.shape[1] // BLOCK):
        cols = slice(pair * BLOCK, (pair + 1) * BLOCK)
        scores = []
        for i, (start, span) in enumerate(spans):
            q_here = q_o[i * BLOCK : (i + 1) * BLOCK, cols]
            both = jnp.concatenate([q_here, q_here], axis=0) * mask
            scores.append(matmul_last(both, k_o[start : start + span, cols]))
        chances = []
        for i, (start, span) in enumerate(spans):
            blocked = bias[i, :, :span]
            score = scores[i] + jnp.concatenate([blocked, blocked], axis=0)
            shifted = jnp.exp(score - jnp.max(score, axis=1, keepdims=True))
            total = jnp.sum(shifted, axis=1, keepdims=True)
            chances.append((shifted * (1.0 / total)).astype(BF))
        for i, (start, span) in enumerate(spans):
            mixed = matmul(chances[i], v_o[start : start + span, cols])
            here = slice(i * BLOCK, (i + 1) * BLOCK)
            a_o[here, cols] = jnp.where(low_half, mixed[:BLOCK], mixed[BLOCK:]).astype(BF)
            p_o[2 * pair, i, :, :span] = chances[i][:BLOCK]
            p_o[2 * pair + 1, i, :, :span] = chances[i][BLOCK:]


def attend(x, query_key, value_output, vec, segments):
    length, width = x.shape
    step = 256
    steps = width // step
    count = length // BLOCK
    part = pl.BlockSpec((length, step), lambda p: (0, p))
    heads = step // HEAD_DIM

    def weight(n):
        return pl.BlockSpec((width, step), lambda p: (0, n * steps + p))

    return call(
        attend_kernel,
        LIMIT,
        9.5,
        grid=(steps,),
        in_specs=[
            whole(x.shape),
            weight(0),
            weight(1),
            weight(0),
            pl.BlockSpec((vec.shape[0], step), lambda p: (0, p)),
            whole((length, 1)),
            whole((1, length)),
        ],
        out_specs=[part, part, part, part, pl.BlockSpec((heads, count, BLOCK, 3 * BLOCK), lambda p: (p, 0, 0, 0))],
        out_shape=[shape_of((length, width), BF)] * 4 + [shape_of((HEADS, count, BLOCK, 3 * BLOCK), BF)],
        scratch_shapes=[pltpu.VMEM((count, BLOCK, 3 * BLOCK), F32)],
        name="attend",
    )(x, query_key, query_key, value_output, vec, segments.reshape(length, 1), segments.reshape(1, length))


def norm_parts(values):
    center = values - jnp.mean(values, axis=1, keepdims=True)
    scale = lax.rsqrt(jnp.mean(center * center, axis=1, keepdims=True) + 1e-12)
    return center * scale, scale


def norm_back(spread_grad, hat, scale):
    return scale * (
        spread_grad
        - jnp.mean(spread_grad, axis=1, keepdims=True)
        - hat * jnp.mean(spread_grad * hat, axis=1, keepdims=True)
    )


def chunk_mask(w, rows):
    lane = lax.broadcasted_iota(jnp.int32, (rows, 2 * BLOCK), 1)
    start = HEAD_DIM * (w % 2)
    return (lane >= start) & (lane < start + 3 * HEAD_DIM)


def window_at(w):
    return w + w // 2


def first_kernel(x, att_a, att_b, wo_a, wo_b, vec, hat_o, scale_o, normed_o, normed_t_o, second_o, x_t_o, branch):
    w = pl.program_id(0)

    @pl.when(w == 0)
    def _():
        branch[...] = x[...].astype(F32) + vec[2:3, :]
        x_t_o[...] = x[...].T

    kept = jnp.where(chunk_mask(w, x.shape[0]), jnp.concatenate([att_a[...], att_b[...]], axis=1).astype(F32), 0.0)
    weight = jnp.concatenate([wo_a[...], wo_b[...]], axis=1)
    first = branch[...] + matmul_last(kept.astype(BF), weight)
    branch[...] = first
    hat, scale = norm_parts(first)
    hat_o[0] = hat.astype(BF)
    scale_o[0] = scale
    normed = hat * vec[3:4, :] + vec[4:5, :]
    second_o[0] = normed + vec[5:6, :]
    low = normed.astype(BF)
    normed_o[0] = low
    normed_t_o[0] = low.T


def first_norm(x, att, weights, vec):
    length, width = x.shape
    base = width // BLOCK
    per_width = pl.BlockSpec((1, length, width), lambda w: (w, 0, 0))
    return call(
        first_kernel,
        LIMIT,
        9.7,
        grid=(WIDTHS,),
        in_specs=[
            whole(x.shape),
            pl.BlockSpec((length, BLOCK), lambda w: (0, window_at(w))),
            pl.BlockSpec((length, BLOCK), lambda w: (0, window_at(w) + 1)),
            pl.BlockSpec((width, BLOCK), lambda w: (0, base + window_at(w))),
            pl.BlockSpec((width, BLOCK), lambda w: (0, base + window_at(w) + 1)),
            whole(vec.shape),
        ],
        out_specs=[
            per_width,
            pl.BlockSpec((1, length, 1), lambda w: (w, 0, 0)),
            per_width,
            pl.BlockSpec((1, width, length), lambda w: (w, 0, 0)),
            per_width,
            whole((width, length)),
        ],
        out_shape=[
            shape_of((WIDTHS, length, width), BF),
            shape_of((WIDTHS, length, 1), F32),
            shape_of((WIDTHS, length, width), BF),
            shape_of((WIDTHS, width, length), BF),
            shape_of((WIDTHS, length, width), F32),
            shape_of((width, length), BF),
        ],
        scratch_shapes=[pltpu.VMEM((length, width), F32)],
        name="first_norm",
    )(x, att, att, weights, weights, vec)


ERF_T = 0.3275911 / math.sqrt(2.0)
BELL = 1.0 / math.sqrt(2.0 * math.pi)
ERF_A = tuple(
    0.5 * entry / BELL for entry in (0.254829592, -0.284496736, 1.421413741, -1.453152027, 1.061405429)
)
ROWS = 256


def gelu_pair(values):
    size = jnp.abs(values)
    bell = jnp.exp2(values * values * (-0.5 * math.log2(math.e)) + math.log2(BELL))
    below = 1.0 + ERF_T * size
    t = pl.reciprocal(below, approx=True)
    t = t * (2.0 - below * t)
    poly = ERF_A[4] * t + ERF_A[3]
    for entry in (ERF_A[2], ERF_A[1], ERF_A[0]):
        poly = poly * t + entry
    tail = poly * t * bell
    step = tail - size * bell
    return jnp.maximum(values, 0.0) - size * tail, jnp.where(values >= 0.0, 1.0 - step, step)


def feed_order(chunks):
    return [(j, w) for j in chunks for w in range(j, WIDTHS)]


def copy_of(source, target, sem):
    return pltpu.make_async_copy(source, target, sem)


def forward_step(normed, weights, bias, act, slope, second, column):
    length, width = normed.shape
    half = weights.shape[1] // 2
    for r in range(0, length, ROWS):
        rows = slice(r, r + ROWS)
        inner = matmul(normed[rows, :], weights[:, column : column + width]) + bias
        active, tilt = gelu_pair(inner)
        active = active.astype(BF)
        act[rows, :] = active
        slope[rows, :] = tilt.astype(BF)
        second[rows, :] += matmul_last(active, weights[:, half + column : half + column + width])


def second_norm(second, og, vec, out, feed, feed_t, sums):
    hat, scale = norm_parts(second[...])
    out[...] = (hat * vec[6:7, :] + vec[7:8, :]).astype(BF)
    grad = og[...].astype(F32)
    sums[0:1, :] += jnp.sum(grad * hat, axis=0, keepdims=True)
    sums[1:2, :] += jnp.sum(grad, axis=0, keepdims=True)
    low = norm_back(grad * vec[6:7, :], hat, scale).astype(BF)
    feed[...] = low
    feed_t[...] = low.T
    sums[2:3, :] += jnp.sum(low.astype(F32), axis=0, keepdims=True)


def backward_step(feed, feed_t, normed_t, act, slope, weights, column, outer, inner, grads, bias, ready=None):
    length, width = feed.shape
    half = weights.shape[1] // 2
    outer[...] += matmul(feed_t[...], act[...])
    if ready is not None:
        ready()
    lows = []
    for r in range(0, length, ROWS):
        rows = slice(r, r + ROWS)
        raw = matmul(feed[rows, :], weights[:, half + column : half + column + width])
        low = (slope[rows, :].astype(F32) * raw).astype(BF)
        bias[...] += jnp.sum(low.astype(F32), axis=0, keepdims=True)
        grads[rows, :] += matmul_last(low, weights[:, column : column + width])
        lows.append(low)
    inner[...] += matmul(normed_t[...], jnp.concatenate(lows, axis=0))


ANY = pl.BlockSpec(memory_space=pl.ANY)
SCALARS = pl.BlockSpec(memory_space=pltpu.SMEM)


def held(array):
    return pl.BlockSpec(memory_space=pltpu.VMEM)


def give_halves(core, outer, inner, mine_h, other_h, sem):
    @pl.when(core == 0)
    def _():
        copy_of(outer, mine_h, sem).start()
        copy_of(inner, other_h, sem).start()

    @pl.when(core != 0)
    def _():
        copy_of(inner, mine_h, sem).start()
        copy_of(outer, other_h, sem).start()

    return [copy_of(outer, mine_h, sem), copy_of(inner, other_h, sem)]


def slot_of(j, w):
    return w if j == 0 else feed_order((1, 2, 3)).index((j, j)) + w - j


def feed_all_kernel(source, table, bi, vec, normed_h, second_h, og_h, normed_t_h, *refs):
    count = len(source.arrays)
    pieces, refs = refs[:count], refs[count:]
    act_h, slope_h, out_h, feed_h, feed_t_h, mine_h, other_h, mine_lo_h, other_lo_h, grad_h, bias, sums = refs[:12]
    weights, normed, second, og, normed_t, act, slope, feed, feed_t, outer, inner, outer_b, inner_b = refs[12:25]
    sem_w, sem_n, sem_s, sem_og, sem_t, sem_act, sem_out, sem_give = refs[25:]
    width = normed.shape[2]
    og_reads = [copy_of(og_h.at[j], og.at[j % 2], sem_og.at[j]) for j in range(WIDTHS)]

    def start_rows(w):
        copy_of(normed_h.at[w], normed.at[w], sem_n.at[w]).start()
        copy_of(second_h.at[w], second.at[w], sem_s.at[w]).start()

    start_rows(0)
    source.start(table, pieces, weights, sem_w.at[0], 0, width, 0)
    for w in range(1, WIDTHS):
        start_rows(w)
    og_reads[0].start()
    og_reads[1].start()
    for j in range(1, WIDTHS):
        source.start(table, pieces, weights, sem_w.at[j], j * width, width, j * width)
    for w in range(1, WIDTHS):
        copy_of(normed_t_h.at[w], normed_t.at[w - 1], sem_t.at[w - 1]).start()
    sums[...] = jnp.zeros_like(sums)
    bias[...] = jnp.zeros_like(bias)
    writes = []
    for j in range(WIDTHS):
        source.wait(weights, sem_w.at[j], width, j * width)

        def body(w, carry, j=j):
            if j == 0:
                copy_of(normed_h.at[w], normed.at[w], sem_n.at[w]).wait()
                copy_of(second_h.at[w], second.at[w], sem_s.at[w]).wait()
            at = slot_of(j, 0) + w
            forward_step(normed.at[w], weights, bi[j], act.at[at], slope.at[at], second.at[w], j * width)
            if j == 0:
                copy_of(act.at[at], act_h.at[w], sem_act.at[w]).start()
                copy_of(slope.at[at], slope_h.at[w], sem_act.at[w]).start()
            return carry

        lax.fori_loop(j, WIDTHS, body, 0)
        og_reads[j].wait()
        second_norm(second.at[j], og.at[j % 2], vec, normed.at[j], feed.at[j], feed_t.at[j], sums)
        if j + 2 < WIDTHS:
            og_reads[j + 2].start()
        for copy in (
            copy_of(normed.at[j], out_h.at[j], sem_out.at[0, j]),
            copy_of(feed.at[j], feed_h.at[j], sem_out.at[1, j]),
            copy_of(feed_t.at[j], feed_t_h.at[j], sem_out.at[2, j]),
        ):
            copy.start()
            writes.append(copy)
        if j == 0:
            for w in range(WIDTHS):
                copy_of(act.at[w], act_h.at[w], sem_act.at[w]).wait()
                copy_of(slope.at[w], slope_h.at[w], sem_act.at[w]).wait()
    for w in range(1, WIDTHS):
        copy_of(normed_t_h.at[w], normed_t.at[w - 1], sem_t.at[w - 1]).wait()
        second[w] = feed[w].astype(F32)
    given = {}
    for j in (3, 2, 1):
        outer[...] = jnp.zeros_like(outer)
        inner[...] = jnp.zeros_like(inner)

        def back(w, carry, j=j):
            at = slot_of(j, 0) + w
            backward_step(
                feed.at[w], feed_t.at[w], normed_t.at[w - 1], act.at[at], slope.at[at], weights, j * width,
                outer, inner, second.at[w], bias.at[j - 1],
            )
            if j == 1:
                copy_of(second.at[w], grad_h.at[w - 1], sem_out.at[3, w]).start()
            return carry

        lax.fori_loop(j, WIDTHS, back, 0)
        slot = j % 2
        if slot in given:
            for copy in given[slot]:
                copy.wait()
        outer_b[slot] = outer[...].astype(BF)
        inner_b[slot] = inner[...].astype(BF)
        columns = pl.ds(j % 2 * width, width)
        targets = (mine_h, other_h) if j > 1 else (mine_lo_h, other_lo_h)
        given[slot] = give_halves(
            table[source.core], outer_b.at[slot], inner_b.at[slot], targets[0].at[:, columns], targets[1].at[:, columns],
            sem_give.at[slot],
        )
    for copies in given.values():
        writes += copies
    for w in range(1, WIDTHS):
        writes.append(copy_of(second.at[w], grad_h.at[w - 1], sem_out.at[3, w]))
    for copy in writes:
        copy.wait()


def feed_all(source, normed, bi, second, og, vec, normed_t):
    _, length, width = normed.shape
    four, four_t = (WIDTHS, length, width), (WIDTHS, width, length)
    many = WIDTHS - 1
    slots = len(feed_order((1, 2, 3)))
    return call(
        functools.partial(feed_all_kernel, source),
        LIMIT,
        58,
        in_specs=[SCALARS, held(bi), held(vec)] + [ANY] * (4 + len(source.arrays)),
        out_specs=[ANY] * 10 + [held(vec), held(vec)],
        out_shape=[
            shape_of(four, BF),
            shape_of(four, BF),
            shape_of(four, BF),
            shape_of(four, BF),
            shape_of(four_t, BF),
            shape_of((width, 2 * width), BF),
            shape_of((width, 2 * width), BF),
            shape_of((width, 2 * width), BF),
            shape_of((width, 2 * width), BF),
            shape_of((many, length, width), F32),
            shape_of((many, 1, width), F32),
            shape_of((8, width), F32),
        ],
        scratch_shapes=[
            pltpu.VMEM((width, 8 * width), BF),
            pltpu.VMEM(four, BF),
            pltpu.VMEM(four, F32),
            pltpu.VMEM((2, length, width), BF),
            pltpu.VMEM((many, width, length), BF),
            pltpu.VMEM((slots, length, width), BF),
            pltpu.VMEM((slots, length, width), BF),
            pltpu.VMEM(four, BF),
            pltpu.VMEM(four_t, BF),
            pltpu.VMEM((width, width), F32),
            pltpu.VMEM((width, width), F32),
            pltpu.VMEM((2, width, width), BF),
            pltpu.VMEM((2, width, width), BF),
            pltpu.SemaphoreType.DMA((WIDTHS, 2)),
            pltpu.SemaphoreType.DMA((WIDTHS,)),
            pltpu.SemaphoreType.DMA((WIDTHS,)),
            pltpu.SemaphoreType.DMA((WIDTHS,)),
            pltpu.SemaphoreType.DMA((many,)),
            pltpu.SemaphoreType.DMA((WIDTHS,)),
            pltpu.SemaphoreType.DMA((4, WIDTHS)),
            pltpu.SemaphoreType.DMA((2,)),
        ],
        name="feed_all",
    )(source.table, bi, vec, normed, second, og, normed_t, *source.arrays)


def feed_zero_kernel(source, table, vec, feed_h, feed_t_h, normed_t_h, act_h, slope_h, grad_in, hat_h, scale_h, att_h, wo_h, *refs):
    count = len(source.arrays)
    pieces, refs = refs[:count], refs[count + 2 :]
    mine_h, other_h, first_g_h, att_g_h, wo_g_h, bias, sums = refs[:7]
    weights, feed, feed_t, normed_t, act, slope, outer, inner, grads, outer_b, inner_b = refs[7:18]
    hat, scale, att, wo, att_g, total, wo_g, wo_g_b = refs[18:26]
    sem_w, sem_in, sem_g, sem_x, sem_out = refs[26:]
    length, width = feed.shape[1:]
    def reads(w):
        return (
            copy_of(feed_t_h.at[w], feed_t.at[w], sem_in.at[0, w]),
            copy_of(act_h.at[w], act.at[w], sem_in.at[1, w]),
            copy_of(feed_h.at[w], feed.at[w], sem_in.at[2, w]),
            copy_of(slope_h.at[w], slope.at[w], sem_in.at[3, w]),
            copy_of(normed_t_h.at[w], normed_t.at[w], sem_in.at[4, w]),
            copy_of(hat_h.at[w], hat.at[w], sem_in.at[5, w]),
            copy_of(scale_h.at[w], scale.at[w], sem_in.at[6, w]),
        )

    for w in reversed(range(WIDTHS)):
        for copy in reads(w)[:5]:
            copy.start()
        if w == WIDTHS - 1:
            source.start(table, pieces, weights, sem_w, 0, width, 0)
        if w > 0:
            copy_of(grad_in.at[w - 1], grads.at[w], sem_g.at[w]).start()
        if w == WIDTHS - 1:
            beside = (copy_of(att_h, att, sem_x.at[0]), copy_of(wo_h.at[:, pl.ds(width, width)], wo, sem_x.at[1]))
            for copy in beside:
                copy.start()
        for copy in reads(w)[5:]:
            copy.start()
    outer[...] = jnp.zeros_like(outer)
    inner[...] = jnp.zeros_like(inner)
    bias[...] = jnp.zeros_like(bias)
    sums[...] = jnp.zeros_like(sums)
    total[...] = jnp.zeros_like(total)
    wo_g[...] = jnp.zeros_like(wo_g)

    def body(step, carry):
        w = WIDTHS - 1 - step
        for copy in reads(w)[:2]:
            copy.wait()

        def ready():
            for copy in reads(w)[2:]:
                copy.wait()

            @pl.when(step == 0)
            def _():
                source.wait(weights, sem_w, width, 0)
                for copy in beside:
                    copy.wait()

            @pl.when(w == 0)
            def _():
                grads[0] = feed[0].astype(F32)

            @pl.when(w > 0)
            def _():
                copy_of(grad_in.at[0], grads.at[w], sem_g.at[w]).wait()

        backward_step(
            feed.at[w], feed_t.at[w], normed_t.at[w], act.at[w], slope.at[w], weights, 0, outer, inner, grads.at[w],
            bias.at[0], ready,
        )
        rough, factor = hat[w].astype(F32), scale[w]
        grad = grads[w]
        sums[0:1, :] += jnp.sum(grad * rough, axis=0, keepdims=True)
        sums[1:2, :] += jnp.sum(grad, axis=0, keepdims=True)
        first_g = norm_back(grad * vec[3:4, :], rough, factor)
        grads[w] = first_g
        copy_of(grads.at[w], first_g_h.at[w], sem_out.at[0]).start()
        low = first_g.astype(BF)
        wide = low.astype(F32)
        sums[2:3, :] += jnp.sum(wide, axis=0, keepdims=True)
        total[...] += wide
        lane = lax.broadcasted_iota(jnp.int32, (length, width), 1)
        kept = lane < (w + 1) * (3 * HEAD_DIM)
        att_g[w] = jnp.where(kept, matmul(low, wo[...]), 0.0).astype(BF)
        copy_of(att_g.at[w], att_g_h.at[w], sem_out.at[1]).start()
        columns = pl.ds(pl.multiple_of(BLOCK * window_at(w), BLOCK), 2 * BLOCK)
        part = jnp.where(chunk_mask(w, length), att[:, columns].astype(F32), 0.0).astype(BF)
        wo_g[:, columns] += matmul(total[...].astype(BF).T, part)
        return carry

    lax.fori_loop(0, WIDTHS, body, 0)
    outer_b[...] = outer[...].astype(BF)
    inner_b[...] = inner[...].astype(BF)
    writes = give_halves(
        table[source.core], outer_b, inner_b, mine_h.at[:, pl.ds(0, width)], other_h.at[:, pl.ds(0, width)], sem_out.at[2]
    )
    wo_g_b[...] = wo_g[...].astype(BF)
    copy = copy_of(wo_g_b, wo_g_h, sem_out.at[2])
    copy.start()
    for copy in writes + [copy, copy_of(grads, first_g_h, sem_out.at[0]), copy_of(att_g, att_g_h, sem_out.at[1])]:
        copy.wait()


def feed_zero(source, vec, feed, feed_t, normed_t, act, slope, grad, hat, scale, att, wo, mine, other):
    _, length, width = feed.shape
    four, four_t = (WIDTHS, length, width), (WIDTHS, width, length)
    first = 12 + len(source.arrays)
    return call(
        functools.partial(feed_zero_kernel, source),
        LIMIT,
        28,
        in_specs=[SCALARS, held(vec)] + [ANY] * (10 + len(source.arrays) + 2),
        out_specs=[ANY] * 5 + [held(vec), held(vec)],
        out_shape=[
            shape_of(mine.shape, BF),
            shape_of(other.shape, BF),
            shape_of(four, F32),
            shape_of(four, BF),
            shape_of((width, width), BF),
            shape_of((1, 1, width), F32),
            shape_of((8, width), F32),
        ],
        scratch_shapes=[
            pltpu.VMEM((width, 2 * width), BF),
            pltpu.VMEM(four, BF),
            pltpu.VMEM(four_t, BF),
            pltpu.VMEM(four_t, BF),
            pltpu.VMEM(four, BF),
            pltpu.VMEM(four, BF),
            pltpu.VMEM((width, width), F32),
            pltpu.VMEM((width, width), F32),
            pltpu.VMEM(four, F32),
            pltpu.VMEM((width, width), BF),
            pltpu.VMEM((width, width), BF),
            pltpu.VMEM(four, BF),
            pltpu.VMEM((WIDTHS, length, 1), F32),
            pltpu.VMEM((length, width), BF),
            pltpu.VMEM((width, width), BF),
            pltpu.VMEM(four, BF),
            pltpu.VMEM((length, width), F32),
            pltpu.VMEM((width, width), F32),
            pltpu.VMEM((width, width), BF),
            pltpu.SemaphoreType.DMA((2,)),
            pltpu.SemaphoreType.DMA((7, WIDTHS)),
            pltpu.SemaphoreType.DMA((WIDTHS,)),
            pltpu.SemaphoreType.DMA((2,)),
            pltpu.SemaphoreType.DMA((3,)),
        ],
        input_output_aliases={first: 0, first + 1: 1},
        name="feed_zero",
    )(source.table, vec, feed, feed_t, normed_t, act, slope, grad, hat, scale, att, wo, *source.arrays, mine, other)


def attend_back_kernel(first_pair, pairs, q, k, v, p, g, dq_o, dk_o, dv_o, all_o, sums_o, dk_t, dv_t):
    pair = first_pair + pl.program_id(0)
    length = q.shape[0]
    spans = windows(length)
    factor = 1.0 / math.sqrt(HEAD_DIM)
    lane = lax.broadcasted_iota(jnp.int32, (BLOCK, BLOCK), 1)
    low_half = lane < HEAD_DIM
    masks = (
        jnp.where(low_half, 1.0, 0.0).astype(BF),
        jnp.where(low_half, 0.0, 1.0).astype(BF),
    )

    def run(first):
        widths = list(range(first, WIDTHS))
        many = len(widths)
        dk_t[...] = jnp.zeros_like(dk_t)
        dv_t[...] = jnp.zeros_like(dv_t)
        q_t = (q[...] * jnp.asarray(factor, BF)).T
        g_t = [g[w].T for w in widths]
        mask = jnp.concatenate([masks[0]] * many + [masks[1]] * many, axis=0)
        wide = jnp.concatenate([low_half] * many, axis=0)
        chance_g = []
        for i, (start, span) in enumerate(spans):
            g_here = jnp.concatenate([g[w, i * BLOCK : (i + 1) * BLOCK, :] for w in widths], axis=0)
            chance_g.append(matmul_last(jnp.concatenate([g_here, g_here], axis=0) * mask, v[start : start + span, :]))
        scores_g = []
        for i, (start, span) in enumerate(spans):
            lows = []
            for half in range(2):
                chances = p[half, i, :, :span].astype(F32)
                for n in range(many):
                    at = (half * many + n) * BLOCK
                    product = chances * chance_g[i][at : at + BLOCK, :]
                    row = jnp.sum(product, axis=1, keepdims=True)
                    lows.append((product - chances * row).astype(BF))
            scores_g.append(lows)
        for i, (start, span) in enumerate(spans):
            here = slice(i * BLOCK, (i + 1) * BLOCK)
            near = slice(start, start + span)
            lows = scores_g[i]
            found = matmul(jnp.concatenate(lows, axis=0), k[near, :] * jnp.asarray(factor, BF))
            dq = jnp.where(wide, found[: many * BLOCK], found[many * BLOCK :]).astype(BF)
            for n, w in enumerate(widths):
                dq_o[w, here, :] = dq[n * BLOCK : (n + 1) * BLOCK, :]
            for half in range(2):
                rows_of = slice(half * HEAD_DIM, (half + 1) * HEAD_DIM)
                for n, w in enumerate(widths):
                    dk_t[w, rows_of, near] += matmul(q_t[rows_of, here], lows[half * many + n])
                stacked = jnp.concatenate([g_t[n][rows_of, here] for n in range(many)], axis=0)
                values_g = matmul(stacked, p[half, i, :, :span])
                for n, w in enumerate(widths):
                    dv_t[w, rows_of, near] += values_g[n * HEAD_DIM : (n + 1) * HEAD_DIM, :]
        totals = [jnp.zeros((length, BLOCK), F32) for _ in range(3)]
        for w in range(WIDTHS):
            if w < first:
                for ref in (dq_o, dk_o, dv_o):
                    ref[w] = jnp.zeros((length, BLOCK), BF)
                continue
            dk_o[w] = dk_t[w].astype(BF).T
            dv_o[w] = dv_t[w].astype(BF).T
            for n, ref in enumerate((dq_o, dk_o, dv_o)):
                totals[n] += ref[w].astype(F32)
        for n in range(3):
            all_o[n] = totals[n].astype(BF)
        sums_o[0:1, :] = jnp.sum(totals[0], axis=0, keepdims=True)
        sums_o[1:2, :] = jnp.sum(totals[2], axis=0, keepdims=True)

    heads_each = HEADS // WIDTHS
    firsts = [(2 * n) // heads_each for n in range(HEADS // 2)]
    for first in sorted(set(firsts)):
        members = [n for n, f in enumerate(firsts) if f == first and first_pair <= n < first_pair + pairs]
        if not members:
            continue

        @pl.when((pair >= members[0]) & (pair <= members[-1]))
        def _(first=first):
            run(first)


def attend_backward(first_pair, pairs, q, k, v, p, g):
    length = q.shape[0]
    columns = pairs * BLOCK
    part = pl.BlockSpec((length, BLOCK), lambda n: (0, first_pair + n))
    wide = pl.BlockSpec((WIDTHS, length, BLOCK), lambda n: (0, 0, first_pair + n))
    wide_o = pl.BlockSpec((WIDTHS, length, BLOCK), lambda n: (0, 0, n))
    return call(
        functools.partial(attend_back_kernel, first_pair, pairs),
        LIMIT,
        10,
        grid=(pairs,),
        in_specs=[part, part, part, pl.BlockSpec((2,) + p.shape[1:], lambda n: (first_pair + n, 0, 0, 0)), wide],
        out_specs=[wide_o] * 3
        + [pl.BlockSpec((3, length, BLOCK), lambda n: (0, 0, n)), pl.BlockSpec((8, BLOCK), lambda n: (0, n))],
        out_shape=[shape_of((WIDTHS, length, columns), BF)] * 3
        + [shape_of((3, length, columns), BF), shape_of((8, columns), F32)],
        scratch_shapes=[pltpu.VMEM((WIDTHS, BLOCK, length), F32)] * 2,
        name="attend_backward",
    )(q, k, v, p, g)


def project_kernel(core, x_t, grads, wo_g, last, mine_o, other_o):
    rows = x_t[...]
    columns = grads.shape[2]

    def fill(first, second):
        first[:, :columns] = matmul(rows, grads[0]).astype(BF)
        first[:, columns : 2 * columns] = matmul(rows, grads[1]).astype(BF)
        second[:, :columns] = matmul(rows, grads[2]).astype(BF)
        second[:, columns : 2 * columns] = wo_g[...]
        if last is not None:
            first[:, 2 * columns :] = last[...]
            second[:, 2 * columns :] = last[...]

    @pl.when(core[0] == 0)
    def _():
        fill(mine_o, other_o)

    @pl.when(core[0] != 0)
    def _():
        fill(other_o, mine_o)


def project_grads(core, x_t, grads, wo_g, part, last):
    width, length = x_t.shape
    columns = grads.shape[2]
    out = (width, 2 * columns + (0 if last is None else last.shape[1]))
    given = [] if last is None else [last]
    kernel = project_kernel
    if last is None:
        kernel = lambda core, x_t, grads, wo_g, *outs: project_kernel(core, x_t, grads, wo_g, None, *outs)
    return call(
        kernel,
        LIMIT,
        4.5,
        grid=(1,),
        in_specs=[
            pl.BlockSpec(memory_space=pltpu.SMEM),
            whole(x_t.shape),
            whole(grads.shape),
            pl.BlockSpec((width, columns), lambda n: (0, part)),
        ]
        + [whole(entry.shape) for entry in given],
        out_specs=[whole(out)] * 2,
        out_shape=[shape_of(out, BF)] * 2,
        name="project_grads",
    )(jnp.full((1,), core, jnp.int32), x_t, grads, wo_g, *given)


def input_kernel(some, first_g, dq_a, dk_a, dv_a, dq_b, dk_b, dv_b, wq, wk, wv, *refs):
    out = refs[-1]
    w = pl.program_id(0)
    split = dq_a.shape[2]
    for section in some:
        kept = -(-(section + 1) * 3 * HEAD_DIM // BLOCK) * BLOCK

        @pl.when(w == section - some[0])
        def _():
            total = first_g[0]
            for low, high, weight in ((dq_a, dq_b, wq), (dk_a, dk_b, wk), (dv_a, dv_b, wv)):
                near = min(kept, split)
                total += matmul_last(low[0, :, :near], weight[:, :near])
                if kept > split:
                    total += matmul_last(high[0, :, : kept - split], weight[:, split:kept])
            out[0] = total


def input_grads(some, first_g, low, high, query_key, value_output, earlier):
    _, length, width = first_g.shape
    base = some[0]
    per_width = pl.BlockSpec((1, length, width), lambda w: (w + base, 0, 0))
    part = pl.BlockSpec((1, length, low[0].shape[2]), lambda w: (w + base, 0, 0))
    last = pl.BlockSpec((1, length, high[0].shape[2]), lambda w: (jnp.maximum(w + base, WIDTHS // 2), 0, 0))
    given = [] if earlier is None else [earlier]

    def weight(n):
        return pl.BlockSpec((width, width), lambda w: (0, n))

    return call(
        functools.partial(input_kernel, some),
        LIMIT,
        8,
        grid=(len(some),),
        in_specs=[per_width] + [part] * 3 + [last] * 3 + [weight(0), weight(1), weight(0)] + [ANY] * len(given),
        out_specs=per_width,
        out_shape=shape_of(first_g.shape, F32),
        input_output_aliases={10: 0} if given else {},
        name="input_grads",
    )(first_g, *low, *high, query_key, query_key, value_output, *given)


def tie(*values):
    return lax.optimization_barrier(values)


class Ring:
    def __init__(self, mesh):
        self.dp = mesh.shape["dp"]
        self.fsdp = mesh.shape["fsdp"]
        self.square = self.fsdp == 8 and self.dp % 2 == 0
        index = lax.axis_index("fsdp")
        self.z = lax.axis_index("dp")
        self.y, self.x, self.c = index // 4, (index // 2) % 2, index % 2

    def swap(self, value, bit):
        total = self.dp * self.fsdp
        return lax.ppermute(value, AXES, [(i, i ^ bit) for i in range(total)])

    def shift(self, value, by):
        total = self.dp * self.fsdp
        return lax.ppermute(value, AXES, [(i, (i + by * self.fsdp) % total) for i in range(total)])

    def mine(self, first, second):
        return jnp.where(self.c == 0, first, second)


CORE, X_SIDE, Y_SIDE = 1, 2, 4


class Gather:
    def __init__(self, ring, halves):
        self.ring, self.halves = ring, halves
        self.shard = halves
        self.line = self.came = self.sides = self.corners = self.crossed = ()

    def start_core(self):
        ring = self.ring
        if ring.square:
            kept, sent = ring.mine(*self.halves), ring.mine(*self.halves[::-1])
            came = ring.swap(sent, CORE)
            self.shard = ring.mine(jnp.concatenate([kept, came], axis=0), jnp.concatenate([came, kept], axis=0))

    def start_line(self):
        ring = self.ring
        if ring.square:
            self.came = tuple(ring.shift(self.shard, by) for by in range(1, ring.dp))

    def ready_line(self):
        if self.ring.square:
            self.line = jnp.stack((self.shard,) + self.came)

    def start_sides(self):
        ring = self.ring
        if ring.square:
            self.sides = (ring.swap(self.line, X_SIDE), ring.swap(self.line, Y_SIDE))

    def start_corners(self):
        ring, half = self.ring, self.ring.dp // 2
        if ring.square:
            self.corners = (
                ring.swap(self.sides[0][:half], Y_SIDE),
                ring.swap(self.sides[1][half:], X_SIDE),
            )

    def cross(self, *values):
        if self.ring.square:
            self.crossed += tuple(self.ring.swap(value, CORE) for value in values)

    def pieces(self):
        ring, half = self.ring, self.ring.dp // 2
        own = (
            (self.line, 0, ring.y, ring.x),
            (self.sides[0], 0, ring.y, 1 - ring.x),
            (self.sides[1], 0, 1 - ring.y, ring.x),
            (self.corners[0], 0, 1 - ring.y, 1 - ring.x),
            (self.corners[1], half, 1 - ring.y, 1 - ring.x),
        )
        rows = self.shard.shape[0]
        copies, at = [], []
        for n, (value, behind, y, x) in enumerate(own):
            for index in range(value.shape[0]):
                z = (ring.z + ring.dp - behind - index) % ring.dp
                copies.append((n, index))
                at.append(jnp.asarray(rows * ((z * 2 + y) * 2 + x), jnp.int32))
        arrays = [value for value, *_ in own] + list(self.crossed)
        return arrays, copies, jnp.stack(at + [jnp.asarray(ring.c, jnp.int32)])

    def source(self):
        return Source(self)


class Source:
    def __init__(self, gather):
        ring = gather.ring
        self.square = ring.square
        self.columns = gather.halves[0].shape[1]
        if ring.square:
            self.rows = gather.shard.shape[0]
            self.arrays, self.copies, self.table = gather.pieces()
        else:
            self.rows = gather.halves[0].shape[0] * ring.dp * ring.fsdp
            self.arrays = [lax.all_gather(half, AXES, axis=0, tiled=True) for half in gather.halves]
            self.copies = []
            self.table = jnp.asarray(ring.c, jnp.int32).reshape(1)
        self.core = len(self.copies)

    def start(self, table, pieces, target, sems, first, columns, to):
        apart = target.shape[1] // 2
        if not self.square:
            for half in range(2):
                pltpu.make_async_copy(
                    pieces[half].at[:, pl.ds(first, columns)],
                    target.at[:, pl.ds(half * apart + to, columns)],
                    sems.at[half],
                ).start()
            return
        core = table[self.core]
        many = len(pieces) // 2
        for side in range(2):
            half = core if side == 0 else 1 - core
            for n, (piece, index) in enumerate(self.copies):
                row = pl.multiple_of(table[n], 16)
                pltpu.make_async_copy(
                    pieces[side * many + piece].at[index, :, pl.ds(first, columns)],
                    target.at[pl.ds(row, self.rows), pl.ds(pl.multiple_of(half * apart + to, BLOCK), columns)],
                    sems.at[half],
                ).start()

    def wait(self, target, sems, columns, to):
        for half in range(2):
            whole_half = target.at[:, pl.ds(half * (target.shape[1] // 2) + to, columns)]
            pltpu.make_async_copy(whole_half, whole_half, sems.at[half]).wait()


def place_rows(source, layout):
    def kernel(table, *refs):
        count = len(source.arrays)
        pieces, outs, sem = refs[:count], refs[count:-1], refs[-1]
        if not source.square:
            copies = [
                pltpu.make_async_copy(pieces[half].at[:, pl.ds(first, columns)], outs[n], sem)
                for n, (half, first, columns) in enumerate(layout)
            ]
            for copy in copies:
                copy.start()
            for copy in copies:
                copy.wait()
            return
        many = count // 2
        core = table[source.core]

        def run(own):
            copies = []
            for n, (half, first, columns) in enumerate(layout):
                for m, (piece, index) in enumerate(source.copies):
                    row = pl.multiple_of(table[m], 16)
                    copies.append(
                        pltpu.make_async_copy(
                            pieces[piece + (0 if half == own else many)].at[index, :, pl.ds(first, columns)],
                            outs[n].at[pl.ds(row, source.rows), :],
                            sem,
                        )
                    )
            for copy in copies:
                copy.start()
            for copy in copies:
                copy.wait()

        for own in range(2):
            pl.when(core == own)(functools.partial(run, own))

    rows = source.rows * max(len(source.copies), 1)
    return call(
        kernel,
        LIMIT,
        5,
        in_specs=[SCALARS] + [ANY] * len(source.arrays),
        out_specs=[pl.BlockSpec(memory_space=pltpu.VMEM)] * len(layout),
        out_shape=[shape_of((rows, columns), BF) for *_, columns in layout],
        scratch_shapes=[pltpu.SemaphoreType.DMA],
        name="place_rows",
    )(source.table, *source.arrays)


class Scatter:
    def __init__(self, ring, mine, other):
        self.ring, self.kept, self.other = ring, mine, other
        self.came = self.sides = self.lines = self.leaving = ()

    def start_core(self):
        if self.ring.square:
            self.came = self.ring.swap(self.other, CORE)

    def block(self, y, x):
        dp = self.ring.dp

        def pick(value):
            value = value.reshape(dp, 2, 2, value.shape[0] // (4 * dp), value.shape[1])
            value = lax.dynamic_index_in_dim(value, y, 1, keepdims=False)
            return lax.dynamic_index_in_dim(value, x, 1, keepdims=False)

        return pick(self.kept).astype(F32) + pick(self.came).astype(F32)

    def ready_sides(self):
        ring = self.ring
        if ring.square:
            to_x = self.block(ring.y, 1 - ring.x).astype(BF)
            to_y = self.block(1 - ring.y, ring.x).astype(BF)
            corner = self.block(1 - ring.y, 1 - ring.x).astype(BF)
            self.leaving = (corner, to_x, to_y)

    def start_sides(self):
        ring = self.ring
        if ring.square:
            corner, to_x, to_y = self.leaving
            self.sides = (ring.swap(corner, X_SIDE | Y_SIDE), ring.swap(to_x, X_SIDE), ring.swap(to_y, Y_SIDE))

    def ready_line(self):
        ring = self.ring
        if ring.square:
            line = self.block(ring.y, ring.x)
            for side in self.sides:
                line = line + side.astype(F32)
            low = line.astype(BF)
            self.own = lax.dynamic_index_in_dim(line, ring.z, 0, keepdims=False)
            self.leaving = tuple(
                lax.dynamic_index_in_dim(low, (ring.z + by) % ring.dp, 0, keepdims=False) for by in range(1, ring.dp)
            )

    def start_line(self):
        ring = self.ring
        if ring.square:
            self.lines = tuple(ring.shift(value, by) for by, value in enumerate(self.leaving, 1))

    def finish(self):
        ring = self.ring
        if not ring.square:
            halves = (ring.mine(self.kept, self.other), ring.mine(self.other, self.kept))
            return tuple(
                lax.psum_scatter(half.astype(F32), AXES, scatter_dimension=0, tiled=True) for half in halves
            )
        total = self.own
        for line in self.lines:
            total = total + line.astype(F32)
        rows = total.shape[0] // 2
        kept, sent = ring.mine(total[:rows], total[rows:]), ring.mine(total[rows:], total[:rows])
        came = ring.swap(sent, CORE)
        return ring.mine(kept, came), ring.mine(came, kept)


def solution(mesh):
    rows_split = P(AXES, None)
    vector_split = P(AXES)

    def per_device(
        tokens,
        segment_ids,
        output_grad,
        query_weight,
        query_bias,
        key_weight,
        value_weight,
        value_bias,
        output_weight,
        output_bias,
        first_gain,
        first_shift,
        inner_weight,
        inner_bias,
        outer_weight,
        outer_bias,
        second_gain,
        second_shift,
    ):
        ring = Ring(mesh)
        devices = ring.dp * ring.fsdp
        width = tokens.shape[1]
        hidden = inner_weight.shape[1]
        own = query_bias.shape[0]
        half = hidden // 2
        singles = (query_bias, value_bias, output_bias, first_gain, first_shift, outer_bias, second_gain, second_shift)
        count = len(singles)
        beside = ring.square and own > count and own * WIDTHS <= BLOCK
        columns = []
        if beside:
            row = lax.broadcasted_iota(jnp.int32, (own, BLOCK), 0)
            block = jnp.zeros((own, own), BF)
            for n, vector in enumerate(singles):
                block = jnp.where(row[:, :own] == n, vector[None], block)
            wide = jnp.where(row[:, : WIDTHS * own] == count, inner_bias[None], jnp.zeros((), BF))
            columns = [
                jnp.pad(block, ((0, 0), (0, BLOCK - own))) + jnp.pad(wide, ((0, 0), (0, BLOCK - WIDTHS * own)))
            ]

        def side(*parts):
            return jnp.concatenate(parts, axis=1)

        one = Gather(ring, (side(query_weight, key_weight, *columns), side(value_weight, output_weight, *columns)))
        two = Gather(ring, (inner_weight, outer_weight))
        pair = 2 * width
        one.start_core()
        one.start_line()
        one.came, two.halves = tie(one.came, two.halves)
        one.ready_line()
        one.start_sides()
        two.start_core()
        two.start_line()
        one.start_corners()
        one.cross(one.line, *one.sides)
        one.cross(*one.corners)
        source_one = one.source()
        two.came, _ = tie(two.came, one.crossed)
        two.ready_line()
        two.start_sides()
        layout = ((0, 0, pair), (1, 0, pair)) + (((0, pair, BLOCK),) if beside else ())
        query_key, value_output, *vectors = place_rows(source_one, layout)
        if beside:
            vectors = vectors[0].astype(F32).reshape(devices, own, BLOCK)
            vec = vectors[:, :count, :own].transpose(1, 0, 2).reshape(count, width)
            bi = vectors[:, count, : WIDTHS * own].reshape(WIDTHS, 1, width)
        else:
            vec = jnp.stack([lax.all_gather(entry, AXES, tiled=True) for entry in singles]).astype(F32)
            bi = lax.all_gather(inner_bias, AXES, tiled=True).astype(F32).reshape(WIDTHS, 1, width)
        q, k, v, att, p = attend(tokens, query_key, value_output, vec, segment_ids[0])
        hat, scale, normed, normed_t, second, x_t = first_norm(tokens, att, value_output, vec)
        normed, two.sides = tie(normed, two.sides)
        two.start_corners()
        two.cross(two.line, *two.sides)
        two.cross(*two.corners)
        source_two = two.source()
        act, slope, out, feed, feed_t, mine_hi, other_hi, mine_lo, other_lo, grad, bias_hi, sums_b = feed_all(
            source_two, normed, bi, second, output_grad, vec, normed_t
        )
        high = Scatter(ring, mine_hi, other_hi)
        high.start_core()
        grad, high.came = tie(grad, high.came)
        high.ready_sides()
        grad, high.leaving = tie(grad, high.leaving)
        high.start_sides()
        mine_lo, other_lo, first_g, att_g, wo_g, bias_0, sums_a = feed_zero(
            source_two, vec, feed, feed_t, normed_t, act, slope, grad, hat, scale, att, value_output, mine_lo, other_lo
        )
        low = Scatter(ring, mine_lo, other_lo)
        att_g, low.other, high.sides = tie(att_g, low.other, high.sides)
        low.start_core()
        high.ready_line()
        att_g, high.leaving = tie(att_g, high.leaving)
        high.start_line()
        pairs = HEADS // 4
        *low_g, all_a, sums_c = attend_backward(0, pairs, q, k, v, p, att_g)
        all_a, low.came, high.lines = tie(all_a, low.came, high.lines)
        low.ready_sides()
        all_a, low.leaving = tie(all_a, low.leaving)
        low.start_sides()
        left = Scatter(ring, *project_grads(ring.c, x_t, all_a, wo_g, 0, None))
        att_g, left.other = tie(att_g, left.other)
        left.start_core()
        *high_g, all_b, sums_d = attend_backward(pairs, pairs, q, k, v, p, att_g)
        all_b, left.came = tie(all_b, left.came)
        left.ready_sides()
        all_b, left.leaving = tie(all_b, left.leaving)
        left.start_sides()
        attention_sums = jnp.concatenate([sums_c[:2], sums_d[:2]], axis=1)
        rows = jnp.concatenate([attention_sums, sums_a[2:3], sums_a[:2], sums_b[2:3], sums_b[:2]], axis=0)
        bias_g = jnp.concatenate([bias_0, bias_hi], axis=0)
        columns_g = None
        if beside:
            rows = rows.reshape(count, devices, own).transpose(1, 0, 2)
            rows = jnp.pad(rows, ((0, 0), (0, own - count), (0, BLOCK - own)))
            bias_g = bias_g.reshape(devices, 1, WIDTHS * own)
            bias_g = jnp.pad(bias_g, ((0, 0), (count, own - count - 1), (0, BLOCK - WIDTHS * own)))
            columns_g = (rows + bias_g).reshape(width, BLOCK).astype(BF)
        right = Scatter(ring, *project_grads(ring.c, x_t, all_b, wo_g, 1, columns_g))
        first_g, right.other, low.sides = tie(first_g, right.other, low.sides)
        right.start_core()
        low.ready_line()
        low.leaving, right.came = tie(low.leaving, right.came)
        low.start_line()
        right.ready_sides()
        first_g, right.leaving = tie(first_g, right.leaving)
        right.start_sides()
        in_g = input_grads((0, 1), first_g, low_g, high_g, query_key, value_output, None)
        in_g, left.sides = tie(in_g, left.sides)
        left.ready_line()
        in_g, left.leaving = tie(in_g, left.leaving)
        left.start_line()
        in_g = input_grads((2, 3), first_g, low_g, high_g, query_key, value_output, in_g)
        in_g, right.sides, low.lines = tie(in_g, right.sides, low.lines)
        right.ready_line()
        right.start_line()

        high_r, low_r, left_r, right_r = high.finish(), low.finish(), left.finish(), right.finish()
        outer_g, inner_g = [side(lower, higher) for lower, higher in zip(low_r, high_r)]
        split = pairs * BLOCK
        wq_g, wk_g, wv_g, wo_g = [
            side(left_r[n // 2][:, at : at + split], right_r[n // 2][:, at : at + split])
            for n, at in enumerate((0, split, 0, split))
        ]
        if beside:
            last = right_r[0][:, 2 * split :]
            vectors_g = [last[n, :own] for n in range(count)] + [last[count, : WIDTHS * own]]
        else:
            vectors_g = [
                lax.psum_scatter(entry, AXES, scatter_dimension=0, tiled=True)
                for entry in list(rows) + [bias_g.reshape(hidden)]
            ]
        bq_g, bv_g, bo_g, ga_g, sa_g, bu_g, gb_g, sb_g, bi_g = vectors_g
        return (
            out, in_g, wq_g, bq_g, wk_g, wv_g, bv_g, wo_g, bo_g, ga_g, sa_g, inner_g, bi_g, outer_g, bu_g, gb_g, sb_g,
        )

    layered = P(None, AXES, None)
    return jax.shard_map(
        per_device,
        mesh=mesh,
        in_specs=(
            rows_split, rows_split, layered, rows_split, vector_split, rows_split, rows_split, vector_split,
            rows_split, vector_split, vector_split, vector_split, rows_split, vector_split, rows_split,
            vector_split, vector_split, vector_split,
        ),
        out_specs=(
            layered, layered, rows_split, vector_split, rows_split, rows_split, vector_split, rows_split,
            vector_split, vector_split, vector_split, rows_split, vector_split, rows_split, vector_split,
            vector_split, vector_split,
        ),
        check_vma=False,
    )
```

time: 425 us -> 344 us (0.81)
  local copies, waits for them, and re-layouts: 54 us -> 21.7 us
  waiting for transfers between devices: 104 us -> 76 us
  Pallas kernels: 179 us -> 157 us
  other arithmetic: 19.6 us -> 28.1 us
    ppermute x42 -> x40, waiting for transfers between devices: 76.7 us -> 36.6 us  [swap(): return lax.ppermute(value, AXES, [(i, i ^ bit) for i in range(total)])]
    pallas_call x9 -> x11, Pallas kernels: 179 us -> 157 us  [the longest x1 58.9 us: feed_all(): call(functools.partial(feed_all_kernel, source), LIMIT, 58, in_specs=[SCA...]
    ppermute x18, waiting for transfers between devices: 27.3 us -> 39.3 us  [shift(): lax.ppermute(value, AXES, [(i, (i + by * self.fsdp) % total) for i in ran...]
    unnamed x46 -> x47, local copies, waits for them, and re-layouts: 12.8 us -> 2.18 us
    concatenate x14 -> x1, local copies, waits for them, and re-layouts: 10.8 us -> 1.36 us  [per_device(): jnp.concatenate([attention_sums, sums_a[2:3], sums_a[:2], sums_b[2:3], su...]
    another operation x23 -> x2, local copies, waits for them, and re-layouts: 10.5 us -> 1.37 us  [the longest x1 0.68 us: pieces(): return (arrays, copies, jnp.stack(at + [jnp.asarray(ring.c, jnp.int32)]))]
    squeeze x7 -> x6, local copies, waits for them, and re-layouts: 7.33 us -> 2.68 us  [the longest x4 1.62 us: ready_line(): lax.dynamic_index_in_dim(low, (ring.z + by) % ring.dp, 0, keepdims=False)]
    select_n x0 -> x16, other arithmetic: none -> 4.5 us  [the longest x14 3.06 us: mine(): return jnp.where(self.c == 0, first, second)]
  transfers between devices with their start and end apart: 60 -> 58, of which waited for: 25 -> 21; matrix products, arithmetic and copies ran while one was open for 12% -> 10% of each run, Pallas kernels for 10% -> 28%
where the time goes in v2:
time: 344 us; the launch traced here: 340 us
  Pallas kernels  157 us (46%)
  waiting for transfers between devices  76 us (22%)
  starting transfers between devices  55.5 us (16%)
  other arithmetic  28.1 us (8%)
  local copies, waits for them, and re-layouts  21.7 us (6%)
    pallas_call x1, Pallas kernels, feed_all(): call(functools.partial(feed_all_kernel, source), LIMIT, 58, in_specs=[SCA...  58.9 us
    ppermute x18, waiting for transfers between devices, shift(): lax.ppermute(value, AXES, [(i, (i + by * self.fsdp) % total) for i in ran...  39.3 us
    ppermute x40, waiting for transfers between devices, swap(): return lax.ppermute(value, AXES, [(i, i ^ bit) for i in range(total)])  36.6 us
    pallas_call x1, Pallas kernels, feed_zero(): call(functools.partial(feed_zero_kernel, source), LIMIT, 28, in_specs=[SC...  28.8 us
    ppermute x18, starting transfers between devices, shift(): lax.ppermute(value, AXES, [(i, (i + by * self.fsdp) % total) for i in ran...  28.2 us
    ppermute x40, starting transfers between devices, swap(): return lax.ppermute(value, AXES, [(i, i ^ bit) for i in range(total)])  27.4 us
    pallas_call x2, Pallas kernels, attend_backward(): call(functools.partial(attend_back_kernel, first_pair, pairs), LIMIT, 10,...  19.1 us
    pallas_call x2, Pallas kernels, input_grads(): call(functools.partial(input_kernel, some), LIMIT, 8, grid=(len(some),),...  16.2 us
  transfers between devices with their start and end apart: 58, of which 21 were waited for; matrix products, arithmetic and copies ran while one was open for 10% of the time, Pallas kernels for 28%

profile of v2, /device:TPU:0, one launch (start us, length us, event | category | flops | bytes accessed | tf_op | source)
XLA Modules:
  0.0 340.1 jit_solution(665123131185973880)
XLA Ops:
  4.5 5.0 %collective-permute-start.3 = (bf16[48,1664]{1,0:T(8,128)(2,1)S(1)}, bf16[48,1664]{1,0:T(8,128)(2,1)S(1)}, u32[]{:S(2)}, u32[]{:S(2)}) collective-permute-start(bf16[48,1664]{1,0:T(8,128)(2,1)S(1)} %maximum_select_fusion.3), channel_id=1, source_target_pairs={{0,24},{1,25},{2,26},{3,27},{4,28},{5,29},{6,30},{7,31},{8,0},{9,1... | collective-permute-start | bytes 479240 | tf_op jit(solution)/shard_map/ppermute | solution.py:821
  10.5 3.5 %collective-permute-done.3 = bf16[48,1664]{1,0:T(8,128)(2,1)S(1)} collective-permute-done((bf16[48,1664]{1,0:T(8,128)(2,1)S(1)}, bf16[48,1664]{1,0:T(8,128)(2,1)S(1)}, u32[]{:S(2)}, u32[]{:S(2)}) %collective-permute-start.3) | collective-permute-done | bytes 159776 | tf_op jit(solution)/shard_map/ppermute | solution.py:821
  14.0 9.3 %collective-permute-done.2 = bf16[48,1664]{1,0:T(8,128)(2,1)S(1)} collective-permute-done((bf16[48,1664]{1,0:T(8,128)(2,1)S(1)}, bf16[48,1664]{1,0:T(8,128)(2,1)S(1)}, u32[]{:S(2)}, u32[]{:S(2)}) %collective-permute-start.2) | collective-permute-done | bytes 159776 | tf_op jit(solution)/shard_map/ppermute | solution.py:821
  24.5 1.6 collective-permute-start.5
  26.1 1.5 collective-permute-start.4
  28.8 1.8 collective-permute-start.15
  30.6 1.9 collective-permute-start.14
  32.5 8.8 %collective-permute-done.5.refs_2_ = bf16[4,48,1664]{2,1,0:T(8,128)(2,1)S(1)} collective-permute-done((bf16[4,48,1664]{2,1,0:T(8,128)(2,1)S(1)}, bf16[4,48,1664]{2,1,0:T(8,128)(2,1)S(1)}, u32[]{:S(2)}, u32[]{:S(2)}) %collective-permute-start.5) | collective-permute-done | bytes 639008 | tf_op jit(solution)/shard_map/ppermute | solution.py:817
  41.4 1.6 collective-permute-start.7
  43.0 1.6 collective-permute-start.6
  44.6 12.0 %collective-permute-done.15 = bf16[48,3072]{1,0:T(8,128)(2,1)S(1)} collective-permute-done((bf16[48,3072]{1,0:T(8,128)(2,1)S(1)}, bf16[48,3072]{1,0:T(8,128)(2,1)S(1)}, u32[]{:S(2)}, u32[]{:S(2)}) %collective-permute-start.15) | collective-permute-done | bytes 294944 | tf_op jit(solution)/shard_map/ppermute | solution.py:821
  64.1 5.5 %place_rows.1 = (bf16[768,1536]{1,0:T(8,128)(2,1)}, bf16[768,1536]{1,0:T(8,128)(2,1)}, bf16[768,128]{1,0:T(8,128)(2,1)}) custom-call(s32[17]{0:T(128)} %stack.115.table, bf16[4,48,1664]{2,1,0:T(8,128)(2,1)} %copy-done.4, bf16[4,48,1664]{2,1,0:T(8,128)(2,1)} %copy-done.6, bf16[4,48,1664]{2,1,0:T(8,128)(2,1)} %copy-done.5, bf16[2,48,1664]{2,1,0:T(8,128)(2,1)} %copy-done.14, ...), custom_call_target="tpu_custom_call" | custom-call | bytes 16500000 | tf_op jit(solution)/shard_map/place_rows/pallas_call | solution.py:973
  71.2 1.6 reshape.422.vec
  72.8 9.6 %attend.1 = (bf16[512,768]{1,0:T(8,128)(2,1)}, bf16[512,768]{1,0:T(8,128)(2,1)}, bf16[512,768]{1,0:T(8,128)(2,1)}, bf16[512,768]{1,0:T(8,128)(2,1)}, bf16[12,4,128,384]{3,2,1,0:T(8,128)(2,1)}) custom-call(bf16[512,768]{1,0:T(8,128)(2,1)} %x.11, bf16[768,1536]{1,0:T(8,128)(2,1)} %get-tuple-element.139.wq.wk, bf16[768,1536]{1,0:T(8,128)(2,1)} %get-tuple-element.139.wq.wk, ...), custom_call_target="tpu_custom_call" | custom-call | bytes 31350000 | tf_op jit(solution)/shard_map/attend/pallas_call | solution.py:113
  82.4 9.8 %first_norm.1 = (bf16[4,512,768]{2,1,0:T(8,128)(2,1)}, f32[4,512,1]{2,1,0:T(8,128)}, bf16[4,512,768]{2,1,0:T(8,128)(2,1)}, bf16[4,768,512]{2,1,0:T(8,128)(2,1)},...) custom-call(bf16[512,768]{1,0:T(8,128)(2,1)} %x.11, bf16[512,768]{1,0:T(8,128)(2,1)} %get-tuple-element.141.att_a.att_b.att_h, ...), custom_call_target="tpu_custom_call" | custom-call | bytes 32010000 | tf_op jit(solution)/shard_map/first_norm/pallas_call | solution.py:184
  93.5 1.6 collective-permute-start.19
  95.6 12.6 %collective-permute-done.20.refs_4_ = bf16[2,48,3072]{2,1,0:T(8,128)(2,1)} collective-permute-done((bf16[2,48,3072]{2,1,0:T(8,128)(2,1)S(1)}, bf16[2,48,3072]{2,1,0:T(8,128)(2,1)}, u32[]{:S(2)}, u32[]{:S(2)}) %collective-permute-start.20) | collective-permute-done | bytes 589856 | tf_op jit(solution)/shard_map/ppermute | solution.py:817
  111.4 58.9 %feed_all.1 = (bf16[4,512,768]{2,1,0:T(8,128)(2,1)}, bf16[4,512,768]{2,1,0:T(8,128)(2,1)}, bf16[4,512,768]{2,1,0:T(8,128)(2,1)}, bf16[4,512,768]{2,1,0:T(8,128)(...) custom-call(s32[17]{0:T(128)} %stack.115.table, ...), custom_call_target="tpu_custom_call" | custom-call | bytes 191400000 | tf_op jit(solution)/shard_map/feed_all/pallas_call | solution.py:416
  170.7 4.5 %collective-permute-done.26 = bf16[768,1536]{1,0:T(8,128)(2,1)S(1)} collective-permute-done((bf16[768,1536]{1,0:T(8,128)(2,1)}, bf16[768,1536]{1,0:T(8,128)(2,1)S(1)}, u32[]{:S(2)}, u32[]{:S(2)}) %collective-permute-start.26) | collective-permute-done | bytes 2359328 | tf_op jit(solution)/shard_map/ppermute | solution.py:817
  175.2 2.9 fusion.8
  178.0 2.0 collective-permute-start.27
  181.5 28.8 %feed_zero.1 = (bf16[768,1536]{1,0:T(8,128)(2,1)}, bf16[768,1536]{1,0:T(8,128)(2,1)}, f32[4,512,768]{2,1,0:T(8,128)}, bf16[4,512,768]{2,1,0:T(8,128)(2,1)}, bf16...) custom-call(s32[17]{0:T(128)} %stack.115.table, ...), custom_call_target="tpu_custom_call", output_to_operand_aliasing={{0}: (22, {}), {1}: (23, {})} | custom-call | bytes 92400000 | tf_op jit(solution)/shard_map/feed_zero/pallas_call | solution.py:566
  211.4 2.0 fusion.43
  214.2 3.7 %collective-permute-start.33 = (bf16[48,1536]{1,0:T(8,128)(2,1)}, bf16[48,1536]{1,0:T(8,128)(2,1)S(1)}, u32[]{:S(2)}, u32[]{:S(2)}) collective-permute-start(bf16[48,1536]{1,0:T(8,128)(2,1)} %get-tuple-element.188), channel_id=1, source_target_pairs={{0,24},{1,25},{2,26},{3,27},{4,28},{5,29},{6,30},{7,31},{8,0},{9,1... | collective-permute-start | bytes 442376 | tf_op jit(solution)/shard_map/ppermute | solution.py:821
  218.0 11.3 %attend_backward.2 = (bf16[4,512,384]{2,1,0:T(8,128)(2,1)}, bf16[4,512,384]{2,1,0:T(8,128)(2,1)}, bf16[4,512,384]{2,1,0:T(8,128)(2,1)}, bf16[3,512,384]{2,1,0:T(8,128)(2,1)}, f32[8,384]{1,0:T(8,128)}) custom-call(bf16[512,768]{1,0:T(8,128)(2,1)} %get-tuple-element.170.q, bf16[512,768]{1,0:T(8,128)(2,1)} %get-tuple-element.171.k, ...), custom_call_target="tpu_custom_call" | custom-call | bytes 33000000 | tf_op jit(solution)/shard_map/attend_backward/pallas_call | solution.py:697
  229.4 3.0 fusion.11
  232.4 4.5 %project_grads.2 = (bf16[768,768]{1,0:T(8,128)(2,1)}, bf16[768,768]{1,0:T(8,128)(2,1)}) custom-call(s32[1]{0:T(128)} %bitcast.16.core, bf16[768,512]{1,0:T(8,128)(2,1)} %get-tuple-element.169.x_t, bf16[3,512,384]{2,1,0:T(8,128)(2,1)} %get-tuple-element.192.grads, bf16[768,768]{1,0:T(8,128)(2,1)} %get-tuple-element.193.wo_g), custom_call_target="tpu_custom_call" | custom-call | bytes 14850000 | tf_op jit(solution)/shard_map/project_grads/pallas_call | solution.py:742
  236.8 2.0 collective-permute-start.35
  247.8 7.8 %attend_backward.3 = (bf16[4,512,384]{2,1,0:T(8,128)(2,1)}, bf16[4,512,384]{2,1,0:T(8,128)(2,1)}, bf16[4,512,384]{2,1,0:T(8,128)(2,1)}, bf16[3,512,384]{2,1,0:T(8,128)(2,1)}, f32[8,384]{1,0:T(8,128)}) custom-call(bf16[512,768]{1,0:T(8,128)(2,1)} %get-tuple-element.170.q, bf16[512,768]{1,0:T(8,128)(2,1)} %get-tuple-element.171.k, ...), custom_call_target="tpu_custom_call" | custom-call | bytes 33000000 | tf_op jit(solution)/shard_map/attend_backward/pallas_call | solution.py:697
  258.2 1.5 reshape.429
  261.4 2.4 fusion.19
  263.9 5.0 %project_grads.3 = (bf16[768,896]{1,0:T(8,128)(2,1)}, bf16[768,896]{1,0:T(8,128)(2,1)}) custom-call(s32[1]{0:T(128)} %bitcast.16.core, bf16[768,512]{1,0:T(8,128)(2,1)} %get-tuple-element.169.x_t, bf16[3,512,384]{2,1,0:T(8,128)(2,1)} %get-tuple-element.201.grads, bf16[768,768]{1,0:T(8,128)(2,1)} %get-tuple-element.193.wo_g, bf16[768,128]{1,0:T(8,128)(2,1)} %bitcast.223), custom_call_target="tpu_custom_call" | custom-call | bytes 14850000 | tf_op jit(solution)/shard_map/project_grads/pallas_call | solution.py:742
  270.0 2.0 collective-permute-start.39
  273.6 2.1 fusion.41
  277.9 6.9 %input_grads.2.refs_0_ = f32[4,512,768]{2,1,0:T(8,128)} custom-call(f32[4,512,768]{2,1,0:T(8,128)} %get-tuple-element.219.first_g, bf16[4,512,384]{2,1,0:T(8,128)(2,1)} %get-tuple-element.220.dq_a, bf16[4,512,384]{2,1,0:T(8,128)(2,1)} %get-tuple-element.221.dk_a, bf16[4,512,384]{2,1,0:T(8,128)(2,1)} %get-tuple-element.222.dv_a, ...), custom_call_target="tpu_custom_call" | custom-call | bytes 26400000 | tf_op jit(solution)/shard_map/input_grads/pallas_call | solution.py:789
  284.8 2.4 collective-permute-done.40
  287.1 1.5 fusion.39
  290.8 2.8 collective-permute-start.50
  293.8 2.0 collective-permute-done.48
  295.7 2.1 collective-permute-done.49
  298.1 2.1 collective-permute-start.45
  301.5 2.0 collective-permute-start.42
  304.4 9.3 %input_grads.3 = f32[4,512,768]{2,1,0:T(8,128)} custom-call(f32[4,512,768]{2,1,0:T(8,128)} %get-tuple-element.219.first_g, bf16[4,512,384]{2,1,0:T(8,128)(2,1)} %get-tuple-element.220.dq_a, bf16[4,512,384]{2,1,0:T(8,128)(2,1)} %get-tuple-element.221.dk_a, bf16[4,512,384]{2,1,0:T(8,128)(2,1)} %get-tuple-element.222.dv_a, ...), custom_call_target="tpu_custom_call", output_to_operand_aliasing={{}: (10, {})} | custom-call | bytes 26400000 | tf_op jit(solution)/shard_map/input_grads/pallas_call | solution.py:789
  316.5 4.2 %collective-permute-done.47 = bf16[48,1536]{1,0:T(8,128)(2,1)S(1)} collective-permute-done((bf16[48,1536]{1,0:T(8,128)(2,1)}, bf16[48,1536]{1,0:T(8,128)(2,1)S(1)}, u32[]{:S(2)}, u32[]{:S(2)}) %collective-permute-start.47) | collective-permute-done | bytes 147488 | tf_op jit(solution)/shard_map/ppermute | solution.py:821
  320.7 2.5 collective-permute-done.44
  325.6 2.8 collective-permute-start.54
  328.6 2.6 collective-permute-done.52
  331.2 3.6 %collective-permute-done.53 = bf16[48,896]{1,0:T(8,128)(2,1)S(1)} collective-permute-done((bf16[48,896]{1,0:T(8,128)(2,1)S(1)}, bf16[48,896]{1,0:T(8,128)(2,1)S(1)}, u32[]{:S(2)}, u32[]{:S(2)}) %collective-permute-start.53) | collective-permute-done | bytes 86048 | tf_op jit(solution)/shard_map/ppermute | solution.py:821
  (193 shorter events, 58.4 us)
Async XLA Ops:
  4.5 9.6 %collective-permute-start.3 = (bf16[48,1664]{1,0:T(8,128)(2,1)S(1)}, bf16[48,1664]{1,0:T(8,128)(2,1)S(1)}, u32[]{:S(2)}, u32[]{:S(2)}) collective-permute-start(bf16[48,1664]{1,0:T(8,128)(2,1)S(1)} %maximum_select_fusion.3), channel_id=1, source_target_pairs={{0,24},{1,25},{2,26},{3,27},{4,28},{5,29},{6,30},{7,31},{8,0},{9,1... | collective-permute-start | bytes 479240 | tf_op jit(solution)/shard_map/ppermute | solution.py:821
  9.5 13.9 %collective-permute-start.2 = (bf16[48,1664]{1,0:T(8,128)(2,1)S(1)}, bf16[48,1664]{1,0:T(8,128)(2,1)S(1)}, u32[]{:S(2)}, u32[]{:S(2)}) collective-permute-start(bf16[48,1664]{1,0:T(8,128)(2,1)S(1)} %maximum_select_fusion.3), channel_id=1, source_target_pairs={{0,16},{1,17},{2,18},{3,19},{4,20},{5,21},{6,22},{7,23},{8,24},{9,... | collective-permute-start | bytes 479240 | tf_op jit(solution)/shard_map/ppermute | solution.py:821
  9.5 13.9 %collective-permute-start.1 = (bf16[48,1664]{1,0:T(8,128)(2,1)S(1)}, bf16[48,1664]{1,0:T(8,128)(2,1)S(1)}, u32[]{:S(2)}, u32[]{:S(2)}) collective-permute-start(bf16[48,1664]{1,0:T(8,128)(2,1)S(1)} %maximum_select_fusion.3), channel_id=1, source_target_pairs={{0,8},{1,9},{2,10},{3,11},{4,12},{5,13},{6,14},{7,15},{8,16},{9,17... | collective-permute-start | bytes 479240 | tf_op jit(solution)/shard_map/ppermute | solution.py:821
  24.5 16.8 %collective-permute-start.5 = (bf16[4,48,1664]{2,1,0:T(8,128)(2,1)S(1)}, bf16[4,48,1664]{2,1,0:T(8,128)(2,1)S(1)}, u32[]{:S(2)}, u32[]{:S(2)}) collective-permute-start(bf16[4,48,1664]{2,1,0:T(8,128)(2,1)S(1)} %pad_maximum_fusion.1.refs_0_), channel_id=1, source_target_pairs={{0,4},{1,5},{2,6},{3,7},{4,0},{5,1},{6,2},{7,3},{8,12},{9,13},{10,... | collective-permute-start | bytes 1916936 | tf_op jit(solution)/shard_map/ppermute | solution.py:817
  26.1 16.8 %collective-permute-start.4 = (bf16[4,48,1664]{2,1,0:T(8,128)(2,1)S(1)}, bf16[4,48,1664]{2,1,0:T(8,128)(2,1)S(1)}, u32[]{:S(2)}, u32[]{:S(2)}) collective-permute-start(bf16[4,48,1664]{2,1,0:T(8,128)(2,1)S(1)} %pad_maximum_fusion.1.refs_0_), channel_id=1, source_target_pairs={{0,2},{1,3},{2,0},{3,1},{4,6},{5,7},{6,4},{7,5},{8,10},{9,11},{10,... | collective-permute-start | bytes 1916936 | tf_op jit(solution)/shard_map/ppermute | solution.py:817
  27.7 16.9 %collective-permute-start.16 = (bf16[48,3072]{1,0:T(8,128)(2,1)S(1)}, bf16[48,3072]{1,0:T(8,128)(2,1)S(1)}, u32[]{:S(2)}, u32[]{:S(2)}) collective-permute-start(bf16[48,3072]{1,0:T(8,128)(2,1)S(1)} %maximum_select_fusion.1), channel_id=1, source_target_pairs={{0,24},{1,25},{2,26},{3,27},{4,28},{5,29},{6,30},{7,31},{8,0},{9,1... | collective-permute-start | bytes 884744 | tf_op jit(solution)/shard_map/ppermute | solution.py:821
  28.8 27.7 %collective-permute-start.15 = (bf16[48,3072]{1,0:T(8,128)(2,1)S(1)}, bf16[48,3072]{1,0:T(8,128)(2,1)S(1)}, u32[]{:S(2)}, u32[]{:S(2)}) collective-permute-start(bf16[48,3072]{1,0:T(8,128)(2,1)S(1)} %maximum_select_fusion.1), channel_id=1, source_target_pairs={{0,16},{1,17},{2,18},{3,19},{4,20},{5,21},{6,22},{7,23},{8,24},{9,... | collective-permute-start | bytes 884744 | tf_op jit(solution)/shard_map/ppermute | solution.py:821
  30.6 26.0 %collective-permute-start.14 = (bf16[48,3072]{1,0:T(8,128)(2,1)S(1)}, bf16[48,3072]{1,0:T(8,128)(2,1)S(1)}, u32[]{:S(2)}, u32[]{:S(2)}) collective-permute-start(bf16[48,3072]{1,0:T(8,128)(2,1)S(1)} %maximum_select_fusion.1), channel_id=1, source_target_pairs={{0,8},{1,9},{2,10},{3,11},{4,12},{5,13},{6,14},{7,15},{8,16},{9,17... | collective-permute-start | bytes 884744 | tf_op jit(solution)/shard_map/ppermute | solution.py:821
  41.4 15.7 %collective-permute-start.7 = (bf16[2,48,1664]{2,1,0:T(8,128)(2,1)S(1)}, bf16[2,48,1664]{2,1,0:T(8,128)(2,1)S(1)}, u32[]{:S(2)}, u32[]{:S(2)}) collective-permute-start(bf16[2,48,1664]{2,1,0:T(8,128)(2,1)S(1)} %slice.196), channel_id=1, source_target_pairs={{0,2},{1,3},{2,0},{3,1},{4,6},{5,7},{6,4},{7,5},{8,10},{9,11},{10,... | collective-permute-start | bytes 958472 | tf_op jit(solution)/shard_map/ppermute | solution.py:817
  43.0 14.2 %collective-permute-start.6 = (bf16[2,48,1664]{2,1,0:T(8,128)(2,1)S(1)}, bf16[2,48,1664]{2,1,0:T(8,128)(2,1)S(1)}, u32[]{:S(2)}, u32[]{:S(2)}) collective-permute-start(bf16[2,48,1664]{2,1,0:T(8,128)(2,1)S(1)} %slice.195), channel_id=1, source_target_pairs={{0,4},{1,5},{2,6},{3,7},{4,0},{5,1},{6,2},{7,3},{8,12},{9,13},{10,... | collective-permute-start | bytes 958472 | tf_op jit(solution)/shard_map/ppermute | solution.py:817
  44.6 13.1 %collective-permute-start.8 = (bf16[4,48,1664]{2,1,0:T(8,128)(2,1)S(1)}, bf16[4,48,1664]{2,1,0:T(8,128)(2,1)S(1)}, u32[]{:S(2)}, u32[]{:S(2)}) collective-permute-start(bf16[4,48,1664]{2,1,0:T(8,128)(2,1)S(1)} %pad_maximum_fusion.1.refs_0_), channel_id=1, source_target_pairs={{0,1},{1,0},{2,3},{3,2},{4,5},{5,4},{6,7},{7,6},{8,9},{9,8},{10,11... | collective-permute-start | bytes 1916936 | tf_op jit(solution)/shard_map/ppermute | solution.py:817
  61.2 30.9 %collective-permute-start.18 = (bf16[4,48,3072]{2,1,0:T(8,128)(2,1)S(1)}, bf16[4,48,3072]{2,1,0:T(8,128)(2,1)S(1)}, u32[]{:S(2)}, u32[]{:S(2)}) collective-permute-start(bf16[4,48,3072]{2,1,0:T(8,128)(2,1)S(1)} %pad_maximum_fusion.refs_0_), channel_id=1, source_target_pairs={{0,4},{1,5},{2,6},{3,7},{4,0},{5,1},{6,2},{7,3},{8,12},{9,13},{10,... | collective-permute-start | bytes 3538952 | tf_op jit(solution)/shard_map/ppermute | solution.py:817
  61.7 30.4 %collective-permute-start.17 = (bf16[4,48,3072]{2,1,0:T(8,128)(2,1)S(1)}, bf16[4,48,3072]{2,1,0:T(8,128)(2,1)S(1)}, u32[]{:S(2)}, u32[]{:S(2)}) collective-permute-start(bf16[4,48,3072]{2,1,0:T(8,128)(2,1)S(1)} %pad_maximum_fusion.refs_0_), channel_id=1, source_target_pairs={{0,2},{1,3},{2,0},{3,1},{4,6},{5,7},{6,4},{7,5},{8,10},{9,11},{10,... | collective-permute-start | bytes 3538952 | tf_op jit(solution)/shard_map/ppermute | solution.py:817
  64.1 46.5 %collective-permute-start.21 = (bf16[4,48,3072]{2,1,0:T(8,128)(2,1)S(1)}, bf16[4,48,3072]{2,1,0:T(8,128)(2,1)}, u32[]{:S(2)}, u32[]{:S(2)}) collective-permute-start(bf16[4,48,3072]{2,1,0:T(8,128)(2,1)S(1)} %pad_maximum_fusion.refs_0_), channel_id=1, source_target_pairs={{0,1},{1,0},{2,3},{3,2},{4,5},{5,4},{6,7},{7,6},{8,9},{9,8},{10,11... | collective-permute-start | bytes 3538952 | tf_op jit(solution)/shard_map/ppermute | solution.py:817
  92.2 15.9 %collective-permute-start.20 = (bf16[2,48,3072]{2,1,0:T(8,128)(2,1)S(1)}, bf16[2,48,3072]{2,1,0:T(8,128)(2,1)}, u32[]{:S(2)}, u32[]{:S(2)}) collective-permute-start(bf16[2,48,3072]{2,1,0:T(8,128)(2,1)S(1)} %slice.163), channel_id=1, source_target_pairs={{0,2},{1,3},{2,0},{3,1},{4,6},{5,7},{6,4},{7,5},{8,10},{9,11},{10,... | collective-permute-start | bytes 1769480 | tf_op jit(solution)/shard_map/ppermute | solution.py:817
  93.5 15.6 %collective-permute-start.19 = (bf16[2,48,3072]{2,1,0:T(8,128)(2,1)S(1)}, bf16[2,48,3072]{2,1,0:T(8,128)(2,1)}, u32[]{:S(2)}, u32[]{:S(2)}) collective-permute-start(bf16[2,48,3072]{2,1,0:T(8,128)(2,1)S(1)} %slice.162), channel_id=1, source_target_pairs={{0,4},{1,5},{2,6},{3,7},{4,0},{5,1},{6,2},{7,3},{8,12},{9,13},{10,... | collective-permute-start | bytes 1769480 | tf_op jit(solution)/shard_map/ppermute | solution.py:817
  95.0 16.4 %collective-permute-start.22 = (bf16[4,48,3072]{2,1,0:T(8,128)(2,1)S(1)}, bf16[4,48,3072]{2,1,0:T(8,128)(2,1)}, u32[]{:S(2)}, u32[]{:S(2)}) collective-permute-start(bf16[4,48,3072]{2,1,0:T(8,128)(2,1)S(1)} %collective-permute-done.17.refs_1_), channel_id=1, source_target_pairs={{0,1},{1,0},{2,3},{3,2},{4,5},{5,4},{6,7},{7,6},{8,9},{9,8},{10,11... | collective-permute-start | bytes 3538952 | tf_op jit(solution)/shard_map/ppermute | solution.py:817
  95.1 16.4 %collective-permute-start.23 = (bf16[4,48,3072]{2,1,0:T(8,128)(2,1)S(1)}, bf16[4,48,3072]{2,1,0:T(8,128)(2,1)}, u32[]{:S(2)}, u32[]{:S(2)}) collective-permute-start(bf16[4,48,3072]{2,1,0:T(8,128)(2,1)S(1)} %collective-permute-done.18.refs_2_), channel_id=1, source_target_pairs={{0,1},{1,0},{2,3},{3,2},{4,5},{5,4},{6,7},{7,6},{8,9},{9,8},{10,11... | collective-permute-start | bytes 3538952 | tf_op jit(solution)/shard_map/ppermute | solution.py:817
  170.4 4.8 %collective-permute-start.26 = (bf16[768,1536]{1,0:T(8,128)(2,1)}, bf16[768,1536]{1,0:T(8,128)(2,1)S(1)}, u32[]{:S(2)}, u32[]{:S(2)}) collective-permute-start(bf16[768,1536]{1,0:T(8,128)(2,1)} %get-tuple-element.159), channel_id=1, source_target_pairs={{0,1},{1,0},{2,3},{3,2},{4,5},{5,4},{6,7},{7,6},{8,9},{9,8},{10,11... | collective-permute-start | bytes 7077896 | tf_op jit(solution)/shard_map/ppermute | solution.py:817
  178.0 32.3 %collective-permute-start.27 = (bf16[4,48,1536]{2,1,0:T(8,128)(2,1)}, bf16[4,48,1536]{2,1,0:T(8,128)(2,1)}, u32[]{:S(2)}, u32[]{:S(2)}) collective-permute-start(bf16[4,48,1536]{2,1,0:T(8,128)(2,1)} %get-tuple-element.176), channel_id=1, source_target_pairs={{0,6},{1,7},{2,4},{3,5},{4,2},{5,3},{6,0},{7,1},{8,14},{9,15},{10,... | collective-permute-start | bytes 1769480 | tf_op jit(solution)/shard_map/ppermute | solution.py:817
  180.0 30.3 %collective-permute-start.28 = (bf16[4,48,1536]{2,1,0:T(8,128)(2,1)}, bf16[4,48,1536]{2,1,0:T(8,128)(2,1)S(1)}, u32[]{:S(2)}, u32[]{:S(2)}) collective-permute-start(bf16[4,48,1536]{2,1,0:T(8,128)(2,1)} %get-tuple-element.177), channel_id=1, source_target_pairs={{0,2},{1,3},{2,0},{3,1},{4,6},{5,7},{6,4},{7,5},{8,10},{9,11},{10,... | collective-permute-start | bytes 1769480 | tf_op jit(solution)/shard_map/ppermute | solution.py:817
  181.0 29.3 %collective-permute-start.29 = (bf16[4,48,1536]{2,1,0:T(8,128)(2,1)}, bf16[4,48,1536]{2,1,0:T(8,128)(2,1)S(1)}, u32[]{:S(2)}, u32[]{:S(2)}) collective-permute-start(bf16[4,48,1536]{2,1,0:T(8,128)(2,1)} %get-tuple-element.178), channel_id=1, source_target_pairs={{0,4},{1,5},{2,6},{3,7},{4,0},{5,1},{6,2},{7,3},{8,12},{9,13},{10,... | collective-permute-start | bytes 1769480 | tf_op jit(solution)/shard_map/ppermute | solution.py:817
  210.4 18.9 %collective-permute-start.30 = (bf16[768,1536]{1,0:T(8,128)(2,1)}, bf16[768,1536]{1,0:T(8,128)(2,1)}, u32[]{:S(2)}, u32[]{:S(2)}) collective-permute-start(bf16[768,1536]{1,0:T(8,128)(2,1)} %get-tuple-element.185), channel_id=1, source_target_pairs={{0,1},{1,0},{2,3},{3,2},{4,5},{5,4},{6,7},{7,6},{8,9},{9,8},{10,11... | collective-permute-start | bytes 7077896 | tf_op jit(solution)/shard_map/ppermute | solution.py:817
  214.1 15.1 %collective-permute-start.31 = (bf16[48,1536]{1,0:T(8,128)(2,1)}, bf16[48,1536]{1,0:T(8,128)(2,1)S(1)}, u32[]{:S(2)}, u32[]{:S(2)}) collective-permute-start(bf16[48,1536]{1,0:T(8,128)(2,1)} %get-tuple-element.186), channel_id=1, source_target_pairs={{0,8},{1,9},{2,10},{3,11},{4,12},{5,13},{6,14},{7,15},{8,16},{9,17... | collective-permute-start | bytes 442376 | tf_op jit(solution)/shard_map/ppermute | solution.py:821
  214.2 15.2 %collective-permute-start.32 = (bf16[48,1536]{1,0:T(8,128)(2,1)}, bf16[48,1536]{1,0:T(8,128)(2,1)S(1)}, u32[]{:S(2)}, u32[]{:S(2)}) collective-permute-start(bf16[48,1536]{1,0:T(8,128)(2,1)} %get-tuple-element.187), channel_id=1, source_target_pairs={{0,16},{1,17},{2,18},{3,19},{4,20},{5,21},{6,22},{7,23},{8,24},{9,... | collective-permute-start | bytes 442376 | tf_op jit(solution)/shard_map/ppermute | solution.py:821
  214.2 15.1 %collective-permute-start.33 = (bf16[48,1536]{1,0:T(8,128)(2,1)}, bf16[48,1536]{1,0:T(8,128)(2,1)S(1)}, u32[]{:S(2)}, u32[]{:S(2)}) collective-permute-start(bf16[48,1536]{1,0:T(8,128)(2,1)} %get-tuple-element.188), channel_id=1, source_target_pairs={{0,24},{1,25},{2,26},{3,27},{4,28},{5,29},{6,30},{7,31},{8,0},{9,1... | collective-permute-start | bytes 442376 | tf_op jit(solution)/shard_map/ppermute | solution.py:821
  236.8 24.6 %collective-permute-start.34 = (bf16[768,768]{1,0:T(8,128)(2,1)}, bf16[768,768]{1,0:T(8,128)(2,1)}, u32[]{:S(2)}, u32[]{:S(2)}) collective-permute-start(bf16[768,768]{1,0:T(8,128)(2,1)} %get-tuple-element.197), channel_id=1, source_target_pairs={{0,1},{1,0},{2,3},{3,2},{4,5},{5,4},{6,7},{7,6},{8,9},{9,8},{10,11... | collective-permute-start | bytes 3538952 | tf_op jit(solution)/shard_map/ppermute | solution.py:817
  236.8 32.0 %collective-permute-start.35 = (bf16[4,48,1536]{2,1,0:T(8,128)(2,1)}, bf16[4,48,1536]{2,1,0:T(8,128)(2,1)}, u32[]{:S(2)}, u32[]{:S(2)}) collective-permute-start(bf16[4,48,1536]{2,1,0:T(8,128)(2,1)} %get-tuple-element.209), channel_id=1, source_target_pairs={{0,6},{1,7},{2,4},{3,5},{4,2},{5,3},{6,0},{7,1},{8,14},{9,15},{10,... | collective-permute-start | bytes 1769480 | tf_op jit(solution)/shard_map/ppermute | solution.py:817
  238.8 30.0 %collective-permute-start.36 = (bf16[4,48,1536]{2,1,0:T(8,128)(2,1)}, bf16[4,48,1536]{2,1,0:T(8,128)(2,1)}, u32[]{:S(2)}, u32[]{:S(2)}) collective-permute-start(bf16[4,48,1536]{2,1,0:T(8,128)(2,1)} %get-tuple-element.210), channel_id=1, source_target_pairs={{0,2},{1,3},{2,0},{3,1},{4,6},{5,7},{6,4},{7,5},{8,10},{9,11},{10,... | collective-permute-start | bytes 1769480 | tf_op jit(solution)/shard_map/ppermute | solution.py:817
  239.8 29.0 %collective-permute-start.37 = (bf16[4,48,1536]{2,1,0:T(8,128)(2,1)}, bf16[4,48,1536]{2,1,0:T(8,128)(2,1)}, u32[]{:S(2)}, u32[]{:S(2)}) collective-permute-start(bf16[4,48,1536]{2,1,0:T(8,128)(2,1)} %get-tuple-element.211), channel_id=1, source_target_pairs={{0,4},{1,5},{2,6},{3,7},{4,0},{5,1},{6,2},{7,3},{8,12},{9,13},{10,... | collective-permute-start | bytes 1769480 | tf_op jit(solution)/shard_map/ppermute | solution.py:817
  268.8 7.6 %collective-permute-start.38 = (bf16[768,896]{1,0:T(8,128)(2,1)}, bf16[768,896]{1,0:T(8,128)(2,1)}, u32[]{:S(2)}, u32[]{:S(2)}) collective-permute-start(bf16[768,896]{1,0:T(8,128)(2,1)} %get-tuple-element.217), channel_id=1, source_target_pairs={{0,1},{1,0},{2,3},{3,2},{4,5},{5,4},{6,7},{7,6},{8,9},{9,8},{10,11... | collective-permute-start | bytes 4128776 | tf_op jit(solution)/shard_map/ppermute | solution.py:817
  270.0 14.7 %collective-permute-start.39 = (bf16[4,48,768]{2,1,0:T(8,128)(2,1)}, bf16[4,48,768]{2,1,0:T(8,128)(2,1)}, u32[]{:S(2)}, u32[]{:S(2)}) collective-permute-start(bf16[4,48,768]{2,1,0:T(8,128)(2,1)} %get-tuple-element.226), channel_id=1, source_target_pairs={{0,6},{1,7},{2,4},{3,5},{4,2},{5,3},{6,0},{7,1},{8,14},{9,15},{10,... | collective-permute-start | bytes 884744 | tf_op jit(solution)/shard_map/ppermute | solution.py:817
  272.1 15.1 %collective-permute-start.40 = (bf16[4,48,768]{2,1,0:T(8,128)(2,1)}, bf16[4,48,768]{2,1,0:T(8,128)(2,1)}, u32[]{:S(2)}, u32[]{:S(2)}) collective-permute-start(bf16[4,48,768]{2,1,0:T(8,128)(2,1)} %get-tuple-element.227), channel_id=1, source_target_pairs={{0,2},{1,3},{2,0},{3,1},{4,6},{5,7},{6,4},{7,5},{8,10},{9,11},{10,... | collective-permute-start | bytes 884744 | tf_op jit(solution)/shard_map/ppermute | solution.py:817
  273.1 14.1 %collective-permute-start.41 = (bf16[4,48,768]{2,1,0:T(8,128)(2,1)}, bf16[4,48,768]{2,1,0:T(8,128)(2,1)}, u32[]{:S(2)}, u32[]{:S(2)}) collective-permute-start(bf16[4,48,768]{2,1,0:T(8,128)(2,1)} %get-tuple-element.228), channel_id=1, source_target_pairs={{0,4},{1,5},{2,6},{3,7},{4,0},{5,1},{6,2},{7,3},{8,12},{9,13},{10,... | collective-permute-start | bytes 884744 | tf_op jit(solution)/shard_map/ppermute | solution.py:817
  288.7 7.1 %collective-permute-start.48 = (bf16[48,768]{1,0:T(8,128)(2,1)S(1)}, bf16[48,768]{1,0:T(8,128)(2,1)S(1)}, u32[]{:S(2)}, u32[]{:S(2)}) collective-permute-start(bf16[48,768]{1,0:T(8,128)(2,1)S(1)} %get-tuple-element.241), channel_id=1, source_target_pairs={{0,8},{1,9},{2,10},{3,11},{4,12},{5,13},{6,14},{7,15},{8,16},{9,17... | collective-permute-start | bytes 221192 | tf_op jit(solution)/shard_map/ppermute | solution.py:821
  290.0 7.9 %collective-permute-start.49 = (bf16[48,768]{1,0:T(8,128)(2,1)S(1)}, bf16[48,768]{1,0:T(8,128)(2,1)S(1)}, u32[]{:S(2)}, u32[]{:S(2)}) collective-permute-start(bf16[48,768]{1,0:T(8,128)(2,1)S(1)} %get-tuple-element.242), channel_id=1, source_target_pairs={{0,16},{1,17},{2,18},{3,19},{4,20},{5,21},{6,22},{7,23},{8,24},{9,... | collective-permute-start | bytes 221192 | tf_op jit(solution)/shard_map/ppermute | solution.py:821
  290.8 7.1 %collective-permute-start.50 = (bf16[48,768]{1,0:T(8,128)(2,1)S(1)}, bf16[48,768]{1,0:T(8,128)(2,1)S(1)}, u32[]{:S(2)}, u32[]{:S(2)}) collective-permute-start(bf16[48,768]{1,0:T(8,128)(2,1)S(1)} %get-tuple-element.243), channel_id=1, source_target_pairs={{0,24},{1,25},{2,26},{3,27},{4,28},{5,29},{6,30},{7,31},{8,0},{9,1... | collective-permute-start | bytes 221192 | tf_op jit(solution)/shard_map/ppermute | solution.py:821
  297.9 15.8 %collective-permute-start.51 = (f32[24,768]{1,0:T(8,128)S(1)}, f32[24,768]{1,0:T(8,128)}, u32[]{:S(2)}, u32[]{:S(2)}) collective-permute-start(f32[24,768]{1,0:T(8,128)S(1)} %slice_select_fusion.6), channel_id=1, source_target_pairs={{0,1},{1,0},{2,3},{3,2},{4,5},{5,4},{6,7},{7,6},{8,9},{9,8},{10,11... | collective-permute-start | bytes 221192 | tf_op jit(solution)/shard_map/ppermute | solution.py:817
  298.1 17.2 %collective-permute-start.45 = (bf16[48,1536]{1,0:T(8,128)(2,1)}, bf16[48,1536]{1,0:T(8,128)(2,1)S(1)}, u32[]{:S(2)}, u32[]{:S(2)}) collective-permute-start(bf16[48,1536]{1,0:T(8,128)(2,1)} %get-tuple-element.237), channel_id=1, source_target_pairs={{0,8},{1,9},{2,10},{3,11},{4,12},{5,13},{6,14},{7,15},{8,16},{9,17... | collective-permute-start | bytes 442376 | tf_op jit(solution)/shard_map/ppermute | solution.py:821
  300.2 16.3 %collective-permute-start.46 = (bf16[48,1536]{1,0:T(8,128)(2,1)}, bf16[48,1536]{1,0:T(8,128)(2,1)S(1)}, u32[]{:S(2)}, u32[]{:S(2)}) collective-permute-start(bf16[48,1536]{1,0:T(8,128)(2,1)} %get-tuple-element.238), channel_id=1, source_target_pairs={{0,16},{1,17},{2,18},{3,19},{4,20},{5,21},{6,22},{7,23},{8,24},{9,... | collective-permute-start | bytes 442376 | tf_op jit(solution)/shard_map/ppermute | solution.py:821
  301.5 19.2 %collective-permute-start.42 = (bf16[4,48,896]{2,1,0:T(8,128)(2,1)S(1)}, bf16[4,48,896]{2,1,0:T(8,128)(2,1)S(1)}, u32[]{:S(2)}, u32[]{:S(2)}) collective-permute-start(bf16[4,48,896]{2,1,0:T(8,128)(2,1)S(1)} %get-tuple-element.234), channel_id=1, source_target_pairs={{0,6},{1,7},{2,4},{3,5},{4,2},{5,3},{6,0},{7,1},{8,14},{9,15},{10,... | collective-permute-start | bytes 1032200 | tf_op jit(solution)/shard_map/ppermute | solution.py:817
  303.4 17.3 %collective-permute-start.43 = (bf16[4,48,896]{2,1,0:T(8,128)(2,1)S(1)}, bf16[4,48,896]{2,1,0:T(8,128)(2,1)S(1)}, u32[]{:S(2)}, u32[]{:S(2)}) collective-permute-start(bf16[4,48,896]{2,1,0:T(8,128)(2,1)S(1)} %get-tuple-element.235), channel_id=1, source_target_pairs={{0,2},{1,3},{2,0},{3,1},{4,6},{5,7},{6,4},{7,5},{8,10},{9,11},{10,... | collective-permute-start | bytes 1032200 | tf_op jit(solution)/shard_map/ppermute | solution.py:817
  313.8 9.4 %collective-permute-start.44 = (bf16[4,48,896]{2,1,0:T(8,128)(2,1)S(1)}, bf16[4,48,896]{2,1,0:T(8,128)(2,1)S(1)}, u32[]{:S(2)}, u32[]{:S(2)}) collective-permute-start(bf16[4,48,896]{2,1,0:T(8,128)(2,1)S(1)} %get-tuple-element.236), channel_id=1, source_target_pairs={{0,4},{1,5},{2,6},{3,7},{4,0},{5,1},{6,2},{7,3},{8,12},{9,13},{10,... | collective-permute-start | bytes 1032200 | tf_op jit(solution)/shard_map/ppermute | solution.py:817
  315.3 5.4 %collective-permute-start.47 = (bf16[48,1536]{1,0:T(8,128)(2,1)}, bf16[48,1536]{1,0:T(8,128)(2,1)S(1)}, u32[]{:S(2)}, u32[]{:S(2)}) collective-permute-start(bf16[48,1536]{1,0:T(8,128)(2,1)} %get-tuple-element.239), channel_id=1, source_target_pairs={{0,24},{1,25},{2,26},{3,27},{4,28},{5,29},{6,30},{7,31},{8,0},{9,1... | collective-permute-start | bytes 442376 | tf_op jit(solution)/shard_map/ppermute | solution.py:821
  324.5 6.7 %collective-permute-start.52 = (bf16[48,896]{1,0:T(8,128)(2,1)S(1)}, bf16[48,896]{1,0:T(8,128)(2,1)S(1)}, u32[]{:S(2)}, u32[]{:S(2)}) collective-permute-start(bf16[48,896]{1,0:T(8,128)(2,1)S(1)} %get-tuple-element.283), channel_id=1, source_target_pairs={{0,8},{1,9},{2,10},{3,11},{4,12},{5,13},{6,14},{7,15},{8,16},{9,17... | collective-permute-start | bytes 258056 | tf_op jit(solution)/shard_map/ppermute | solution.py:821
  325.6 5.5 %collective-permute-start.54 = (bf16[48,896]{1,0:T(8,128)(2,1)S(1)}, bf16[48,896]{1,0:T(8,128)(2,1)S(1)}, u32[]{:S(2)}, u32[]{:S(2)}) collective-permute-start(bf16[48,896]{1,0:T(8,128)(2,1)S(1)} %get-tuple-element.284), channel_id=1, source_target_pairs={{0,24},{1,25},{2,26},{3,27},{4,28},{5,29},{6,30},{7,31},{8,0},{9,1... | collective-permute-start | bytes 258056 | tf_op jit(solution)/shard_map/ppermute | solution.py:821
  328.4 6.4 %collective-permute-start.53 = (bf16[48,896]{1,0:T(8,128)(2,1)S(1)}, bf16[48,896]{1,0:T(8,128)(2,1)S(1)}, u32[]{:S(2)}, u32[]{:S(2)}) collective-permute-start(bf16[48,896]{1,0:T(8,128)(2,1)S(1)} %get-tuple-element.285), channel_id=1, source_target_pairs={{0,16},{1,17},{2,18},{3,19},{4,20},{5,21},{6,22},{7,23},{8,24},{9,... | collective-permute-start | bytes 258056 | tf_op jit(solution)/shard_map/ppermute | solution.py:821
  328.5 6.4 %collective-permute-start.56 = (f32[24,1536]{1,0:T(8,128)S(1)}, f32[24,1536]{1,0:T(8,128)S(1)}, u32[]{:S(2)}, u32[]{:S(2)}) collective-permute-start(f32[24,1536]{1,0:T(8,128)S(1)} %slice_select_fusion.3), channel_id=1, source_target_pairs={{0,1},{1,0},{2,3},{3,2},{4,5},{5,4},{6,7},{7,6},{8,9},{9,8},{10,11... | collective-permute-start | bytes 442376 | tf_op jit(solution)/shard_map/ppermute | solution.py:817
  (33 other events, 179.5 us)

commit v3 on v2

--- a/solution.py
+++ b/solution.py
@@ -17,6 +17,8 @@
 F32 = jnp.float32
 MIB = 1024 * 1024
 LIMIT = 60
+LIMIT_PLACE = 60
+LIMIT_ATTEND = 60
 BYTES = 3.3e6
 
 
@@ -112,7 +114,7 @@
 
     return call(
         attend_kernel,
-        LIMIT,
+        LIMIT_ATTEND,
         9.5,
         grid=(steps,),
         in_specs=[
@@ -250,12 +252,12 @@
     half = weights.shape[1] // 2
     for r in range(0, length, ROWS):
         rows = slice(r, r + ROWS)
-        inner = matmul(normed[rows, :], weights[:, column : column + width]) + bias
+        inner = matmul(normed[rows, :], weights[:, pl.ds(column, width)]) + bias
         active, tilt = gelu_pair(inner)
         active = active.astype(BF)
         act[rows, :] = active
         slope[rows, :] = tilt.astype(BF)
-        second[rows, :] += matmul_last(active, weights[:, half + column : half + column + width])
+        second[rows, :] += matmul_last(active, weights[:, pl.ds(half + column, width)])
 
 
 def second_norm(second, og, vec, out, feed, feed_t, sums):
@@ -279,10 +281,10 @@
     lows = []
     for r in range(0, length, ROWS):
         rows = slice(r, r + ROWS)
-        raw = matmul(feed[rows, :], weights[:, half + column : half + column + width])
+        raw = matmul(feed[rows, :], weights[:, pl.ds(half + column, width)])
         low = (slope[rows, :].astype(F32) * raw).astype(BF)
         bias[...] += jnp.sum(low.astype(F32), axis=0, keepdims=True)
-        grads[rows, :] += matmul_last(low, weights[:, column : column + width])
+        grads[rows, :] += matmul_last(low, weights[:, pl.ds(column, width)])
         lows.append(low)
     inner[...] += matmul(normed_t[...], jnp.concatenate(lows, axis=0))
 
@@ -309,160 +311,292 @@
     return [copy_of(outer, mine_h, sem), copy_of(inner, other_h, sem)]
 
 
-def slot_of(j, w):
-    return w if j == 0 else feed_order((1, 2, 3)).index((j, j)) + w - j
-
-
-def feed_all_kernel(source, table, bi, vec, normed_h, second_h, og_h, normed_t_h, *refs):
+def feed_high_kernel(source, table, bi, vec, normed_h, second_h, og_h, normed_t_h, *refs):
     count = len(source.arrays)
     pieces, refs = refs[:count], refs[count:]
-    act_h, slope_h, out_h, feed_h, feed_t_h, mine_h, other_h, mine_lo_h, other_lo_h, grad_h, bias, sums = refs[:12]
+    act_h, slope_h, act_1_h, slope_1_h, out_h, feed_h, feed_t_h, mine_h, other_h, grad_h, bias, sums = refs[:12]
     weights, normed, second, og, normed_t, act, slope, feed, feed_t, outer, inner, outer_b, inner_b = refs[12:25]
-    sem_w, sem_n, sem_s, sem_og, sem_t, sem_act, sem_out, sem_give = refs[25:]
+    sem_w, sem_n, sem_act, sem_out, sem_give = refs[25:]
     width = normed.shape[2]
-    og_reads = [copy_of(og_h.at[j], og.at[j % 2], sem_og.at[j]) for j in range(WIDTHS)]
-
-    def start_rows(w):
-        copy_of(normed_h.at[w], normed.at[w], sem_n.at[w]).start()
-        copy_of(second_h.at[w], second.at[w], sem_s.at[w]).start()
-
-    start_rows(0)
-    source.start(table, pieces, weights, sem_w.at[0], 0, width, 0)
-    for w in range(1, WIDTHS):
-        start_rows(w)
-    og_reads[0].start()
-    og_reads[1].start()
-    for j in range(1, WIDTHS):
+    low = WIDTHS - 2
+
+    def rows_of(n):
+        return (
+            copy_of(normed_h.at[low + n], normed.at[n], sem_n.at[0, n]),
+            copy_of(second_h.at[low + n], second.at[n], sem_n.at[1, n]),
+            copy_of(og_h.at[low + n], og.at[n], sem_n.at[2, n]),
+            copy_of(normed_t_h.at[low + n], normed_t.at[n], sem_n.at[3, n]),
+        )
+
+    for copy in rows_of(1)[:2]:
+        copy.start()
+    for j in range(WIDTHS):
         source.start(table, pieces, weights, sem_w.at[j], j * width, width, j * width)
-    for w in range(1, WIDTHS):
-        copy_of(normed_t_h.at[w], normed_t.at[w - 1], sem_t.at[w - 1]).start()
+    for copy in rows_of(1)[2:] + rows_of(0):
+        copy.start()
     sums[...] = jnp.zeros_like(sums)
     bias[...] = jnp.zeros_like(bias)
-    writes = []
-    for j in range(WIDTHS):
-        source.wait(weights, sem_w.at[j], width, j * width)
-
-        def body(w, carry, j=j):
-            if j == 0:
-                copy_of(normed_h.at[w], normed.at[w], sem_n.at[w]).wait()
-                copy_of(second_h.at[w], second.at[w], sem_s.at[w]).wait()
-            at = slot_of(j, 0) + w
-            forward_step(normed.at[w], weights, bi[j], act.at[at], slope.at[at], second.at[w], j * width)
-            if j == 0:
-                copy_of(act.at[at], act_h.at[w], sem_act.at[w]).start()
-                copy_of(slope.at[at], slope_h.at[w], sem_act.at[w]).start()
+    for copy in rows_of(1)[:2]:
+        copy.wait()
+    writes, given = [], []
+    for n in (1, 0):
+        w = low + n
+        if n == 0:
+            for copy in rows_of(0)[:2]:
+                copy.wait()
+
+        def body(j, carry, n=n, w=w):
+            if n == 1:
+                source.wait(weights, sem_w.at[j], width, 0)
+            at = 4 * (1 - n) + j
+            column = pl.multiple_of(j * width, BLOCK)
+            forward_step(normed.at[n], weights, bi[j], act.at[at], slope.at[at], second.at[n], column)
+
+            @pl.when(j == 0)
+            def _():
+                copy_of(act.at[at], act_h.at[w], sem_act.at[n, 0]).start()
+                copy_of(slope.at[at], slope_h.at[w], sem_act.at[n, 1]).start()
+
+            @pl.when(j == 1)
+            def _():
+                copy_of(act.at[at], act_1_h.at[n], sem_act.at[n, 2]).start()
+                copy_of(slope.at[at], slope_1_h.at[n], sem_act.at[n, 3]).start()
+
             return carry
 
-        lax.fori_loop(j, WIDTHS, body, 0)
-        og_reads[j].wait()
-        second_norm(second.at[j], og.at[j % 2], vec, normed.at[j], feed.at[j], feed_t.at[j], sums)
-        if j + 2 < WIDTHS:
-            og_reads[j + 2].start()
-        for copy in (
-            copy_of(normed.at[j], out_h.at[j], sem_out.at[0, j]),
-            copy_of(feed.at[j], feed_h.at[j], sem_out.at[1, j]),
-            copy_of(feed_t.at[j], feed_t_h.at[j], sem_out.at[2, j]),
+        lax.fori_loop(0, w + 1, body, 0)
+        base = 4 * (1 - n)
+        writes += [
+            copy_of(act.at[base], act_h.at[w], sem_act.at[n, 0]),
+            copy_of(slope.at[base], slope_h.at[w], sem_act.at[n, 1]),
+            copy_of(act.at[base + 1], act_1_h.at[n], sem_act.at[n, 2]),
+            copy_of(slope.at[base + 1], slope_1_h.at[n], sem_act.at[n, 3]),
+        ]
+        for copy in rows_of(n)[2:]:
+            copy.wait()
+        second_norm(second.at[n], og.at[n], vec, normed.at[n], feed.at[n], feed_t.at[n], sums)
+        for m, copy in enumerate(
+            (
+                copy_of(normed.at[n], out_h.at[w], sem_out.at[0, n]),
+                copy_of(feed.at[n], feed_h.at[w], sem_out.at[1, n]),
+                copy_of(feed_t.at[n], feed_t_h.at[w], sem_out.at[2, n]),
+            )
         ):
             copy.start()
             writes.append(copy)
-        if j == 0:
-            for w in range(WIDTHS):
-                copy_of(act.at[w], act_h.at[w], sem_act.at[w]).wait()
-                copy_of(slope.at[w], slope_h.at[w], sem_act.at[w]).wait()
-    for w in range(1, WIDTHS):
-        copy_of(normed_t_h.at[w], normed_t.at[w - 1], sem_t.at[w - 1]).wait()
-        second[w] = feed[w].astype(F32)
-    given = {}
-    for j in (3, 2, 1):
+        second[n] = feed[n].astype(F32)
         outer[...] = jnp.zeros_like(outer)
         inner[...] = jnp.zeros_like(inner)
 
-        def back(w, carry, j=j):
-            at = slot_of(j, 0) + w
+        def back(m, carry, n=n, w=w):
+            at = jnp.where(m == 1, w, 4 + w) if n == 0 else w
             backward_step(
-                feed.at[w], feed_t.at[w], normed_t.at[w - 1], act.at[at], slope.at[at], weights, j * width,
-                outer, inner, second.at[w], bias.at[j - 1],
+                feed.at[m], feed_t.at[m], normed_t.at[m], act.at[at], slope.at[at], weights, w * width,
+                outer, inner, second.at[m], bias.at[n],
             )
-            if j == 1:
-                copy_of(second.at[w], grad_h.at[w - 1], sem_out.at[3, w]).start()
             return carry
 
-        lax.fori_loop(j, WIDTHS, back, 0)
-        slot = j % 2
-        if slot in given:
-            for copy in given[slot]:
+        lax.fori_loop(n, 2, back, 0)
+        outer_b[n] = outer[...].astype(BF)
+        inner_b[n] = inner[...].astype(BF)
+        columns = pl.ds(n * width, width)
+        given += give_halves(
+            table[source.core], outer_b.at[n], inner_b.at[n], mine_h.at[:, columns], other_h.at[:, columns], sem_give.at[n]
+        )
+    last = copy_of(second, grad_h, sem_out.at[3, 0])
+    last.start()
+    for copy in writes + given + [last]:
+        copy.wait()
+
+
+def feed_high(source, normed, bi, second, og, vec, normed_t):
+    _, length, width = normed.shape
+    four, four_t = (WIDTHS, length, width), (WIDTHS, width, length)
+    two, two_t = (2, length, width), (2, width, length)
+    slots = 7
+    return call(
+        functools.partial(feed_high_kernel, source),
+        LIMIT,
+        35,
+        in_specs=[SCALARS, held(bi), held(vec)] + [ANY] * (4 + len(source.arrays)),
+        out_specs=[ANY] * 10 + [held(vec), held(vec)],
+        out_shape=[
+            shape_of(four, BF),
+            shape_of(four, BF),
+            shape_of(two, BF),
+            shape_of(two, BF),
+            shape_of(four, BF),
+            shape_of(four, BF),
+            shape_of(four_t, BF),
+            shape_of((width, 2 * width), BF),
+            shape_of((width, 2 * width), BF),
+            shape_of(two, F32),
+            shape_of((2, 1, width), F32),
+            shape_of((8, width), F32),
+        ],
+        scratch_shapes=[
+            pltpu.VMEM((width, 8 * width), BF),
+            pltpu.VMEM(two, BF),
+            pltpu.VMEM(two, F32),
+            pltpu.VMEM(two, BF),
+            pltpu.VMEM(two_t, BF),
+            pltpu.VMEM((slots, length, width), BF),
+            pltpu.VMEM((slots, length, width), BF),
+            pltpu.VMEM(two, BF),
+            pltpu.VMEM(two_t, BF),
+            pltpu.VMEM((width, width), F32),
+            pltpu.VMEM((width, width), F32),
+            pltpu.VMEM((2, width, width), BF),
+            pltpu.VMEM((2, width, width), BF),
+            pltpu.SemaphoreType.DMA((WIDTHS, 2)),
+            pltpu.SemaphoreType.DMA((4, 2)),
+            pltpu.SemaphoreType.DMA((2, 4)),
+            pltpu.SemaphoreType.DMA((4, 2)),
+            pltpu.SemaphoreType.DMA((2,)),
+        ],
+        name="feed_high",
+    )(source.table, bi, vec, normed, second, og, normed_t, *source.arrays)
+
+
+def feed_mid_kernel(source, table, bi, vec, normed_h, second_h, og_h, normed_t_h, act_1_h, slope_1_h, grad_in, feed_in, feed_t_in, *refs):
+    count = len(source.arrays)
+    pieces, refs = refs[:count], refs[count + 3 :]
+    act_h, slope_h, out_h, feed_h, feed_t_h, mine_h, other_h, grad_h, bias, sums = refs[:10]
+    weights, normed, second, og, normed_t, act, slope, feed, feed_t, grads, outer, inner, outer_b, inner_b = refs[10:24]
+    sem_w, sem_n, sem_b, sem_act, sem_out, sem_give = refs[24:]
+    width = normed.shape[2]
+
+    def rows_of(w):
+        return (
+            copy_of(normed_h.at[w], normed.at[w], sem_n.at[0, w]),
+            copy_of(second_h.at[w], second.at[w], sem_n.at[1, w]),
+            copy_of(og_h.at[w], og.at[w], sem_n.at[2, w]),
+        )
+
+    def back_rows(m):
+        return (
+            copy_of(feed_t_in.at[2 + m], feed_t.at[2 + m], sem_b.at[0, m]),
+            copy_of(act_1_h.at[m], act.at[1 + m], sem_b.at[1, m]),
+            copy_of(feed_in.at[2 + m], feed.at[2 + m], sem_b.at[2, m]),
+            copy_of(slope_1_h.at[m], slope.at[1 + m], sem_b.at[3, m]),
+            copy_of(grad_in.at[m], grads.at[1 + m], sem_b.at[4, m]),
+        )
+
+    turned = [copy_of(normed_t_h.at[w], normed_t.at[w - 1], sem_n.at[3, w - 1]) for w in range(1, WIDTHS)]
+    for copy in rows_of(1)[:2]:
+        copy.start()
+    for j in range(2):
+        source.start(table, pieces, weights, sem_w.at[j], j * width, width, j * width)
+    for copy in rows_of(1)[2:] + rows_of(0) + (turned[0],) + back_rows(0) + (turned[1],) + back_rows(1) + (turned[2],):
+        copy.start()
+    sums[...] = jnp.zeros_like(sums)
+    bias[...] = jnp.zeros_like(bias)
+    outer[...] = jnp.zeros_like(outer)
+    inner[...] = jnp.zeros_like(inner)
+    writes = []
+    for w in (1, 0):
+        for copy in rows_of(w)[:2]:
+            copy.wait()
+        for j in range(w + 1):
+            if w == 1:
+                source.wait(weights, sem_w.at[j], width, 0)
+            at = 0 if j == 1 else 3 + w
+            forward_step(normed.at[w], weights, bi[j], act.at[at], slope.at[at], second.at[w], j * width)
+            if j == 0:
+                for m, copy in enumerate(
+                    (copy_of(act.at[at], act_h.at[w], sem_act.at[0, w]), copy_of(slope.at[at], slope_h.at[w], sem_act.at[1, w]))
+                ):
+                    copy.start()
+                    writes.append(copy)
+        rows_of(w)[2].wait()
+        second_norm(second.at[w], og.at[w], vec, normed.at[w], feed.at[w], feed_t.at[w], sums)
+        for copy in (
+            copy_of(normed.at[w], out_h.at[w], sem_out.at[0, w]),
+            copy_of(feed.at[w], feed_h.at[w], sem_out.at[1, w]),
+            copy_of(feed_t.at[w], feed_t_h.at[w], sem_out.at[2, w]),
+        ):
+            copy.start()
+            writes.append(copy)
+    grads[0] = feed[1].astype(F32)
+    for copy in turned:
+        copy.wait()
+
+    def back(m, carry):
+        @pl.when(m > 0)
+        def _():
+            for copy in back_rows(m - 1):
                 copy.wait()
-        outer_b[slot] = outer[...].astype(BF)
-        inner_b[slot] = inner[...].astype(BF)
-        columns = pl.ds(j % 2 * width, width)
-        targets = (mine_h, other_h) if j > 1 else (mine_lo_h, other_lo_h)
-        given[slot] = give_halves(
-            table[source.core], outer_b.at[slot], inner_b.at[slot], targets[0].at[:, columns], targets[1].at[:, columns],
-            sem_give.at[slot],
+
+        backward_step(
+            feed.at[1 + m], feed_t.at[1 + m], normed_t.at[m], act.at[m], slope.at[m], weights, width,
+            outer, inner, grads.at[m], bias.at[0],
         )
-    for copies in given.values():
-        writes += copies
-    for w in range(1, WIDTHS):
-        writes.append(copy_of(second.at[w], grad_h.at[w - 1], sem_out.at[3, w]))
+        copy_of(grads.at[m], grad_h.at[m], sem_out.at[3, m]).start()
+        return carry
+
+    lax.fori_loop(0, WIDTHS - 1, back, 0)
+    outer_b[...] = outer[...].astype(BF)
+    inner_b[...] = inner[...].astype(BF)
+    writes += give_halves(table[source.core], outer_b, inner_b, mine_h, other_h, sem_give)
+    writes += [copy_of(grads.at[m], grad_h.at[m], sem_out.at[3, m]) for m in range(WIDTHS - 1)]
     for copy in writes:
         copy.wait()
 
 
-def feed_all(source, normed, bi, second, og, vec, normed_t):
+def feed_mid(source, normed, bi, second, og, vec, normed_t, act_1, slope_1, grad, act, slope, out, feed, feed_t):
     _, length, width = normed.shape
     four, four_t = (WIDTHS, length, width), (WIDTHS, width, length)
+    two = (2, length, width)
     many = WIDTHS - 1
-    slots = len(feed_order((1, 2, 3)))
+    first = 12 + len(source.arrays)
     return call(
-        functools.partial(feed_all_kernel, source),
+        functools.partial(feed_mid_kernel, source),
         LIMIT,
-        58,
-        in_specs=[SCALARS, held(bi), held(vec)] + [ANY] * (4 + len(source.arrays)),
-        out_specs=[ANY] * 10 + [held(vec), held(vec)],
+        22,
+        in_specs=[SCALARS, held(bi), held(vec)] + [ANY] * (9 + len(source.arrays) + 3),
+        out_specs=[ANY] * 8 + [held(vec), held(vec)],
         out_shape=[
             shape_of(four, BF),
             shape_of(four, BF),
             shape_of(four, BF),
             shape_of(four, BF),
             shape_of(four_t, BF),
-            shape_of((width, 2 * width), BF),
-            shape_of((width, 2 * width), BF),
-            shape_of((width, 2 * width), BF),
-            shape_of((width, 2 * width), BF),
+            shape_of((width, width), BF),
+            shape_of((width, width), BF),
             shape_of((many, length, width), F32),
-            shape_of((many, 1, width), F32),
+            shape_of((1, 1, width), F32),
             shape_of((8, width), F32),
         ],
         scratch_shapes=[
-            pltpu.VMEM((width, 8 * width), BF),
-            pltpu.VMEM(four, BF),
-            pltpu.VMEM(four, F32),
-            pltpu.VMEM((2, length, width), BF),
+            pltpu.VMEM((width, 4 * width), BF),
+            pltpu.VMEM(two, BF),
+            pltpu.VMEM(two, F32),
+            pltpu.VMEM(two, BF),
             pltpu.VMEM((many, width, length), BF),
-            pltpu.VMEM((slots, length, width), BF),
-            pltpu.VMEM((slots, length, width), BF),
+            pltpu.VMEM((5, length, width), BF),
+            pltpu.VMEM((5, length, width), BF),
             pltpu.VMEM(four, BF),
             pltpu.VMEM(four_t, BF),
+            pltpu.VMEM((many, length, width), F32),
             pltpu.VMEM((width, width), F32),
             pltpu.VMEM((width, width), F32),
-            pltpu.VMEM((2, width, width), BF),
-            pltpu.VMEM((2, width, width), BF),
-            pltpu.SemaphoreType.DMA((WIDTHS, 2)),
-            pltpu.SemaphoreType.DMA((WIDTHS,)),
-            pltpu.SemaphoreType.DMA((WIDTHS,)),
-            pltpu.SemaphoreType.DMA((WIDTHS,)),
-            pltpu.SemaphoreType.DMA((many,)),
-            pltpu.SemaphoreType.DMA((WIDTHS,)),
-            pltpu.SemaphoreType.DMA((4, WIDTHS)),
-            pltpu.SemaphoreType.DMA((2,)),
+            pltpu.VMEM((width, width), BF),
+            pltpu.VMEM((width, width), BF),
+            pltpu.SemaphoreType.DMA((2, 2)),
+            pltpu.SemaphoreType.DMA((4, many)),
+            pltpu.SemaphoreType.DMA((5, 2)),
+            pltpu.SemaphoreType.DMA((2, 2)),
+            pltpu.SemaphoreType.DMA((4, many)),
+            pltpu.SemaphoreType.DMA,
         ],
-        name="feed_all",
-    )(source.table, bi, vec, normed, second, og, normed_t, *source.arrays)
+        input_output_aliases={10: 3, 11: 4, first: 0, first + 1: 1, first + 2: 2},
+        name="feed_mid",
+    )(source.table, bi, vec, normed, second, og, normed_t, act_1, slope_1, grad, feed, feed_t, *source.arrays, act, slope, out)
 
 
 def feed_zero_kernel(source, table, vec, feed_h, feed_t_h, normed_t_h, act_h, slope_h, grad_in, hat_h, scale_h, att_h, wo_h, *refs):
     count = len(source.arrays)
-    pieces, refs = refs[:count], refs[count + 2 :]
+    pieces, refs = refs[:count], refs[count:]
     mine_h, other_h, first_g_h, att_g_h, wo_g_h, bias, sums = refs[:7]
     weights, feed, feed_t, normed_t, act, slope, outer, inner, grads, outer_b, inner_b = refs[7:18]
     hat, scale, att, wo, att_g, total, wo_g, wo_g_b = refs[18:26]
@@ -505,14 +639,12 @@
             copy.wait()
 
         def ready():
-            for copy in reads(w)[2:]:
+            for copy in reads(w)[2:5]:
                 copy.wait()
 
             @pl.when(step == 0)
             def _():
                 source.wait(weights, sem_w, width, 0)
-                for copy in beside:
-                    copy.wait()
 
             @pl.when(w == 0)
             def _():
@@ -526,6 +658,14 @@
             feed.at[w], feed_t.at[w], normed_t.at[w], act.at[w], slope.at[w], weights, 0, outer, inner, grads.at[w],
             bias.at[0], ready,
         )
+        for copy in reads(w)[5:]:
+            copy.wait()
+
+        @pl.when(step == 0)
+        def _():
+            for copy in beside:
+                copy.wait()
+
         rough, factor = hat[w].astype(F32), scale[w]
         grad = grads[w]
         sums[0:1, :] += jnp.sum(grad * rough, axis=0, keepdims=True)
@@ -549,9 +689,7 @@
     lax.fori_loop(0, WIDTHS, body, 0)
     outer_b[...] = outer[...].astype(BF)
     inner_b[...] = inner[...].astype(BF)
-    writes = give_halves(
-        table[source.core], outer_b, inner_b, mine_h.at[:, pl.ds(0, width)], other_h.at[:, pl.ds(0, width)], sem_out.at[2]
-    )
+    writes = give_halves(table[source.core], outer_b, inner_b, mine_h, other_h, sem_out.at[2])
     wo_g_b[...] = wo_g[...].astype(BF)
     copy = copy_of(wo_g_b, wo_g_h, sem_out.at[2])
     copy.start()
@@ -559,19 +697,18 @@
         copy.wait()
 
 
-def feed_zero(source, vec, feed, feed_t, normed_t, act, slope, grad, hat, scale, att, wo, mine, other):
+def feed_zero(source, vec, feed, feed_t, normed_t, act, slope, grad, hat, scale, att, wo):
     _, length, width = feed.shape
     four, four_t = (WIDTHS, length, width), (WIDTHS, width, length)
-    first = 12 + len(source.arrays)
     return call(
         functools.partial(feed_zero_kernel, source),
         LIMIT,
         28,
-        in_specs=[SCALARS, held(vec)] + [ANY] * (10 + len(source.arrays) + 2),
+        in_specs=[SCALARS, held(vec)] + [ANY] * (10 + len(source.arrays)),
         out_specs=[ANY] * 5 + [held(vec), held(vec)],
         out_shape=[
-            shape_of(mine.shape, BF),
-            shape_of(other.shape, BF),
+            shape_of((width, width), BF),
+            shape_of((width, width), BF),
             shape_of(four, F32),
             shape_of(four, BF),
             shape_of((width, width), BF),
@@ -604,13 +741,15 @@
             pltpu.SemaphoreType.DMA((2,)),
             pltpu.SemaphoreType.DMA((3,)),
         ],
-        input_output_aliases={first: 0, first + 1: 1},
         name="feed_zero",
-    )(source.table, vec, feed, feed_t, normed_t, act, slope, grad, hat, scale, att, wo, *source.arrays, mine, other)
-
-
-def attend_back_kernel(first_pair, pairs, q, k, v, p, g, dq_o, dk_o, dv_o, all_o, sums_o, dk_t, dv_t):
-    pair = first_pair + pl.program_id(0)
+    )(source.table, vec, feed, feed_t, normed_t, act, slope, grad, hat, scale, att, wo, *source.arrays)
+
+
+def attend_back_kernel(first_pair, pairs, own, core, x_t, wo_g, q, k, v, p, g, *refs):
+    dq_o, dk_o, dv_o, mine_o, other_o, sums_o, dk_t, dv_t = refs
+    step = pl.program_id(0)
+    pair = first_pair + step
+    columns = pairs * BLOCK
     length = q.shape[0]
     spans = windows(length)
     factor = 1.0 / math.sqrt(HEAD_DIM)
@@ -671,10 +810,20 @@
             dv_o[w] = dv_t[w].astype(BF).T
             for n, ref in enumerate((dq_o, dk_o, dv_o)):
                 totals[n] += ref[w].astype(F32)
-        for n in range(3):
-            all_o[n] = totals[n].astype(BF)
-        sums_o[0:1, :] = jnp.sum(totals[0], axis=0, keepdims=True)
-        sums_o[1:2, :] = jnp.sum(totals[2], axis=0, keepdims=True)
+        here = pl.ds(pl.multiple_of(step * BLOCK, BLOCK), BLOCK)
+        beside = pl.ds(pl.multiple_of(columns + step * BLOCK, BLOCK), BLOCK)
+        sums_o[0:1, here] = jnp.sum(totals[0], axis=0, keepdims=True)
+        sums_o[1:2, here] = jnp.sum(totals[2], axis=0, keepdims=True)
+        parts = [matmul(x_t[...], total.astype(BF)).astype(BF) for total in totals]
+
+        def fill(first, second):
+            first[:, here] = parts[0]
+            first[:, beside] = parts[1]
+            second[:, here] = parts[2]
+            second[:, beside] = wo_g[...]
+
+        pl.when(core[0] == 0)(lambda: fill(mine_o, other_o))
+        pl.when(core[0] != 0)(lambda: fill(other_o, mine_o))
 
     heads_each = HEADS // WIDTHS
     firsts = [(2 * n) // heads_each for n in range(HEADS // 2)]
@@ -688,73 +837,81 @@
             run(first)
 
 
-def attend_backward(first_pair, pairs, q, k, v, p, g):
-    length = q.shape[0]
+def vector_rows(own, sums_o, given):
+    sums_c, sums_a, sums_b, sums_b2, bias_0, bias_1, bias_hi = given
+    width = sums_a.shape[1]
+    rows = [
+        jnp.concatenate([sums_c[0:1, :], sums_o[0:1, :]], axis=1),
+        jnp.concatenate([sums_c[1:2, :], sums_o[1:2, :]], axis=1),
+        sums_a[2:3, :],
+        sums_a[0:1, :],
+        sums_a[1:2, :],
+        sums_b[2:3, :] + sums_b2[2:3, :],
+        sums_b[0:1, :] + sums_b2[0:1, :],
+        sums_b[1:2, :] + sums_b2[1:2, :],
+        jnp.zeros((8, width), F32),
+    ]
+    for j in range(WIDTHS):
+        rows += [(bias_0[0], bias_1[0], bias_hi[0], bias_hi[1])[j]] * WIDTHS
+    rows.append(jnp.zeros((BLOCK - 16 - WIDTHS * WIDTHS, width), F32))
+    turned = jnp.concatenate(rows, axis=0).T
+    lane = lax.broadcasted_iota(jnp.int32, (own, BLOCK), 1)
+    blocks = []
+    each = width // (own * WIDTHS)
+    for j in range(WIDTHS):
+        for n in range(each):
+            at = (j * each + n) * own
+            block = jnp.where(lane < 8, turned[at : at + own, :], 0.0)
+            for m in range(WIDTHS):
+                start = (n * WIDTHS + m) * own
+                block = jnp.where(lane == 16 + WIDTHS * j + m, turned[start : start + own, :], block)
+            blocks.append(block.astype(BF))
+    return jnp.concatenate(blocks, axis=0)
+
+
+def attend_back_last_kernel(first_pair, pairs, own, *refs):
+    given, rest = refs[8:-8], refs[-8:]
+    attend_back_kernel(first_pair, pairs, own, *refs[:8], *rest)
+    if given:
+        mine_o, other_o, sums_o = rest[3:6]
+
+        @pl.when(pl.program_id(0) == pairs - 1)
+        def _():
+            block = vector_rows(own, sums_o, given)
+            mine_o[:, 2 * pairs * BLOCK :] = block
+            other_o[:, 2 * pairs * BLOCK :] = block
+
+
+def attend_backward(core, first_pair, pairs, own, x_t, wo_g, q, k, v, p, g, given):
+    length, width = q.shape
     columns = pairs * BLOCK
     part = pl.BlockSpec((length, BLOCK), lambda n: (0, first_pair + n))
     wide = pl.BlockSpec((WIDTHS, length, BLOCK), lambda n: (0, 0, first_pair + n))
     wide_o = pl.BlockSpec((WIDTHS, length, BLOCK), lambda n: (0, 0, n))
+    out = (width, 2 * columns + (BLOCK if given else 0))
     return call(
-        functools.partial(attend_back_kernel, first_pair, pairs),
+        functools.partial(attend_back_last_kernel, first_pair, pairs, own),
         LIMIT,
-        10,
+        12,
         grid=(pairs,),
-        in_specs=[part, part, part, pl.BlockSpec((2,) + p.shape[1:], lambda n: (first_pair + n, 0, 0, 0)), wide],
-        out_specs=[wide_o] * 3
-        + [pl.BlockSpec((3, length, BLOCK), lambda n: (0, 0, n)), pl.BlockSpec((8, BLOCK), lambda n: (0, n))],
+        in_specs=[
+            SCALARS,
+            whole(x_t.shape),
+            pl.BlockSpec((width, BLOCK), lambda n: (0, first_pair + n)),
+            part,
+            part,
+            part,
+            pl.BlockSpec((2,) + p.shape[1:], lambda n: (first_pair + n, 0, 0, 0)),
+            wide,
+        ]
+        + [whole(entry.shape) for entry in given],
+        out_specs=[wide_o] * 3 + [whole(out)] * 2 + [whole((8, columns))],
         out_shape=[shape_of((WIDTHS, length, columns), BF)] * 3
-        + [shape_of((3, length, columns), BF), shape_of((8, columns), F32)],
+        + [shape_of(out, BF)] * 2
+        + [shape_of((8, columns), F32)],
         scratch_shapes=[pltpu.VMEM((WIDTHS, BLOCK, length), F32)] * 2,
         name="attend_backward",
-    )(q, k, v, p, g)
-
-
-def project_kernel(core, x_t, grads, wo_g, last, mine_o, other_o):
-    rows = x_t[...]
-    columns = grads.shape[2]
-
-    def fill(first, second):
-        first[:, :columns] = matmul(rows, grads[0]).astype(BF)
-        first[:, columns : 2 * columns] = matmul(rows, grads[1]).astype(BF)
-        second[:, :columns] = matmul(rows, grads[2]).astype(BF)
-        second[:, columns : 2 * columns] = wo_g[...]
-        if last is not None:
-            first[:, 2 * columns :] = last[...]
-            second[:, 2 * columns :] = last[...]
-
-    @pl.when(core[0] == 0)
-    def _():
-        fill(mine_o, other_o)
-
-    @pl.when(core[0] != 0)
-    def _():
-        fill(other_o, mine_o)
-
-
-def project_grads(core, x_t, grads, wo_g, part, last):
-    width, length = x_t.shape
-    columns = grads.shape[2]
-    out = (width, 2 * columns + (0 if last is None else last.shape[1]))
-    given = [] if last is None else [last]
-    kernel = project_kernel
-    if last is None:
-        kernel = lambda core, x_t, grads, wo_g, *outs: project_kernel(core, x_t, grads, wo_g, None, *outs)
-    return call(
-        kernel,
-        LIMIT,
-        4.5,
-        grid=(1,),
-        in_specs=[
-            pl.BlockSpec(memory_space=pltpu.SMEM),
-            whole(x_t.shape),
-            whole(grads.shape),
-            pl.BlockSpec((width, columns), lambda n: (0, part)),
-        ]
-        + [whole(entry.shape) for entry in given],
-        out_specs=[whole(out)] * 2,
-        out_shape=[shape_of(out, BF)] * 2,
-        name="project_grads",
-    )(jnp.full((1,), core, jnp.int32), x_t, grads, wo_g, *given)
+    )(jnp.full((1,), core, jnp.int32), x_t, wo_g, q, k, v, p, g, *given)
 
 
 def input_kernel(some, first_g, dq_a, dk_a, dv_a, dq_b, dk_b, dv_b, wq, wk, wv, *refs):
@@ -807,7 +964,7 @@
     def __init__(self, mesh):
         self.dp = mesh.shape["dp"]
         self.fsdp = mesh.shape["fsdp"]
-        self.square = self.fsdp == 8 and self.dp % 2 == 0
+        self.square = self.fsdp == 8 and self.dp == 4
         index = lax.axis_index("fsdp")
         self.z = lax.axis_index("dp")
         self.y, self.x, self.c = index // 4, (index // 2) % 2, index % 2
@@ -819,6 +976,10 @@
     def shift(self, value, by):
         total = self.dp * self.fsdp
         return lax.ppermute(value, AXES, [(i, (i + by * self.fsdp) % total) for i in range(total)])
+
+    def along(self, value, bit):
+        total = self.dp * self.fsdp
+        return lax.ppermute(value, AXES, [(i, i ^ (bit * self.fsdp)) for i in range(total)])
 
     def mine(self, first, second):
         return jnp.where(self.c == 0, first, second)
@@ -840,14 +1001,16 @@
             came = ring.swap(sent, CORE)
             self.shard = ring.mine(jnp.concatenate([kept, came], axis=0), jnp.concatenate([came, kept], axis=0))
 
-    def start_line(self):
+    def start_line(self, first=0, columns=None):
         ring = self.ring
         if ring.square:
-            self.came = tuple(ring.shift(self.shard, by) for by in range(1, ring.dp))
+            part = self.shard[:, first : self.shard.shape[1] if columns is None else first + columns]
+            self.came += (tuple(ring.shift(part, by) for by in range(1, ring.dp)),)
 
     def ready_line(self):
         if self.ring.square:
-            self.line = jnp.stack((self.shard,) + self.came)
+            came = [jnp.concatenate(parts, axis=1) for parts in zip(*self.came)]
+            self.line = jnp.stack([self.shard] + came)
 
     def start_sides(self):
         ring = self.ring
@@ -887,6 +1050,37 @@
 
     def source(self):
         return Source(self)
+
+
+class PlaneFirst(Gather):
+    def start_plane(self):
+        ring = self.ring
+        if ring.square:
+            row = jnp.stack([self.shard, ring.swap(self.shard, X_SIDE)])
+            self.sides = (row, ring.swap(row, Y_SIDE))
+
+    def ready_line(self):
+        if self.ring.square:
+            self.line = jnp.concatenate(self.sides)
+
+    def start_line(self):
+        ring = self.ring
+        if ring.square:
+            self.came = tuple(ring.shift(self.line, by) for by in range(1, ring.dp))
+
+    def pieces(self):
+        ring = self.ring
+        rows = self.shard.shape[0]
+        copies, at = [], []
+        for behind in range(ring.dp):
+            z = (ring.z + ring.dp - behind) % ring.dp
+            for index, (y, x) in enumerate(
+                ((ring.y, ring.x), (ring.y, 1 - ring.x), (1 - ring.y, ring.x), (1 - ring.y, 1 - ring.x))
+            ):
+                copies.append((behind, index))
+                at.append(jnp.asarray(rows * ((z * 2 + y) * 2 + x), jnp.int32))
+        arrays = [self.line, *self.came, *self.crossed]
+        return arrays, copies, jnp.stack(at + [jnp.asarray(ring.c, jnp.int32)])
 
 
 class Source:
@@ -932,13 +1126,16 @@
             pltpu.make_async_copy(whole_half, whole_half, sems.at[half]).wait()
 
 
-def place_rows(source, layout):
+def place_rows(source, layout, beside):
+    count = len(source.arrays)
+    rows = source.rows * max(len(source.copies), 1)
+
     def kernel(table, *refs):
-        count = len(source.arrays)
-        pieces, outs, sem = refs[:count], refs[count:-1], refs[-1]
+        pieces, outs = refs[:count], refs[count : count + len(layout)]
+        sem = refs[-1]
         if not source.square:
             copies = [
-                pltpu.make_async_copy(pieces[half].at[:, pl.ds(first, columns)], outs[n], sem)
+                pltpu.make_async_copy(pieces[half].at[:, pl.ds(first, columns)], outs[n], sem.at[0])
                 for n, (half, first, columns) in enumerate(layout)
             ]
             for copy in copies:
@@ -948,44 +1145,84 @@
             return
         many = count // 2
         core = table[source.core]
+        parts = [(half, first, columns, outs[n], 0) for n, (half, first, columns) in enumerate(layout)]
+        if beside is not None:
+            vec, bi, block = refs[count + len(layout) : -1]
+            parts.insert(0, (0, beside, BLOCK, block, 1))
 
         def run(own):
             copies = []
-            for n, (half, first, columns) in enumerate(layout):
+            for half, first, columns, out, which in parts:
                 for m, (piece, index) in enumerate(source.copies):
                     row = pl.multiple_of(table[m], 16)
                     copies.append(
-                        pltpu.make_async_copy(
-                            pieces[piece + (0 if half == own else many)].at[index, :, pl.ds(first, columns)],
-                            outs[n].at[pl.ds(row, source.rows), :],
-                            sem,
+                        (
+                            which,
+                            pltpu.make_async_copy(
+                                pieces[piece + (0 if half == own else many)].at[index, :, pl.ds(first, columns)],
+                                out.at[pl.ds(row, source.rows), :],
+                                sem.at[which],
+                            ),
                         )
                     )
-            for copy in copies:
+            for _, copy in copies:
                 copy.start()
-            for copy in copies:
-                copy.wait()
+            for which, copy in copies:
+                if which == 1:
+                    copy.wait()
+            if beside is not None:
+                vector_columns(block, vec, bi)
+            for which, copy in copies:
+                if which == 0:
+                    copy.wait()
 
         for own in range(2):
             pl.when(core == own)(functools.partial(run, own))
 
-    rows = source.rows * max(len(source.copies), 1)
+    more = ([], [], [])
+    if beside is not None:
+        more = (
+            [pl.BlockSpec(memory_space=pltpu.VMEM)] * 2,
+            [shape_of((8, rows), F32), shape_of((WIDTHS, rows), F32)],
+            [pltpu.VMEM((rows, BLOCK), BF)],
+        )
     return call(
         kernel,
-        LIMIT,
+        LIMIT_PLACE,
         5,
-        in_specs=[SCALARS] + [ANY] * len(source.arrays),
-        out_specs=[pl.BlockSpec(memory_space=pltpu.VMEM)] * len(layout),
-        out_shape=[shape_of((rows, columns), BF) for *_, columns in layout],
-        scratch_shapes=[pltpu.SemaphoreType.DMA],
+        in_specs=[SCALARS] + [ANY] * count,
+        out_specs=[pl.BlockSpec(memory_space=pltpu.VMEM)] * len(layout) + more[0],
+        out_shape=[shape_of((rows, columns), BF) for *_, columns in layout] + more[1],
+        scratch_shapes=more[2] + [pltpu.SemaphoreType.DMA((2,))],
         name="place_rows",
     )(source.table, *source.arrays)
+
+
+def vector_columns(block, vec, bi):
+    full = block[...].astype(F32)
+    width = full.shape[0]
+    vec[...] = full.T[:8, :]
+    each = 8
+    own = width // (each * WIDTHS)
+    lane = lax.broadcasted_iota(jnp.int32, (own, BLOCK), 1)
+    pieces = []
+    for n in range(each):
+        for m in range(WIDTHS):
+            piece = jnp.zeros((own, BLOCK), F32)
+            for j in range(WIDTHS):
+                start = (j * each + n) * own
+                piece = jnp.where(lane == 16 + WIDTHS * j + m, full[start : start + own, :], piece)
+            pieces.append(piece)
+    turned = jnp.concatenate(pieces, axis=0).T
+    for j in range(WIDTHS):
+        at = 16 + WIDTHS * j
+        bi[j : j + 1, :] = jnp.sum(turned[at : at + WIDTHS, :], axis=0, keepdims=True)
 
 
 class Scatter:
     def __init__(self, ring, mine, other):
         self.ring, self.kept, self.other = ring, mine, other
-        self.came = self.sides = self.lines = self.leaving = ()
+        self.came = self.sides = self.leaving = self.far = self.near = self.own = ()
 
     def start_core(self):
         if self.ring.square:
@@ -1015,7 +1252,32 @@
             corner, to_x, to_y = self.leaving
             self.sides = (ring.swap(corner, X_SIDE | Y_SIDE), ring.swap(to_x, X_SIDE), ring.swap(to_y, Y_SIDE))
 
-    def ready_line(self):
+    def ready_far(self):
+        ring = self.ring
+        if ring.square:
+            line = self.block(ring.y, ring.x)
+            for side in self.sides:
+                line = line + side.astype(F32)
+            line = line.reshape(2, 2, *line.shape[1:])
+            self.leaving = lax.dynamic_index_in_dim(line, 1 - ring.z // 2, 0, keepdims=False).astype(BF)
+            self.own = lax.dynamic_index_in_dim(line, ring.z // 2, 0, keepdims=False)
+
+    def start_far(self):
+        if self.ring.square:
+            self.far = self.ring.along(self.leaving, 2)
+
+    def ready_near(self):
+        ring = self.ring
+        if ring.square:
+            pair = self.own + self.far.astype(F32)
+            self.leaving = lax.dynamic_index_in_dim(pair, 1 - ring.z % 2, 0, keepdims=False).astype(BF)
+            self.own = lax.dynamic_index_in_dim(pair, ring.z % 2, 0, keepdims=False)
+
+    def start_near(self):
+        if self.ring.square:
+            self.near = (self.ring.along(self.leaving, 1),)
+
+    def ready_last(self):
         ring = self.ring
         if ring.square:
             line = self.block(ring.y, ring.x)
@@ -1027,25 +1289,26 @@
                 lax.dynamic_index_in_dim(low, (ring.z + by) % ring.dp, 0, keepdims=False) for by in range(1, ring.dp)
             )
 
-    def start_line(self):
+    def start_last(self):
         ring = self.ring
         if ring.square:
-            self.lines = tuple(ring.shift(value, by) for by, value in enumerate(self.leaving, 1))
-
-    def finish(self):
-        ring = self.ring
-        if not ring.square:
-            halves = (ring.mine(self.kept, self.other), ring.mine(self.other, self.kept))
-            return tuple(
-                lax.psum_scatter(half.astype(F32), AXES, scatter_dimension=0, tiled=True) for half in halves
-            )
-        total = self.own
-        for line in self.lines:
-            total = total + line.astype(F32)
-        rows = total.shape[0] // 2
-        kept, sent = ring.mine(total[:rows], total[rows:]), ring.mine(total[rows:], total[:rows])
-        came = ring.swap(sent, CORE)
-        return ring.mine(kept, came), ring.mine(came, kept)
+            self.near = tuple(ring.shift(value, by) for by, value in enumerate(self.leaving, 1))
+
+
+def finish(ring, groups):
+    if not ring.square:
+        halves = (
+            jnp.concatenate([ring.mine(group.kept, group.other) for group in groups], axis=1),
+            jnp.concatenate([ring.mine(group.other, group.kept) for group in groups], axis=1),
+        )
+        return tuple(lax.psum_scatter(half.astype(F32), AXES, scatter_dimension=0, tiled=True) for half in halves)
+    total = jnp.concatenate(
+        [functools.reduce(lambda sum_, part: sum_ + part.astype(F32), group.near, group.own) for group in groups], axis=1
+    )
+    rows = total.shape[0] // 2
+    kept, sent = ring.mine(total[:rows], total[rows:]), ring.mine(total[rows:], total[:rows])
+    came = ring.swap(sent, CORE)
+    return ring.mine(kept, came), ring.mine(came, kept)
 
 
 def solution(mesh):
@@ -1080,17 +1343,18 @@
         half = hidden // 2
         singles = (query_bias, value_bias, output_bias, first_gain, first_shift, outer_bias, second_gain, second_shift)
         count = len(singles)
-        beside = ring.square and own > count and own * WIDTHS <= BLOCK
+        beside = ring.square and own % 8 == 0
         columns = []
         if beside:
-            row = lax.broadcasted_iota(jnp.int32, (own, BLOCK), 0)
-            block = jnp.zeros((own, own), BF)
+            row = lax.broadcasted_iota(jnp.int32, (BLOCK, own), 0)
+            block = jnp.zeros((BLOCK, own), BF)
             for n, vector in enumerate(singles):
-                block = jnp.where(row[:, :own] == n, vector[None], block)
-            wide = jnp.where(row[:, : WIDTHS * own] == count, inner_bias[None], jnp.zeros((), BF))
-            columns = [
-                jnp.pad(block, ((0, 0), (0, BLOCK - own))) + jnp.pad(wide, ((0, 0), (0, BLOCK - WIDTHS * own)))
-            ]
+                block = jnp.where(row == n, vector[None], block)
+            chunk = (ring.z * ring.fsdp + lax.axis_index("fsdp")) // (devices // WIDTHS)
+            for n in range(WIDTHS):
+                quarter = inner_bias[n * own : (n + 1) * own]
+                block = jnp.where(row == 16 + WIDTHS * chunk + n, quarter[None], block)
+            columns = [block.T]
 
         def side(*parts):
             return jnp.concatenate(parts, axis=1)
@@ -1099,111 +1363,128 @@
         two = Gather(ring, (inner_weight, outer_weight))
         pair = 2 * width
         one.start_core()
+        one.shard, two.halves = tie(one.shard, two.halves)
         one.start_line()
-        one.came, two.halves = tie(one.came, two.halves)
+        two.start_core()
+        one.came, two.shard = tie(one.came, two.shard)
         one.ready_line()
         one.start_sides()
-        two.start_core()
-        two.start_line()
+        two.start_line(0, half)
+        one.line, one.sides, two.came = tie(one.line, one.sides, two.came)
         one.start_corners()
-        one.cross(one.line, *one.sides)
-        one.cross(*one.corners)
-        source_one = one.source()
-        two.came, _ = tie(two.came, one.crossed)
+        two.start_line(half, half)
+        one.line, one.sides, one.corners, two.came = tie(one.line, one.sides, one.corners, two.came)
+        one.cross(one.line, *one.sides, *one.corners)
         two.ready_line()
         two.start_sides()
-        layout = ((0, 0, pair), (1, 0, pair)) + (((0, pair, BLOCK),) if beside else ())
-        query_key, value_output, *vectors = place_rows(source_one, layout)
+        source_one = one.source()
+        query_key, value_output, *vectors = place_rows(source_one, ((0, 0, pair), (1, 0, pair)), pair if beside else None)
         if beside:
-            vectors = vectors[0].astype(F32).reshape(devices, own, BLOCK)
-            vec = vectors[:, :count, :own].transpose(1, 0, 2).reshape(count, width)
-            bi = vectors[:, count, : WIDTHS * own].reshape(WIDTHS, 1, width)
+            vec, bi = vectors
+            bi = bi.reshape(WIDTHS, 1, width)
         else:
             vec = jnp.stack([lax.all_gather(entry, AXES, tiled=True) for entry in singles]).astype(F32)
             bi = lax.all_gather(inner_bias, AXES, tiled=True).astype(F32).reshape(WIDTHS, 1, width)
         q, k, v, att, p = attend(tokens, query_key, value_output, vec, segment_ids[0])
-        hat, scale, normed, normed_t, second, x_t = first_norm(tokens, att, value_output, vec)
-        normed, two.sides = tie(normed, two.sides)
+        att, two.line, two.sides = tie(att, two.line, two.sides)
         two.start_corners()
         two.cross(two.line, *two.sides)
+        hat, scale, normed, normed_t, second, x_t = first_norm(tokens, att, value_output, vec)
+        normed, two.corners, two.crossed = tie(normed, two.corners, two.crossed)
         two.cross(*two.corners)
         source_two = two.source()
-        act, slope, out, feed, feed_t, mine_hi, other_hi, mine_lo, other_lo, grad, bias_hi, sums_b = feed_all(
+
+        act, slope, act_1, slope_1, out, feed, feed_t, mine, other, grad, bias_hi, sums_b = feed_high(
             source_two, normed, bi, second, output_grad, vec, normed_t
         )
-        high = Scatter(ring, mine_hi, other_hi)
+        high = Scatter(ring, mine, other)
         high.start_core()
         grad, high.came = tie(grad, high.came)
         high.ready_sides()
         grad, high.leaving = tie(grad, high.leaving)
         high.start_sides()
-        mine_lo, other_lo, first_g, att_g, wo_g, bias_0, sums_a = feed_zero(
-            source_two, vec, feed, feed_t, normed_t, act, slope, grad, hat, scale, att, value_output, mine_lo, other_lo
+        act, slope, out, feed, feed_t, mine, other, grad, bias_1, sums_b2 = feed_mid(
+            source_two, normed, bi, second, output_grad, vec, normed_t, act_1, slope_1, grad, act, slope, out, feed, feed_t
         )
-        low = Scatter(ring, mine_lo, other_lo)
-        att_g, low.other, high.sides = tie(att_g, low.other, high.sides)
+        grad, other, high.sides = tie(grad, other, high.sides)
+
+        mid = Scatter(ring, mine, other)
+        mid.start_core()
+        high.ready_far()
+        mid.ready_sides()
+        grad, mid.leaving, high.leaving = tie(grad, mid.leaving, high.leaving)
+        mid.start_sides()
+        high.start_far()
+        mine, other, first_g, att_g, wo_g, bias_0, sums_a = feed_zero(
+            source_two, vec, feed, feed_t, normed_t, act, slope, grad, hat, scale, att, value_output
+        )
+        att_g, other, mid.sides, high.far = tie(att_g, other, mid.sides, high.far)
+
+        low = Scatter(ring, mine, other)
         low.start_core()
-        high.ready_line()
-        att_g, high.leaving = tie(att_g, high.leaving)
-        high.start_line()
+        high.ready_near()
+        mid.ready_far()
+        low.ready_sides()
+        att_g, low.leaving, mid.leaving, high.leaving = tie(att_g, low.leaving, mid.leaving, high.leaving)
+        low.start_sides()
+        mid.start_far()
+        high.start_near()
         pairs = HEADS // 4
-        *low_g, all_a, sums_c = attend_backward(0, pairs, q, k, v, p, att_g)
-        all_a, low.came, high.lines = tie(all_a, low.came, high.lines)
-        low.ready_sides()
-        all_a, low.leaving = tie(all_a, low.leaving)
-        low.start_sides()
-        left = Scatter(ring, *project_grads(ring.c, x_t, all_a, wo_g, 0, None))
-        att_g, left.other = tie(att_g, left.other)
+        *low_g, mine, other, sums_c = attend_backward(ring.c, 0, pairs, own, x_t, wo_g, q, k, v, p, att_g, ())
+        att_g, other, low.sides, mid.far, high.near = tie(att_g, other, low.sides, mid.far, high.near)
+
+        left = Scatter(ring, mine, other)
         left.start_core()
-        *high_g, all_b, sums_d = attend_backward(pairs, pairs, q, k, v, p, att_g)
-        all_b, left.came = tie(all_b, left.came)
+        mid.ready_near()
+        low.ready_far()
         left.ready_sides()
-        all_b, left.leaving = tie(all_b, left.leaving)
+        att_g, left.leaving, low.leaving, mid.leaving = tie(att_g, left.leaving, low.leaving, mid.leaving)
         left.start_sides()
-        attention_sums = jnp.concatenate([sums_c[:2], sums_d[:2]], axis=1)
-        rows = jnp.concatenate([attention_sums, sums_a[2:3], sums_a[:2], sums_b[2:3], sums_b[:2]], axis=0)
-        bias_g = jnp.concatenate([bias_0, bias_hi], axis=0)
-        columns_g = None
+        low.start_far()
+        mid.start_near()
+        given = (sums_c, sums_a, sums_b, sums_b2, bias_0, bias_1, bias_hi) if beside else ()
+        *high_g, mine, other, sums_d = attend_backward(
+            ring.c, pairs, pairs, own, x_t, wo_g, q, k, v, p, att_g, given
+        )
+        first_g, other, left.sides, low.far, mid.near = tie(first_g, other, left.sides, low.far, mid.near)
+
+        right = Scatter(ring, mine, other)
+        right.start_core()
+        low.ready_near()
+        left.ready_far()
+        right.ready_sides()
+        first_g, right.leaving, left.leaving, low.leaving = tie(first_g, right.leaving, left.leaving, low.leaving)
+        right.start_sides()
+        left.start_far()
+        low.start_near()
+        in_g = input_grads(tuple(range(WIDTHS)), first_g, low_g, high_g, query_key, value_output, None)
+        in_g, right.sides, left.far, low.near = tie(in_g, right.sides, left.far, low.near)
+
+        left.ready_near()
+        right.ready_last()
+        right.leaving, left.leaving = tie(right.leaving, left.leaving)
+        right.start_last()
+        left.start_near()
+        outer_g, inner_g = finish(ring, (low, mid, high))
+        right.near, left.near, outer_g = tie(right.near, left.near, outer_g)
+        first_half, second_half = finish(ring, (left, right))
+        split = pairs * BLOCK
+        parts = [
+            side(entry[:, at : at + split], entry[:, at + 2 * split : at + 3 * split])
+            for entry in (first_half, second_half)
+            for at in (0, split)
+        ]
+        wq_g, wk_g, wv_g, wo_g = parts
         if beside:
-            rows = rows.reshape(count, devices, own).transpose(1, 0, 2)
-            rows = jnp.pad(rows, ((0, 0), (0, own - count), (0, BLOCK - own)))
-            bias_g = bias_g.reshape(devices, 1, WIDTHS * own)
-            bias_g = jnp.pad(bias_g, ((0, 0), (count, own - count - 1), (0, BLOCK - WIDTHS * own)))
-            columns_g = (rows + bias_g).reshape(width, BLOCK).astype(BF)
-        right = Scatter(ring, *project_grads(ring.c, x_t, all_b, wo_g, 1, columns_g))
-        first_g, right.other, low.sides = tie(first_g, right.other, low.sides)
-        right.start_core()
-        low.ready_line()
-        low.leaving, right.came = tie(low.leaving, right.came)
-        low.start_line()
-        right.ready_sides()
-        first_g, right.leaving = tie(first_g, right.leaving)
-        right.start_sides()
-        in_g = input_grads((0, 1), first_g, low_g, high_g, query_key, value_output, None)
-        in_g, left.sides = tie(in_g, left.sides)
-        left.ready_line()
-        in_g, left.leaving = tie(in_g, left.leaving)
-        left.start_line()
-        in_g = input_grads((2, 3), first_g, low_g, high_g, query_key, value_output, in_g)
-        in_g, right.sides, low.lines = tie(in_g, right.sides, low.lines)
-        right.ready_line()
-        right.start_line()
-
-        high_r, low_r, left_r, right_r = high.finish(), low.finish(), left.finish(), right.finish()
-        outer_g, inner_g = [side(lower, higher) for lower, higher in zip(low_r, high_r)]
-        split = pairs * BLOCK
-        wq_g, wk_g, wv_g, wo_g = [
-            side(left_r[n // 2][:, at : at + split], right_r[n // 2][:, at : at + split])
-            for n, at in enumerate((0, split, 0, split))
-        ]
-        if beside:
-            last = right_r[0][:, 2 * split :]
-            vectors_g = [last[n, :own] for n in range(count)] + [last[count, : WIDTHS * own]]
+            last = first_half[:, 4 * split :]
+            bias_g = last[:, 16 : 16 + WIDTHS * WIDTHS].reshape(own, WIDTHS, WIDTHS).sum(axis=1)
+            vectors_g = [last[:, n] for n in range(count)] + [bias_g.T.reshape(own * WIDTHS)]
         else:
-            vectors_g = [
-                lax.psum_scatter(entry, AXES, scatter_dimension=0, tiled=True)
-                for entry in list(rows) + [bias_g.reshape(hidden)]
-            ]
+            attention_sums = jnp.concatenate([sums_c[:2], sums_d[:2]], axis=1)
+            sums_b = sums_b + sums_b2
+            rows = [*attention_sums, sums_a[2], sums_a[0], sums_a[1], sums_b[2], sums_b[0], sums_b[1]]
+            rows.append(jnp.concatenate([bias_0, bias_1, bias_hi], axis=0).reshape(hidden))
+            vectors_g = [lax.psum_scatter(entry, AXES, scatter_dimension=0, tiled=True) for entry in rows]
         bq_g, bv_g, bo_g, ga_g, sa_g, bu_g, gb_g, sb_g, bi_g = vectors_g
         return (
             out, in_g, wq_g, bq_g, wk_g, wv_g, bv_g, wo_g, bo_g, ga_g, sa_g, inner_g, bi_g, outer_g, bu_g, gb_g, sb_g,

time: 344 us -> 328 us (0.953)
  waiting for transfers between devices: 76 us -> 55.5 us
  starting transfers between devices: 55.5 us -> 66 us
  local copies, waits for them, and re-layouts: 21.7 us -> 15.6 us
  other arithmetic: 28.1 us -> 23.9 us
  Pallas kernels: 157 us -> 161 us
    ppermute x18 -> x12, waiting for transfers between devices: 39.3 us -> 25 us  [shift(): lax.ppermute(value, AXES, [(i, (i + by * self.fsdp) % total) for i in ran...]
    ppermute x40 -> x42, waiting for transfers between devices: 36.6 us -> 24.6 us  [swap(): return lax.ppermute(value, AXES, [(i, i ^ bit) for i in range(total)])]
    ppermute x0 -> x8, starting transfers between devices: none -> 12 us  [along(): lax.ppermute(value, AXES, [(i, i ^ bit * self.fsdp) for i in range(total)])]
    slice x10 -> x7, local copies, waits for them, and re-layouts: 8.45 us -> 1.88 us  [the longest x1 0.88 us: per_device(): quarter = inner_bias[n * own:(n + 1) * own]]
    convert_element_type x5 -> x1, other arithmetic: 7.78 us -> 1.21 us  [ready_last(): low = line.astype(BF)]
    add x5 -> x13, other arithmetic: 1.27 us -> 7.35 us  [the longest x4 6.16 us: ready_far(): line = line + side.astype(F32)]
    ppermute x0 -> x8, waiting for transfers between devices: none -> 5.84 us  [along(): lax.ppermute(value, AXES, [(i, i ^ bit * self.fsdp) for i in range(total)])]
    pallas_call x7 -> x6, Pallas kernels: 102 us -> 108 us  [the longest x1 39 us: feed_high(): call(functools.partial(feed_high_kernel, source), LIMIT, 35, in_specs=[SC...]
  transfers between devices with their start and end apart: 58 -> 62, of which waited for: 21 -> 25; matrix products, arithmetic and copies ran while one was open for 10% -> 5% of each run, Pallas kernels for 28% -> 38%
where the time goes in v3:
time: 328 us; the launch traced here: 324 us
  Pallas kernels  161 us (49%)
  starting transfers between devices  66 us (20%)
  waiting for transfers between devices  55.5 us (17%)
  other arithmetic  23.9 us (7%)
  local copies, waits for them, and re-layouts  15.6 us (5%)
    pallas_call x1, Pallas kernels, feed_high(): call(functools.partial(feed_high_kernel, source), LIMIT, 35, in_specs=[SC...  39 us
    pallas_call x1, Pallas kernels, feed_zero(): call(functools.partial(feed_zero_kernel, source), LIMIT, 28, in_specs=[SC...  31 us
    ppermute x42, starting transfers between devices, swap(): return lax.ppermute(value, AXES, [(i, i ^ bit) for i in range(total)])  30.7 us
    pallas_call x1, Pallas kernels, feed_mid(): call(functools.partial(feed_mid_kernel, source), LIMIT, 22, in_specs=[SCA...  28.3 us
    pallas_call x2, Pallas kernels, attend_backward(): call(functools.partial(attend_back_last_kernel, first_pair, pairs, own),...  25.5 us
    ppermute x12, waiting for transfers between devices, shift(): lax.ppermute(value, AXES, [(i, (i + by * self.fsdp) % total) for i in ran...  25 us
    ppermute x42, waiting for transfers between devices, swap(): return lax.ppermute(value, AXES, [(i, i ^ bit) for i in range(total)])  24.6 us
    ppermute x12, starting transfers between devices, shift(): lax.ppermute(value, AXES, [(i, (i + by * self.fsdp) % total) for i in ran...  23.3 us
  transfers between devices with their start and end apart: 62, of which 25 were waited for; matrix products, arithmetic and copies ran while one was open for 5% of the time, Pallas kernels for 38%

profile of v3, /device:TPU:0, one launch (start us, length us, event | category | flops | bytes accessed | tf_op | source)
XLA Modules:
  0.0 323.9 jit_solution(9468775103650901036)
XLA Ops:
  6.3 2.7 collective-permute-start.1
  9.0 2.6 collective-permute-start.2
  13.0 3.1 collective-permute-done.1
  16.1 6.5 %collective-permute-done.2 = bf16[48,1664]{1,0:T(8,128)(2,1)S(1)} collective-permute-done((bf16[48,1664]{1,0:T(8,128)(2,1)S(1)}, bf16[48,1664]{1,0:T(8,128)(2,1)S(1)}, u32[]{:S(2)}, u32[]{:S(2)}) %collective-permute-start.2) | collective-permute-done | bytes 159776 | tf_op jit(solution)/shard_map/ppermute | solution.py:978
  23.5 1.5 collective-permute-start.5
  25.0 1.5 collective-permute-start.6
  26.6 4.0 %collective-permute-start.7 = (bf16[48,1536]{1,0:T(8,128)(2,1)S(1)}, bf16[48,1536]{1,0:T(8,128)(2,1)S(1)}, u32[]{:S(2)}, u32[]{:S(2)}) collective-permute-start(bf16[48,1536]{1,0:T(8,128)(2,1)S(1)} %get-tuple-element.366), channel_id=1, source_target_pairs={{0,8},{1,9},{2,10},{3,11},{4,12},{5,13},{6,14},{7,15},{8,16},{9,17... | collective-permute-start | bytes 442376 | tf_op jit(solution)/shard_map/ppermute | solution.py:978
  30.5 1.6 collective-permute-start.8
  33.0 3.5 %collective-permute-done.7 = bf16[48,1536]{1,0:T(8,128)(2,1)S(1)} collective-permute-done((bf16[48,1536]{1,0:T(8,128)(2,1)S(1)}, bf16[48,1536]{1,0:T(8,128)(2,1)S(1)}, u32[]{:S(2)}, u32[]{:S(2)}) %collective-permute-start.7) | collective-permute-done | bytes 147488 | tf_op jit(solution)/shard_map/ppermute | solution.py:978
  36.4 4.6 %collective-permute-done.8 = bf16[48,1536]{1,0:T(8,128)(2,1)S(1)} collective-permute-done((bf16[48,1536]{1,0:T(8,128)(2,1)S(1)}, bf16[48,1536]{1,0:T(8,128)(2,1)S(1)}, u32[]{:S(2)}, u32[]{:S(2)}) %collective-permute-start.8) | collective-permute-done | bytes 147488 | tf_op jit(solution)/shard_map/ppermute | solution.py:978
  42.3 1.6 collective-permute-start.10
  45.5 4.0 %collective-permute-start.12 = (bf16[48,1536]{1,0:T(8,128)(2,1)S(1)}, bf16[48,1536]{1,0:T(8,128)(2,1)S(1)}, u32[]{:S(2)}, u32[]{:S(2)}) collective-permute-start(bf16[48,1536]{1,0:T(8,128)(2,1)S(1)} %get-tuple-element.365), channel_id=1, source_target_pairs={{0,8},{1,9},{2,10},{3,11},{4,12},{5,13},{6,14},{7,15},{8,16},{9,17... | collective-permute-start | bytes 442376 | tf_op jit(solution)/shard_map/ppermute | solution.py:978
  51.8 3.0 collective-permute-done.12
  54.8 4.3 %collective-permute-done.13 = bf16[48,1536]{1,0:T(8,128)(2,1)S(1)} collective-permute-done((bf16[48,1536]{1,0:T(8,128)(2,1)S(1)}, bf16[48,1536]{1,0:T(8,128)(2,1)S(1)}, u32[]{:S(2)}, u32[]{:S(2)}) %collective-permute-start.13) | collective-permute-done | bytes 147488 | tf_op jit(solution)/shard_map/ppermute | solution.py:978
  59.4 1.6 collective-permute-start.20
  67.2 5.5 %place_rows.1 = (bf16[768,1536]{1,0:T(8,128)(2,1)}, bf16[768,1536]{1,0:T(8,128)(2,1)}, f32[8,768]{1,0:T(8,128)}, f32[4,768]{1,0:T(4,128)}) custom-call(s32[17]{0:T(128)} %stack.119.table, bf16[4,48,1664]{2,1,0:T(8,128)(2,1)} %pad_maximum_fusion.1.refs_0_, bf16[4,48,1664]{2,1,0:T(8,128)(2,1)} %collective-permute-done.5.refs_1_, ...), custom_call_target="tpu_custom_call" | custom-call | bytes 16500000 | tf_op jit(solution)/shard_map/place_rows/pallas_call | solution.py:1189
  72.7 9.6 %attend.1 = (bf16[512,768]{1,0:T(8,128)(2,1)}, bf16[512,768]{1,0:T(8,128)(2,1)}, bf16[512,768]{1,0:T(8,128)(2,1)}, bf16[512,768]{1,0:T(8,128)(2,1)}, bf16[12,4,128,384]{3,2,1,0:T(8,128)(2,1)}) custom-call(bf16[512,768]{1,0:T(8,128)(2,1)} %x.3, bf16[768,1536]{1,0:T(8,128)(2,1)} %get-tuple-element.195.wq.wk, bf16[768,1536]{1,0:T(8,128)(2,1)} %get-tuple-element.195.wq.wk, ...), custom_call_target="tpu_custom_call" | custom-call | bytes 31350000 | tf_op jit(solution)/shard_map/attend/pallas_call | solution.py:115
  82.3 4.2 %collective-permute-done.20.refs_1_ = bf16[4,48,3072]{2,1,0:T(8,128)(2,1)S(1)} collective-permute-done((bf16[4,48,3072]{2,1,0:T(8,128)(2,1)S(1)}, bf16[4,48,3072]{2,1,0:T(8,128)(2,1)S(1)}, u32[]{:S(2)}, u32[]{:S(2)}) %collective-permute-start.20) | collective-permute-done | bytes 1179680 | tf_op jit(solution)/shard_map/ppermute | solution.py:974
  89.9 1.6 collective-permute-start.22
  92.0 9.8 %first_norm.1 = (bf16[4,512,768]{2,1,0:T(8,128)(2,1)}, f32[4,512,1]{2,1,0:T(8,128)}, bf16[4,512,768]{2,1,0:T(8,128)(2,1)}, bf16[4,768,512]{2,1,0:T(8,128)(2,1)},...) custom-call(bf16[512,768]{1,0:T(8,128)(2,1)} %x.3, bf16[512,768]{1,0:T(8,128)(2,1)} %get-tuple-element.204.att_a.att_b.att_h, ...), custom_call_target="tpu_custom_call" | custom-call | bytes 32010000 | tf_op jit(solution)/shard_map/first_norm/pallas_call | solution.py:186
  101.8 4.1 %collective-permute-done.22.refs_3_ = bf16[2,48,3072]{2,1,0:T(8,128)(2,1)} collective-permute-done((bf16[2,48,3072]{2,1,0:T(8,128)(2,1)}, bf16[2,48,3072]{2,1,0:T(8,128)(2,1)}, u32[]{:S(2)}, u32[]{:S(2)}) %collective-permute-start.22) | collective-permute-done | bytes 589856 | tf_op jit(solution)/shard_map/ppermute | solution.py:974
  111.1 39.0 %feed_high.1 = (bf16[4,512,768]{2,1,0:T(8,128)(2,1)}, bf16[4,512,768]{2,1,0:T(8,128)(2,1)}, bf16[2,512,768]{2,1,0:T(8,128)(2,1)}, bf16[2,512,768]{2,1,0:T(8,128)...) custom-call(s32[17]{0:T(128)} %stack.119.table, ...), custom_call_target="tpu_custom_call" | custom-call | bytes 115500000 | tf_op jit(solution)/shard_map/feed_high/pallas_call | solution.py:417
  150.5 4.5 %collective-permute-done.29 = bf16[768,1536]{1,0:T(8,128)(2,1)S(1)} collective-permute-done((bf16[768,1536]{1,0:T(8,128)(2,1)}, bf16[768,1536]{1,0:T(8,128)(2,1)S(1)}, u32[]{:S(2)}, u32[]{:S(2)}) %collective-permute-start.29) | collective-permute-done | bytes 2359328 | tf_op jit(solution)/shard_map/ppermute | solution.py:974
  155.0 2.7 fusion.6
  159.6 1.6 collective-permute-start.32
  161.2 28.3 %feed_mid.1 = (bf16[4,512,768]{2,1,0:T(8,128)(2,1)}, bf16[4,512,768]{2,1,0:T(8,128)(2,1)}, bf16[4,512,768]{2,1,0:T(8,128)(2,1)}, bf16[4,512,768]{2,1,0:T(8,128)(...) custom-call(s32[17]{0:T(128)} %stack.119.table, ...), custom_call_target="tpu_custom_call", output_to_operand_aliasing={{3}: (10, {}), {4}: (11, {}), {0}: (22, {}), {1}: (23, {}),... | custom-call | bytes 72600000 | tf_op jit(solution)/shard_map/feed_mid/pallas_call | solution.py:552
  189.7 2.0 fusion.1
  192.8 1.4 fusion.18
  196.1 1.6 collective-permute-start.36
  197.7 2.7 collective-permute-start.37
  200.4 31.0 %feed_zero.1 = (bf16[768,768]{1,0:T(8,128)(2,1)}, bf16[768,768]{1,0:T(8,128)(2,1)}, f32[4,512,768]{2,1,0:T(8,128)}, bf16[4,512,768]{2,1,0:T(8,128)(2,1)}, bf16[7...) custom-call(s32[17]{0:T(128)} %stack.119.table, f32[8,768]{1,0:T(8,128)} %get-tuple-element.194.vec, ...), custom_call_target="tpu_custom_call" | custom-call | bytes 92400000 | tf_op jit(solution)/shard_map/feed_zero/pallas_call | solution.py:703
  232.2 1.4 fusion.12
  238.3 1.6 collective-permute-start.41
  240.1 3.7 %collective-permute-start.43 = (bf16[48,1536]{1,0:T(8,128)(2,1)}, bf16[48,1536]{1,0:T(8,128)(2,1)S(1)}, u32[]{:S(2)}, u32[]{:S(2)}) collective-permute-start(bf16[48,1536]{1,0:T(8,128)(2,1)} %fusion.30), channel_id=1, source_target_pairs={{0,8},{1,9},{2,10},{3,11},{4,12},{5,13},{6,14},{7,15},{8,0},{9,1},... | collective-permute-start | bytes 442376 | tf_op jit(solution)/shard_map/ppermute | solution.py:982
  243.8 14.3 %attend_backward.2 = (bf16[4,512,384]{2,1,0:T(8,128)(2,1)}, bf16[4,512,384]{2,1,0:T(8,128)(2,1)}, bf16[4,512,384]{2,1,0:T(8,128)(2,1)}, bf16[768,768]{1,0:T(8,12...) custom-call(s32[1]{0:T(128)} %bitcast.16.refs_0_, bf16[768,512]{1,0:T(8,128)(2,1)} %get-tuple-element.250.refs_1_, ...), custom_call_target="tpu_custom_call" | custom-call | bytes 39600000 | tf_op jit(solution)/shard_map/attend_backward/pallas_call | solution.py:892
  264.7 1.6 collective-permute-start.47
  267.3 11.2 %attend_backward.3 = (bf16[4,512,384]{2,1,0:T(8,128)(2,1)}, bf16[4,512,384]{2,1,0:T(8,128)(2,1)}, bf16[4,512,384]{2,1,0:T(8,128)(2,1)}, bf16[768,896]{1,0:T(8,12...) custom-call(s32[1]{0:T(128)} %bitcast.16.refs_0_, bf16[768,512]{1,0:T(8,128)(2,1)} %get-tuple-element.250.refs_1_, ...), custom_call_target="tpu_custom_call" | custom-call | bytes 39600000 | tf_op jit(solution)/shard_map/attend_backward/pallas_call | solution.py:892
  280.9 1.4 fusion.8
  283.0 2.4 fusion.15
  286.0 1.5 collective-permute-start.52
  287.5 1.4 collective-permute-start.53
  288.9 1.7 collective-permute-start.54
  290.6 2.0 collective-permute-start.55
  292.7 12.4 %input_grads.1 = f32[4,512,768]{2,1,0:T(8,128)} custom-call(f32[4,512,768]{2,1,0:T(8,128)} %get-tuple-element.304.first_g, bf16[4,512,384]{2,1,0:T(8,128)(2,1)} %get-tuple-element.305.dq_a, bf16[4,512,384]{2,1,0:T(8,128)(2,1)} %get-tuple-element.306.dk_a, bf16[4,512,384]{2,1,0:T(8,128)(2,1)} %get-tuple-element.307.dv_a, ...), custom_call_target="tpu_custom_call" | custom-call | bytes 26400000 | tf_op jit(solution)/shard_map/input_grads/pallas_call | solution.py:946
  306.7 2.4 collective-permute-start.57
  309.2 1.4 collective-permute-start.58
  312.1 5.8 %collective-permute-done.59 = bf16[48,768]{1,0:T(8,128)(2,1)S(1)} collective-permute-done((bf16[48,768]{1,0:T(8,128)(2,1)S(1)}, bf16[48,768]{1,0:T(8,128)(2,1)S(1)}, u32[]{:S(2)}, u32[]{:S(2)}) %collective-permute-start.59) | collective-permute-done | bytes 73760 | tf_op jit(solution)/shard_map/ppermute | solution.py:982
  318.1 1.4 collective-permute-done.61
  (208 shorter events, 58.9 us)
Async XLA Ops:
  5.9 7.1 %collective-permute-start.4 = (bf16[24,3072]{1,0:T(8,128)(2,1)S(1)}, bf16[24,3072]{1,0:T(8,128)(2,1)S(1)}, u32[]{:S(2)}, u32[]{:S(2)}) collective-permute-start(bf16[24,3072]{1,0:T(8,128)(2,1)S(1)} %get-tuple-element.368), channel_id=1, source_target_pairs={{0,1},{1,0},{2,3},{3,2},{4,5},{5,4},{6,7},{7,6},{8,9},{9,8},{10,11... | collective-permute-start | bytes 442376 | tf_op jit(solution)/shard_map/ppermute | solution.py:974
  6.3 9.8 %collective-permute-start.1 = (bf16[48,1664]{1,0:T(8,128)(2,1)S(1)}, bf16[48,1664]{1,0:T(8,128)(2,1)S(1)}, u32[]{:S(2)}, u32[]{:S(2)}) collective-permute-start(bf16[48,1664]{1,0:T(8,128)(2,1)S(1)} %maximum_select_fusion.1), channel_id=1, source_target_pairs={{0,8},{1,9},{2,10},{3,11},{4,12},{5,13},{6,14},{7,15},{8,16},{9,17... | collective-permute-start | bytes 479240 | tf_op jit(solution)/shard_map/ppermute | solution.py:978
  9.0 13.6 %collective-permute-start.2 = (bf16[48,1664]{1,0:T(8,128)(2,1)S(1)}, bf16[48,1664]{1,0:T(8,128)(2,1)S(1)}, u32[]{:S(2)}, u32[]{:S(2)}) collective-permute-start(bf16[48,1664]{1,0:T(8,128)(2,1)S(1)} %maximum_select_fusion.1), channel_id=1, source_target_pairs={{0,16},{1,17},{2,18},{3,19},{4,20},{5,21},{6,22},{7,23},{8,24},{9,... | collective-permute-start | bytes 479240 | tf_op jit(solution)/shard_map/ppermute | solution.py:978
  11.6 11.0 %collective-permute-start.3 = (bf16[48,1664]{1,0:T(8,128)(2,1)S(1)}, bf16[48,1664]{1,0:T(8,128)(2,1)S(1)}, u32[]{:S(2)}, u32[]{:S(2)}) collective-permute-start(bf16[48,1664]{1,0:T(8,128)(2,1)S(1)} %maximum_select_fusion.1), channel_id=1, source_target_pairs={{0,24},{1,25},{2,26},{3,27},{4,28},{5,29},{6,30},{7,31},{8,0},{9,1... | collective-permute-start | bytes 479240 | tf_op jit(solution)/shard_map/ppermute | solution.py:978
  23.5 17.5 %collective-permute-start.5 = (bf16[4,48,1664]{2,1,0:T(8,128)(2,1)}, bf16[4,48,1664]{2,1,0:T(8,128)(2,1)}, u32[]{:S(2)}, u32[]{:S(2)}) collective-permute-start(bf16[4,48,1664]{2,1,0:T(8,128)(2,1)} %pad_maximum_fusion.1.refs_0_), channel_id=1, source_target_pairs={{0,2},{1,3},{2,0},{3,1},{4,6},{5,7},{6,4},{7,5},{8,10},{9,11},{10,... | collective-permute-start | bytes 1916936 | tf_op jit(solution)/shard_map/ppermute | solution.py:974
  25.0 16.3 %collective-permute-start.6 = (bf16[4,48,1664]{2,1,0:T(8,128)(2,1)}, bf16[4,48,1664]{2,1,0:T(8,128)(2,1)}, u32[]{:S(2)}, u32[]{:S(2)}) collective-permute-start(bf16[4,48,1664]{2,1,0:T(8,128)(2,1)} %pad_maximum_fusion.1.refs_0_), channel_id=1, source_target_pairs={{0,4},{1,5},{2,6},{3,7},{4,0},{5,1},{6,2},{7,3},{8,12},{9,13},{10,... | collective-permute-start | bytes 1916936 | tf_op jit(solution)/shard_map/ppermute | solution.py:974
  26.6 9.9 %collective-permute-start.7 = (bf16[48,1536]{1,0:T(8,128)(2,1)S(1)}, bf16[48,1536]{1,0:T(8,128)(2,1)S(1)}, u32[]{:S(2)}, u32[]{:S(2)}) collective-permute-start(bf16[48,1536]{1,0:T(8,128)(2,1)S(1)} %get-tuple-element.366), channel_id=1, source_target_pairs={{0,8},{1,9},{2,10},{3,11},{4,12},{5,13},{6,14},{7,15},{8,16},{9,17... | collective-permute-start | bytes 442376 | tf_op jit(solution)/shard_map/ppermute | solution.py:978
  30.5 10.5 %collective-permute-start.8 = (bf16[48,1536]{1,0:T(8,128)(2,1)S(1)}, bf16[48,1536]{1,0:T(8,128)(2,1)S(1)}, u32[]{:S(2)}, u32[]{:S(2)}) collective-permute-start(bf16[48,1536]{1,0:T(8,128)(2,1)S(1)} %get-tuple-element.366), channel_id=1, source_target_pairs={{0,16},{1,17},{2,18},{3,19},{4,20},{5,21},{6,22},{7,23},{8,24},{9,... | collective-permute-start | bytes 442376 | tf_op jit(solution)/shard_map/ppermute | solution.py:978
  32.2 8.9 %collective-permute-start.9 = (bf16[48,1536]{1,0:T(8,128)(2,1)S(1)}, bf16[48,1536]{1,0:T(8,128)(2,1)S(1)}, u32[]{:S(2)}, u32[]{:S(2)}) collective-permute-start(bf16[48,1536]{1,0:T(8,128)(2,1)S(1)} %get-tuple-element.366), channel_id=1, source_target_pairs={{0,24},{1,25},{2,26},{3,27},{4,28},{5,29},{6,30},{7,31},{8,0},{9,1... | collective-permute-start | bytes 442376 | tf_op jit(solution)/shard_map/ppermute | solution.py:978
  42.3 16.9 %collective-permute-start.10 = (bf16[2,48,1664]{2,1,0:T(8,128)(2,1)S(1)}, bf16[2,48,1664]{2,1,0:T(8,128)(2,1)S(1)}, u32[]{:S(2)}, u32[]{:S(2)}) collective-permute-start(bf16[2,48,1664]{2,1,0:T(8,128)(2,1)S(1)} %slice.112), channel_id=1, source_target_pairs={{0,4},{1,5},{2,6},{3,7},{4,0},{5,1},{6,2},{7,3},{8,12},{9,13},{10,... | collective-permute-start | bytes 958472 | tf_op jit(solution)/shard_map/ppermute | solution.py:974
  44.9 14.3 %collective-permute-start.11 = (bf16[2,48,1664]{2,1,0:T(8,128)(2,1)S(1)}, bf16[2,48,1664]{2,1,0:T(8,128)(2,1)S(1)}, u32[]{:S(2)}, u32[]{:S(2)}) collective-permute-start(bf16[2,48,1664]{2,1,0:T(8,128)(2,1)S(1)} %slice.113), channel_id=1, source_target_pairs={{0,2},{1,3},{2,0},{3,1},{4,6},{5,7},{6,4},{7,5},{8,10},{9,11},{10,... | collective-permute-start | bytes 958472 | tf_op jit(solution)/shard_map/ppermute | solution.py:974
  45.5 9.3 %collective-permute-start.12 = (bf16[48,1536]{1,0:T(8,128)(2,1)S(1)}, bf16[48,1536]{1,0:T(8,128)(2,1)S(1)}, u32[]{:S(2)}, u32[]{:S(2)}) collective-permute-start(bf16[48,1536]{1,0:T(8,128)(2,1)S(1)} %get-tuple-element.365), channel_id=1, source_target_pairs={{0,8},{1,9},{2,10},{3,11},{4,12},{5,13},{6,14},{7,15},{8,16},{9,17... | collective-permute-start | bytes 442376 | tf_op jit(solution)/shard_map/ppermute | solution.py:978
  49.5 9.7 %collective-permute-start.13 = (bf16[48,1536]{1,0:T(8,128)(2,1)S(1)}, bf16[48,1536]{1,0:T(8,128)(2,1)S(1)}, u32[]{:S(2)}, u32[]{:S(2)}) collective-permute-start(bf16[48,1536]{1,0:T(8,128)(2,1)S(1)} %get-tuple-element.365), channel_id=1, source_target_pairs={{0,16},{1,17},{2,18},{3,19},{4,20},{5,21},{6,22},{7,23},{8,24},{9,... | collective-permute-start | bytes 442376 | tf_op jit(solution)/shard_map/ppermute | solution.py:978
  50.6 8.5 %collective-permute-start.14 = (bf16[48,1536]{1,0:T(8,128)(2,1)S(1)}, bf16[48,1536]{1,0:T(8,128)(2,1)S(1)}, u32[]{:S(2)}, u32[]{:S(2)}) collective-permute-start(bf16[48,1536]{1,0:T(8,128)(2,1)S(1)} %get-tuple-element.365), channel_id=1, source_target_pairs={{0,24},{1,25},{2,26},{3,27},{4,28},{5,29},{6,30},{7,31},{8,0},{9,1... | collective-permute-start | bytes 442376 | tf_op jit(solution)/shard_map/ppermute | solution.py:978
  59.4 27.1 %collective-permute-start.20 = (bf16[4,48,3072]{2,1,0:T(8,128)(2,1)S(1)}, bf16[4,48,3072]{2,1,0:T(8,128)(2,1)S(1)}, u32[]{:S(2)}, u32[]{:S(2)}) collective-permute-start(bf16[4,48,3072]{2,1,0:T(8,128)(2,1)S(1)} %pad_maximum_fusion.refs_0_), channel_id=1, source_target_pairs={{0,2},{1,3},{2,0},{3,1},{4,6},{5,7},{6,4},{7,5},{8,10},{9,11},{10,... | collective-permute-start | bytes 3538952 | tf_op jit(solution)/shard_map/ppermute | solution.py:974
  61.0 26.6 %collective-permute-start.21 = (bf16[4,48,3072]{2,1,0:T(8,128)(2,1)S(1)}, bf16[4,48,3072]{2,1,0:T(8,128)(2,1)S(1)}, u32[]{:S(2)}, u32[]{:S(2)}) collective-permute-start(bf16[4,48,3072]{2,1,0:T(8,128)(2,1)S(1)} %pad_maximum_fusion.refs_0_), channel_id=1, source_target_pairs={{0,4},{1,5},{2,6},{3,7},{4,0},{5,1},{6,2},{7,3},{8,12},{9,13},{10,... | collective-permute-start | bytes 3538952 | tf_op jit(solution)/shard_map/ppermute | solution.py:974
  87.6 19.6 %collective-permute-start.24 = (bf16[4,48,3072]{2,1,0:T(8,128)(2,1)S(1)}, bf16[4,48,3072]{2,1,0:T(8,128)(2,1)}, u32[]{:S(2)}, u32[]{:S(2)}) collective-permute-start(bf16[4,48,3072]{2,1,0:T(8,128)(2,1)S(1)} %pad_maximum_fusion.refs_0_), channel_id=1, source_target_pairs={{0,1},{1,0},{2,3},{3,2},{4,5},{5,4},{6,7},{7,6},{8,9},{9,8},{10,11... | collective-permute-start | bytes 3538952 | tf_op jit(solution)/shard_map/ppermute | solution.py:974
  87.6 19.6 %collective-permute-start.25 = (bf16[4,48,3072]{2,1,0:T(8,128)(2,1)S(1)}, bf16[4,48,3072]{2,1,0:T(8,128)(2,1)}, u32[]{:S(2)}, u32[]{:S(2)}) collective-permute-start(bf16[4,48,3072]{2,1,0:T(8,128)(2,1)S(1)} %collective-permute-done.20.refs_1_), channel_id=1, source_target_pairs={{0,1},{1,0},{2,3},{3,2},{4,5},{5,4},{6,7},{7,6},{8,9},{9,8},{10,11... | collective-permute-start | bytes 3538952 | tf_op jit(solution)/shard_map/ppermute | solution.py:974
  88.1 19.1 %collective-permute-start.26 = (bf16[4,48,3072]{2,1,0:T(8,128)(2,1)S(1)}, bf16[4,48,3072]{2,1,0:T(8,128)(2,1)}, u32[]{:S(2)}, u32[]{:S(2)}) collective-permute-start(bf16[4,48,3072]{2,1,0:T(8,128)(2,1)S(1)} %collective-permute-done.21.refs_2_), channel_id=1, source_target_pairs={{0,1},{1,0},{2,3},{3,2},{4,5},{5,4},{6,7},{7,6},{8,9},{9,8},{10,11... | collective-permute-start | bytes 3538952 | tf_op jit(solution)/shard_map/ppermute | solution.py:974
  89.9 16.0 %collective-permute-start.22 = (bf16[2,48,3072]{2,1,0:T(8,128)(2,1)}, bf16[2,48,3072]{2,1,0:T(8,128)(2,1)}, u32[]{:S(2)}, u32[]{:S(2)}) collective-permute-start(bf16[2,48,3072]{2,1,0:T(8,128)(2,1)} %slice.115), channel_id=1, source_target_pairs={{0,4},{1,5},{2,6},{3,7},{4,0},{5,1},{6,2},{7,3},{8,12},{9,13},{10,... | collective-permute-start | bytes 1769480 | tf_op jit(solution)/shard_map/ppermute | solution.py:974
  91.5 15.7 %collective-permute-start.23 = (bf16[2,48,3072]{2,1,0:T(8,128)(2,1)}, bf16[2,48,3072]{2,1,0:T(8,128)(2,1)}, u32[]{:S(2)}, u32[]{:S(2)}) collective-permute-start(bf16[2,48,3072]{2,1,0:T(8,128)(2,1)} %slice.116), channel_id=1, source_target_pairs={{0,2},{1,3},{2,0},{3,1},{4,6},{5,7},{6,4},{7,5},{8,10},{9,11},{10,... | collective-permute-start | bytes 1769480 | tf_op jit(solution)/shard_map/ppermute | solution.py:974
  157.7 31.8 %collective-permute-start.30 = (bf16[4,48,1536]{2,1,0:T(8,128)(2,1)}, bf16[4,48,1536]{2,1,0:T(8,128)(2,1)}, u32[]{:S(2)}, u32[]{:S(2)}) collective-permute-start(bf16[4,48,1536]{2,1,0:T(8,128)(2,1)} %get-tuple-element.237), channel_id=1, source_target_pairs={{0,6},{1,7},{2,4},{3,5},{4,2},{5,3},{6,0},{7,1},{8,14},{9,15},{10,... | collective-permute-start | bytes 1769480 | tf_op jit(solution)/shard_map/ppermute | solution.py:974
  158.3 31.3 %collective-permute-start.31 = (bf16[4,48,1536]{2,1,0:T(8,128)(2,1)S(1)}, bf16[4,48,1536]{2,1,0:T(8,128)(2,1)}, u32[]{:S(2)}, u32[]{:S(2)}) collective-permute-start(bf16[4,48,1536]{2,1,0:T(8,128)(2,1)S(1)} %get-tuple-element.238), channel_id=1, source_target_pairs={{0,2},{1,3},{2,0},{3,1},{4,6},{5,7},{6,4},{7,5},{8,10},{9,11},{10,... | collective-permute-start | bytes 1769480 | tf_op jit(solution)/shard_map/ppermute | solution.py:974
  159.6 29.9 %collective-permute-start.32 = (bf16[4,48,1536]{2,1,0:T(8,128)(2,1)S(1)}, bf16[4,48,1536]{2,1,0:T(8,128)(2,1)}, u32[]{:S(2)}, u32[]{:S(2)}) collective-permute-start(bf16[4,48,1536]{2,1,0:T(8,128)(2,1)S(1)} %get-tuple-element.239), channel_id=1, source_target_pairs={{0,4},{1,5},{2,6},{3,7},{4,0},{5,1},{6,2},{7,3},{8,12},{9,13},{10,... | collective-permute-start | bytes 1769480 | tf_op jit(solution)/shard_map/ppermute | solution.py:974
  194.2 37.3 %collective-permute-start.34 = (bf16[4,48,768]{2,1,0:T(8,128)(2,1)S(1)}, bf16[4,48,768]{2,1,0:T(8,128)(2,1)S(1)}, u32[]{:S(2)}, u32[]{:S(2)}) collective-permute-start(bf16[4,48,768]{2,1,0:T(8,128)(2,1)S(1)} %get-tuple-element.258), channel_id=1, source_target_pairs={{0,6},{1,7},{2,4},{3,5},{4,2},{5,3},{6,0},{7,1},{8,14},{9,15},{10,... | collective-permute-start | bytes 884744 | tf_op jit(solution)/shard_map/ppermute | solution.py:974
  194.8 36.7 %collective-permute-start.35 = (bf16[4,48,768]{2,1,0:T(8,128)(2,1)S(1)}, bf16[4,48,768]{2,1,0:T(8,128)(2,1)S(1)}, u32[]{:S(2)}, u32[]{:S(2)}) collective-permute-start(bf16[4,48,768]{2,1,0:T(8,128)(2,1)S(1)} %get-tuple-element.259), channel_id=1, source_target_pairs={{0,2},{1,3},{2,0},{3,1},{4,6},{5,7},{6,4},{7,5},{8,10},{9,11},{10,... | collective-permute-start | bytes 884744 | tf_op jit(solution)/shard_map/ppermute | solution.py:974
  196.1 35.3 %collective-permute-start.36 = (bf16[4,48,768]{2,1,0:T(8,128)(2,1)S(1)}, bf16[4,48,768]{2,1,0:T(8,128)(2,1)}, u32[]{:S(2)}, u32[]{:S(2)}) collective-permute-start(bf16[4,48,768]{2,1,0:T(8,128)(2,1)S(1)} %get-tuple-element.260), channel_id=1, source_target_pairs={{0,4},{1,5},{2,6},{3,7},{4,0},{5,1},{6,2},{7,3},{8,12},{9,13},{10,... | collective-permute-start | bytes 884744 | tf_op jit(solution)/shard_map/ppermute | solution.py:974
  197.7 33.7 %collective-permute-start.37 = (bf16[2,48,1536]{2,1,0:T(8,128)(2,1)S(1)}, bf16[2,48,1536]{2,1,0:T(8,128)(2,1)S(1)}, u32[]{:S(2)}, u32[]{:S(2)}) collective-permute-start(bf16[2,48,1536]{2,1,0:T(8,128)(2,1)S(1)} %fusion.19), channel_id=1, source_target_pairs={{0,16},{1,17},{2,18},{3,19},{4,20},{5,21},{6,22},{7,23},{8,24},{9,... | collective-permute-start | bytes 884744 | tf_op jit(solution)/shard_map/ppermute | solution.py:982
  236.4 21.8 %collective-permute-start.39 = (bf16[4,48,768]{2,1,0:T(8,128)(2,1)}, bf16[4,48,768]{2,1,0:T(8,128)(2,1)S(1)}, u32[]{:S(2)}, u32[]{:S(2)}) collective-permute-start(bf16[4,48,768]{2,1,0:T(8,128)(2,1)} %get-tuple-element.271), channel_id=1, source_target_pairs={{0,6},{1,7},{2,4},{3,5},{4,2},{5,3},{6,0},{7,1},{8,14},{9,15},{10,... | collective-permute-start | bytes 884744 | tf_op jit(solution)/shard_map/ppermute | solution.py:974
  236.9 21.3 %collective-permute-start.40 = (bf16[4,48,768]{2,1,0:T(8,128)(2,1)S(1)}, bf16[4,48,768]{2,1,0:T(8,128)(2,1)S(1)}, u32[]{:S(2)}, u32[]{:S(2)}) collective-permute-start(bf16[4,48,768]{2,1,0:T(8,128)(2,1)S(1)} %get-tuple-element.272), channel_id=1, source_target_pairs={{0,2},{1,3},{2,0},{3,1},{4,6},{5,7},{6,4},{7,5},{8,10},{9,11},{10,... | collective-permute-start | bytes 884744 | tf_op jit(solution)/shard_map/ppermute | solution.py:974
  238.3 19.9 %collective-permute-start.41 = (bf16[4,48,768]{2,1,0:T(8,128)(2,1)S(1)}, bf16[4,48,768]{2,1,0:T(8,128)(2,1)S(1)}, u32[]{:S(2)}, u32[]{:S(2)}) collective-permute-start(bf16[4,48,768]{2,1,0:T(8,128)(2,1)S(1)} %get-tuple-element.273), channel_id=1, source_target_pairs={{0,4},{1,5},{2,6},{3,7},{4,0},{5,1},{6,2},{7,3},{8,12},{9,13},{10,... | collective-permute-start | bytes 884744 | tf_op jit(solution)/shard_map/ppermute | solution.py:974
  239.8 18.3 %collective-permute-start.42 = (bf16[2,48,768]{2,1,0:T(8,128)(2,1)}, bf16[2,48,768]{2,1,0:T(8,128)(2,1)}, u32[]{:S(2)}, u32[]{:S(2)}) collective-permute-start(bf16[2,48,768]{2,1,0:T(8,128)(2,1)} %fusion.29), channel_id=1, source_target_pairs={{0,16},{1,17},{2,18},{3,19},{4,20},{5,21},{6,22},{7,23},{8,24},{9,... | collective-permute-start | bytes 442376 | tf_op jit(solution)/shard_map/ppermute | solution.py:982
  240.1 18.1 %collective-permute-start.43 = (bf16[48,1536]{1,0:T(8,128)(2,1)}, bf16[48,1536]{1,0:T(8,128)(2,1)S(1)}, u32[]{:S(2)}, u32[]{:S(2)}) collective-permute-start(bf16[48,1536]{1,0:T(8,128)(2,1)} %fusion.30), channel_id=1, source_target_pairs={{0,8},{1,9},{2,10},{3,11},{4,12},{5,13},{6,14},{7,15},{8,0},{9,1},... | collective-permute-start | bytes 442376 | tf_op jit(solution)/shard_map/ppermute | solution.py:982
  262.7 15.8 %collective-permute-start.45 = (bf16[4,48,768]{2,1,0:T(8,128)(2,1)S(1)}, bf16[4,48,768]{2,1,0:T(8,128)(2,1)S(1)}, u32[]{:S(2)}, u32[]{:S(2)}) collective-permute-start(bf16[4,48,768]{2,1,0:T(8,128)(2,1)S(1)} %get-tuple-element.292), channel_id=1, source_target_pairs={{0,6},{1,7},{2,4},{3,5},{4,2},{5,3},{6,0},{7,1},{8,14},{9,15},{10,... | collective-permute-start | bytes 884744 | tf_op jit(solution)/shard_map/ppermute | solution.py:974
  263.3 15.2 %collective-permute-start.46 = (bf16[4,48,768]{2,1,0:T(8,128)(2,1)S(1)}, bf16[4,48,768]{2,1,0:T(8,128)(2,1)}, u32[]{:S(2)}, u32[]{:S(2)}) collective-permute-start(bf16[4,48,768]{2,1,0:T(8,128)(2,1)S(1)} %get-tuple-element.293), channel_id=1, source_target_pairs={{0,2},{1,3},{2,0},{3,1},{4,6},{5,7},{6,4},{7,5},{8,10},{9,11},{10,... | collective-permute-start | bytes 884744 | tf_op jit(solution)/shard_map/ppermute | solution.py:974
  264.7 14.8 %collective-permute-start.47 = (bf16[4,48,768]{2,1,0:T(8,128)(2,1)S(1)}, bf16[4,48,768]{2,1,0:T(8,128)(2,1)}, u32[]{:S(2)}, u32[]{:S(2)}) collective-permute-start(bf16[4,48,768]{2,1,0:T(8,128)(2,1)S(1)} %get-tuple-element.294), channel_id=1, source_target_pairs={{0,4},{1,5},{2,6},{3,7},{4,0},{5,1},{6,2},{7,3},{8,12},{9,13},{10,... | collective-permute-start | bytes 884744 | tf_op jit(solution)/shard_map/ppermute | solution.py:974
  266.3 12.3 %collective-permute-start.48 = (bf16[2,48,768]{2,1,0:T(8,128)(2,1)S(1)}, bf16[2,48,768]{2,1,0:T(8,128)(2,1)S(1)}, u32[]{:S(2)}, u32[]{:S(2)}) collective-permute-start(bf16[2,48,768]{2,1,0:T(8,128)(2,1)S(1)} %fusion.31), channel_id=1, source_target_pairs={{0,16},{1,17},{2,18},{3,19},{4,20},{5,21},{6,22},{7,23},{8,24},{9,... | collective-permute-start | bytes 442376 | tf_op jit(solution)/shard_map/ppermute | solution.py:982
  266.3 12.2 %collective-permute-start.49 = (bf16[48,768]{1,0:T(8,128)(2,1)S(1)}, bf16[48,768]{1,0:T(8,128)(2,1)S(1)}, u32[]{:S(2)}, u32[]{:S(2)}) collective-permute-start(bf16[48,768]{1,0:T(8,128)(2,1)S(1)} %fusion.33), channel_id=1, source_target_pairs={{0,8},{1,9},{2,10},{3,11},{4,12},{5,13},{6,14},{7,15},{8,0},{9,1},... | collective-permute-start | bytes 221192 | tf_op jit(solution)/shard_map/ppermute | solution.py:982
  285.4 19.7 %collective-permute-start.51 = (bf16[4,48,896]{2,1,0:T(8,128)(2,1)}, bf16[4,48,896]{2,1,0:T(8,128)(2,1)S(1)}, u32[]{:S(2)}, u32[]{:S(2)}) collective-permute-start(bf16[4,48,896]{2,1,0:T(8,128)(2,1)} %get-tuple-element.311), channel_id=1, source_target_pairs={{0,6},{1,7},{2,4},{3,5},{4,2},{5,3},{6,0},{7,1},{8,14},{9,15},{10,... | collective-permute-start | bytes 1032200 | tf_op jit(solution)/shard_map/ppermute | solution.py:974
  286.0 19.1 %collective-permute-start.52 = (bf16[4,48,896]{2,1,0:T(8,128)(2,1)}, bf16[4,48,896]{2,1,0:T(8,128)(2,1)S(1)}, u32[]{:S(2)}, u32[]{:S(2)}) collective-permute-start(bf16[4,48,896]{2,1,0:T(8,128)(2,1)} %get-tuple-element.312), channel_id=1, source_target_pairs={{0,2},{1,3},{2,0},{3,1},{4,6},{5,7},{6,4},{7,5},{8,10},{9,11},{10,... | collective-permute-start | bytes 1032200 | tf_op jit(solution)/shard_map/ppermute | solution.py:974
  287.5 17.7 %collective-permute-start.53 = (bf16[4,48,896]{2,1,0:T(8,128)(2,1)}, bf16[4,48,896]{2,1,0:T(8,128)(2,1)S(1)}, u32[]{:S(2)}, u32[]{:S(2)}) collective-permute-start(bf16[4,48,896]{2,1,0:T(8,128)(2,1)} %get-tuple-element.313), channel_id=1, source_target_pairs={{0,4},{1,5},{2,6},{3,7},{4,0},{5,1},{6,2},{7,3},{8,12},{9,13},{10,... | collective-permute-start | bytes 1032200 | tf_op jit(solution)/shard_map/ppermute | solution.py:974
  288.9 16.2 %collective-permute-start.54 = (bf16[2,48,768]{2,1,0:T(8,128)(2,1)S(1)}, bf16[2,48,768]{2,1,0:T(8,128)(2,1)S(1)}, u32[]{:S(2)}, u32[]{:S(2)}) collective-permute-start(bf16[2,48,768]{2,1,0:T(8,128)(2,1)S(1)} %fusion.32), channel_id=1, source_target_pairs={{0,16},{1,17},{2,18},{3,19},{4,20},{5,21},{6,22},{7,23},{8,24},{9,... | collective-permute-start | bytes 442376 | tf_op jit(solution)/shard_map/ppermute | solution.py:982
  290.6 14.5 %collective-permute-start.55 = (bf16[48,768]{1,0:T(8,128)(2,1)}, bf16[48,768]{1,0:T(8,128)(2,1)S(1)}, u32[]{:S(2)}, u32[]{:S(2)}) collective-permute-start(bf16[48,768]{1,0:T(8,128)(2,1)} %fusion.34), channel_id=1, source_target_pairs={{0,8},{1,9},{2,10},{3,11},{4,12},{5,13},{6,14},{7,15},{8,0},{9,1},... | collective-permute-start | bytes 221192 | tf_op jit(solution)/shard_map/ppermute | solution.py:982
  305.3 5.9 %collective-permute-start.60 = (f32[24,3072]{1,0:T(8,128)S(1)}, f32[24,3072]{1,0:T(8,128)S(1)}, u32[]{:S(2)}, u32[]{:S(2)}) collective-permute-start(f32[24,3072]{1,0:T(8,128)S(1)} %slice_select_fusion), channel_id=1, source_target_pairs={{0,1},{1,0},{2,3},{3,2},{4,5},{5,4},{6,7},{7,6},{8,9},{9,8},{10,11... | collective-permute-start | bytes 884744 | tf_op jit(solution)/shard_map/ppermute | solution.py:974
  306.7 11.2 %collective-permute-start.56 = (bf16[48,896]{1,0:T(8,128)(2,1)S(1)}, bf16[48,896]{1,0:T(8,128)(2,1)S(1)}, u32[]{:S(2)}, u32[]{:S(2)}) collective-permute-start(bf16[48,896]{1,0:T(8,128)(2,1)S(1)} %get-tuple-element.321), channel_id=1, source_target_pairs={{0,8},{1,9},{2,10},{3,11},{4,12},{5,13},{6,14},{7,15},{8,16},{9,17... | collective-permute-start | bytes 258056 | tf_op jit(solution)/shard_map/ppermute | solution.py:978
  306.7 11.2 %collective-permute-start.57 = (bf16[48,896]{1,0:T(8,128)(2,1)S(1)}, bf16[48,896]{1,0:T(8,128)(2,1)S(1)}, u32[]{:S(2)}, u32[]{:S(2)}) collective-permute-start(bf16[48,896]{1,0:T(8,128)(2,1)S(1)} %get-tuple-element.322), channel_id=1, source_target_pairs={{0,16},{1,17},{2,18},{3,19},{4,20},{5,21},{6,22},{7,23},{8,24},{9,... | collective-permute-start | bytes 258056 | tf_op jit(solution)/shard_map/ppermute | solution.py:978
  309.2 8.7 %collective-permute-start.58 = (bf16[48,896]{1,0:T(8,128)(2,1)S(1)}, bf16[48,896]{1,0:T(8,128)(2,1)S(1)}, u32[]{:S(2)}, u32[]{:S(2)}) collective-permute-start(bf16[48,896]{1,0:T(8,128)(2,1)S(1)} %get-tuple-element.323), channel_id=1, source_target_pairs={{0,24},{1,25},{2,26},{3,27},{4,28},{5,29},{6,30},{7,31},{8,0},{9,1... | collective-permute-start | bytes 258056 | tf_op jit(solution)/shard_map/ppermute | solution.py:978
  310.6 7.3 %collective-permute-start.59 = (bf16[48,768]{1,0:T(8,128)(2,1)S(1)}, bf16[48,768]{1,0:T(8,128)(2,1)S(1)}, u32[]{:S(2)}, u32[]{:S(2)}) collective-permute-start(bf16[48,768]{1,0:T(8,128)(2,1)S(1)} %fusion.35), channel_id=1, source_target_pairs={{0,8},{1,9},{2,10},{3,11},{4,12},{5,13},{6,14},{7,15},{8,0},{9,1},... | collective-permute-start | bytes 221192 | tf_op jit(solution)/shard_map/ppermute | solution.py:982
  (41 other events, 182.3 us)
